TPU v7x, 128 devices: a whole 4x4x4 slice. The times are simulated.
128 devices in a mesh: dp: 16 (over y_hi, x, core), expert: 8 (over z, y_lo).
Axes of the slice: x: 4, y: 4 (y_hi: 2, y_lo: 2; y = y_hi * 2 + y_lo), z: 4, core: 2. Of those that a mesh axis runs over, the one named last changes fastest.
Arguments:
- tokens: bfloat16 [4096, 4, 4096], P(('dp', 'expert')), may hold values from -6 to 6
- cotangent: bfloat16 [4096, 4, 4096], P(('dp', 'expert')), may hold values from -6 to 6
- group_of: int32 [4096, 4], P(('dp', 'expert')), may hold values from 0 to 127, as said below
- mixer: bfloat16 [4096, 32], replicated, may hold values from -0.1875 to 0.1875
- w_in: bfloat16 [32, 4096, 2048], P('dp', None, 'expert'), may hold values from -0.09375 to 0.09375
- w_out: bfloat16 [32, 2048, 4096], P('dp', 'expert'), may hold values from -0.125 to 0.125
Outputs:
- grad_tokens: bfloat16 [4096, 4, 4096], P(('dp', 'expert'))
- grad_mixer: float32 [4096, 32], replicated
- grad_in: bfloat16 [32, 4096, 2048], P('dp', None, 'expert')
- grad_out: bfloat16 [32, 2048, 4096], P('dp', 'expert')
Inputs may be any that keep to these rules, and one draw needn't show every extreme that they name: `group_of`: sequences lie on devices in the order of dp, then expert. Group number q lies on the devices whose expert index is q // 16; at each position it takes exactly 2 sequences of each of them, so every group has 32 members.
All inputs are finite; a program needn't handle non-finite values.
Results may differ from a plain program's by a relative error of at most 0.024.
Values may be sent and summed in bfloat16 or wider, within the bound.
No kernel may reach another device: no remote copies, remote signals or barrier semaphores. Data moves between devices by JAX's collectives and lax.ppermute only.
A program may use at most 192 MiB of HBM per device.

v0:
```python
import jax
import jax.numpy as jnp
from jax import lax
from jax.sharding import PartitionSpec as P

soft_cap = 15.0


def expert_local(rows_mixed, rows_grad, w_in, w_out):
    pre_act = jnp.einsum("sepd,edh->seph", rows_mixed, w_in, preferred_element_type=jnp.float32)
    sigma_pre = jax.nn.sigmoid(pre_act)
    hidden = (pre_act * sigma_pre).astype(jnp.bfloat16)
    back_hidden = jnp.einsum("sepd,ehd->seph", rows_grad, w_out, preferred_element_type=jnp.float32)
    slope = (back_hidden * sigma_pre * (1.0 + pre_act * (1.0 - sigma_pre))).astype(jnp.bfloat16)
    grad_in = jnp.einsum(
        "sepd,seph->edh", rows_mixed, slope, preferred_element_type=jnp.float32
    ).astype(jnp.bfloat16)
    grad_out = jnp.einsum(
        "seph,sepd->ehd", hidden, rows_grad, preferred_element_type=jnp.float32
    ).astype(jnp.bfloat16)
    return (hidden, slope, grad_in, grad_out)


def shards(tokens, cotangent, group_of, mixer, w_in, w_out):
    seq_count, pos_count, model_width = tokens.shape
    owner_count = lax.axis_size("dp")
    block_count = lax.axis_size("expert")
    members = seq_count // owner_count
    local_experts = w_in.shape[0]
    ranking = jnp.argsort(group_of, axis=0, stable=True)
    picked = ranking[:, :, None]
    sorted_tok = jnp.take_along_axis(tokens, picked, axis=0).reshape(
        owner_count, members, pos_count, model_width
    )
    sorted_cot = jnp.take_along_axis(cotangent, picked, axis=0).reshape(
        owner_count, members, pos_count, model_width
    )
    got_tok, got_cot = (
        lax.all_to_all(sorted_tok, "dp", split_axis=0, concat_axis=0, tiled=True),
        lax.all_to_all(sorted_cot, "dp", split_axis=0, concat_axis=0, tiled=True),
    )
    group_tok = got_tok.reshape(owner_count * members, pos_count, model_width)
    group_cot = got_cot.reshape(owner_count * members, pos_count, model_width)
    logits = jnp.einsum("gpd,de->gpe", group_tok, mixer, preferred_element_type=jnp.float32)
    scaled = jnp.tanh(logits / soft_cap)
    exponent = jnp.exp(soft_cap * scaled)
    weights = exponent / jnp.sum(exponent, axis=0, keepdims=True)
    mixed = jnp.einsum(
        "gpe,gpd->epd", weights, group_tok, preferred_element_type=jnp.float32
    ).astype(jnp.bfloat16)
    dmixed = jnp.einsum(
        "gpe,gpd->epd", weights, group_cot, preferred_element_type=jnp.float32
    ).astype(jnp.bfloat16)
    mixed = mixed.reshape(owner_count, local_experts, pos_count, model_width)
    dmixed = dmixed.reshape(owner_count, local_experts, pos_count, model_width)
    full_shape = (owner_count, block_count, local_experts, pos_count, model_width)
    flat_shape = (owner_count * block_count, local_experts, pos_count, model_width)
    spread_mixed = jnp.broadcast_to(mixed[:, None], full_shape).reshape(flat_shape)
    spread_grad = jnp.broadcast_to(dmixed[:, None], full_shape).reshape(flat_shape)
    rows_mixed, rows_grad = (
        lax.all_to_all(spread_mixed, ("dp", "expert"), split_axis=0, concat_axis=0, tiled=True),
        lax.all_to_all(spread_grad, ("dp", "expert"), split_axis=0, concat_axis=0, tiled=True),
    )
    hidden, slope, grad_in, grad_out = expert_local(rows_mixed, rows_grad, w_in, w_out)
    part_out = jnp.einsum(
        "seph,ehd->sepd", hidden, w_out, preferred_element_type=jnp.float32
    ).astype(jnp.bfloat16)
    part_grad = jnp.einsum(
        "seph,edh->sepd", slope, w_in, preferred_element_type=jnp.float32
    ).astype(jnp.bfloat16)
    back_out, back_grad = (
        lax.all_to_all(part_out, ("dp", "expert"), split_axis=0, concat_axis=0, tiled=True),
        lax.all_to_all(part_grad, ("dp", "expert"), split_axis=0, concat_axis=0, tiled=True),
    )
    expert_out = back_out.reshape(full_shape).astype(jnp.float32).sum(axis=1)
    grad_mixed = back_grad.reshape(full_shape).astype(jnp.float32).sum(axis=1)
    expert_out = expert_out.reshape(owner_count * local_experts, pos_count, model_width)
    grad_mixed = grad_mixed.reshape(owner_count * local_experts, pos_count, model_width)
    d_weights = jnp.einsum(
        "gpd,epd->gpe", group_cot, expert_out, preferred_element_type=jnp.float32
    ) + jnp.einsum("gpd,epd->gpe", group_tok, grad_mixed, preferred_element_type=jnp.float32)
    column_sum = jnp.sum(weights * d_weights, axis=0, keepdims=True)
    d_logits = weights * (d_weights - column_sum) * (1.0 - scaled * scaled)
    mixer_wide = mixer.astype(jnp.float32)
    grad_group = jnp.einsum("gpe,epd->gpd", weights, grad_mixed) + jnp.einsum(
        "gpe,de->gpd", d_logits, mixer_wide
    )
    grad_group = grad_group.astype(jnp.bfloat16).reshape(
        owner_count, members, pos_count, model_width
    )
    mixer_part = jnp.einsum("gpd,gpe->de", group_tok, d_logits, preferred_element_type=jnp.float32)
    grad_mixer = lax.psum(mixer_part, ("dp", "expert"))
    back_tokens = lax.all_to_all(grad_group, "dp", split_axis=0, concat_axis=0, tiled=True).reshape(
        seq_count, pos_count, model_width
    )
    inverse = jnp.argsort(ranking, axis=0)
    grad_tokens = jnp.take_along_axis(back_tokens, inverse[:, :, None], axis=0)
    return (grad_tokens, grad_mixer, grad_in, grad_out)


def solution(mesh):
    placed = (
        P(("dp", "expert"), None, None),
        P(("dp", "expert"), None, None),
        P(("dp", "expert"), None),
        P(),
        P("dp", None, "expert"),
        P("dp", "expert", None),
    )
    return jax.shard_map(
        shards,
        mesh=mesh,
        in_specs=placed,
        out_specs=(
            P(("dp", "expert"), None, None),
            P(),
            P("dp", None, "expert"),
            P("dp", "expert", None),
        ),
        check_vma=False,
    )
```

profile of v0, /device:TPU:1, one launch (start us, length us, event | category | flops | bytes accessed | tf_op | source)
XLA Modules:
  0.0 725.4 jit_solution(1924898681775553081)
XLA Ops:
  9.3 4.8 gather_fusion.1
  23.1 8.4 %all-to-all-start.1 = ((bf16[16,2,4,4096]{3,1,2,0:T(2,128)(2,1)}), bf16[16,2,4,4096]{3,1,2,0:T(2,128)(2,1)S(1)}, u32[]{:S(2)}, u32[]{:S(2)}) async-start(bf16[16,2,4,4096]{3,1,2,0:T(2,128)(2,1)} %copy.82), calls=%async_computation.1 | async-start | bytes 2097152 | tf_op jit(solution)/shard_map/all_to_all | solution.py:39
  33.7 15.3 %all-to-all-done.1 = bf16[16,2,4,4096]{3,1,2,0:T(2,128)(2,1)S(1)} async-done(((bf16[16,2,4,4096]{3,1,2,0:T(2,128)(2,1)}), bf16[16,2,4,4096]{3,1,2,0:T(2,128)(2,1)S(1)}, u32[]{:S(2)}, u32[]{:S(2)}) %all-to-all-start.1) | async-done | bytes 1048608 | tf_op jit(solution)/shard_map/all_to_all | solution.py:39
  58.7 12.1 %all-to-all-done = bf16[16,2,4,4096]{3,1,2,0:T(2,128)(2,1)S(1)} async-done(((bf16[16,2,4,4096]{3,1,2,0:T(2,128)(2,1)}), bf16[16,2,4,4096]{3,1,2,0:T(2,128)(2,1)S(1)}, u32[]{:S(2)}, u32[]{:S(2)}) %all-to-all-start) | async-done | bytes 1048608 | tf_op jit(solution)/shard_map/all_to_all | solution.py:40
  70.7 7.5 %broadcast_in_dim.32 = bf16[16,8,2,4,4096]{4,3,2,1,0:T(4,128)(2,1)} broadcast(bf16[16,2,4,4096]{3,2,1,0:T(4,128)(2,1)S(1)} %bitcast.117), dimensions={0,2,3,4} | broadcast | bytes 9437184 | tf_op jit(solution)/shard_map/broadcast_in_dim | solution.py:58
  78.2 6.5 all-to-all-start.3
  87.6 98.8 %all-to-all-done.3 = bf16[128,2,4,4096]{3,2,1,0:T(4,128)(2,1)} async-done(((bf16[128,2,4,4096]{3,2,1,0:T(4,128)(2,1)}), bf16[128,2,4,4096]{3,2,1,0:T(4,128)(2,1)}, u32[]{:S(2)}, u32[]{:S(2)}) %all-to-all-start.3) | async-done | bytes 8388640 | tf_op jit(solution)/shard_map/all_to_all | solution.py:61
  186.4 7.5 %broadcast_in_dim.30 = bf16[16,8,2,4,4096]{4,3,2,1,0:T(4,128)(2,1)} broadcast(bf16[16,2,4,4096]{3,2,1,0:T(4,128)(2,1)S(1)} %bitcast.118), dimensions={0,2,3,4} | broadcast | bytes 9437184 | tf_op jit(solution)/shard_map/broadcast_in_dim | solution.py:59
  193.9 8.0 %all-to-all-start.2 = ((bf16[128,2,4,4096]{3,2,1,0:T(4,128)(2,1)}), bf16[128,2,4,4096]{3,2,1,0:T(4,128)(2,1)}, u32[]{:S(2)}, u32[]{:S(2)}) async-start(bf16[128,2,4,4096]{3,2,1,0:T(4,128)(2,1)} %bitcast.115), calls=%async_computation.2 | async-start | bytes 16777216 | tf_op jit(solution)/shard_map/all_to_all | solution.py:62
  201.9 14.6 %copy.103 = bf16[128,2,4,4096]{0,3,2,1:T(8,128)(2,1)} copy(bf16[128,2,4,4096]{3,2,1,0:T(4,128)(2,1)} %all-to-all-done.3) | data formatting | bytes 16777216 | tf_op jit(solution)/shard_map/all_to_all | solution.py:61
  216.4 8.1 %fusion.19 = f32[128,2,4,256]{3,0,2,1:T(8,128)S(1)} fusion(bf16[128,2,4,4096]{0,3,2,1:T(8,128)(2,1)} %copy.103, bf16[2,4096,256]{2,1,0:T(8,128)(2,1)} %param.12), kind=kOutput, calls=%fused_computation.31 | convolution fusion | flops 2147483648 | bytes 13631488 | tf_op jit(solution)/shard_map/sepd,edh->seph/dot_general | solution.py:10
  226.9 18.0 %copy.94 = bf16[128,2,4,4096]{3,2,1,0:T(4,128)(2,1)} copy(bf16[128,2,4,4096]{3,0,2,1:T(8,128)(2,1)S(1)} %convert_bitcast_fusion) | data formatting | bytes 16777216 | tf_op jit(solution)/shard_map/convert_element_type | solution.py:67
  244.9 59.2 %all-to-all-done.2 = bf16[128,2,4,4096]{3,2,1,0:T(4,128)(2,1)} async-done(((bf16[128,2,4,4096]{3,2,1,0:T(4,128)(2,1)}), bf16[128,2,4,4096]{3,2,1,0:T(4,128)(2,1)}, u32[]{:S(2)}, u32[]{:S(2)}) %all-to-all-start.2) | async-done | bytes 8388640 | tf_op jit(solution)/shard_map/all_to_all | solution.py:62
  304.1 8.4 %all-to-all-start.5 = ((bf16[128,2,4,4096]{3,2,1,0:T(4,128)(2,1)}), bf16[128,2,4,4096]{3,2,1,0:T(4,128)(2,1)}, u32[]{:S(2)}, u32[]{:S(2)}) async-start(bf16[128,2,4,4096]{3,2,1,0:T(4,128)(2,1)} %copy.94), calls=%async_computation.5 | async-start | bytes 16777216 | tf_op jit(solution)/shard_map/all_to_all | solution.py:72
  312.6 14.4 %fusion.37 = bf16[128,2,4,256]{3,0,2,1:T(8,128)(2,1)S(1)} fusion(bf16[2,256,4096]{2,1,0:T(8,128)(2,1)} %param.13, bf16[128,2,4,4096]{3,2,1,0:T(4,128)(2,1)} %all-to-all-done.2, f32[128,2,4,256]{3,0,2,1:T(8,128)S(1)} %fusion.19), kind=kOutput, calls=%fused_computation.35 | convolution fusion | flops 2149842944 | bytes 14155776 | tf_op jit(solution)/shard_map/sepd,ehd->seph/dot_general | solution.py:13
  329.5 18.0 %copy.90 = bf16[128,2,4,4096]{3,2,1,0:T(4,128)(2,1)} copy(bf16[128,2,4,4096]{3,0,2,1:T(8,128)(2,1)S(1)} %convert_bitcast_fusion.1) | data formatting | bytes 16777216 | tf_op jit(solution)/shard_map/convert_element_type | solution.py:70
  347.6 66.2 %all-to-all-done.5 = bf16[128,2,4,4096]{3,2,1,0:T(4,128)(2,1)} async-done(((bf16[128,2,4,4096]{3,2,1,0:T(4,128)(2,1)}), bf16[128,2,4,4096]{3,2,1,0:T(4,128)(2,1)}, u32[]{:S(2)}, u32[]{:S(2)}) %all-to-all-start.5) | async-done | bytes 8388640 | tf_op jit(solution)/shard_map/all_to_all | solution.py:72
  413.8 7.6 %all-to-all-start.4 = ((bf16[128,2,4,4096]{3,2,1,0:T(4,128)(2,1)}), bf16[128,2,4,4096]{3,2,1,0:T(4,128)(2,1)}, u32[]{:S(2)}, u32[]{:S(2)}) async-start(bf16[128,2,4,4096]{3,2,1,0:T(4,128)(2,1)} %copy.90), calls=%async_computation.4 | async-start | bytes 16777216 | tf_op jit(solution)/shard_map/all_to_all | solution.py:73
  422.6 8.5 %convert_reduce_fusion = bf16[16,2,4,4096]{3,2,1,0:T(4,128)(2,1)S(1)} fusion(bf16[128,2,4,4096]{3,2,1,0:T(4,128)(2,1)} %all-to-all-done.5), kind=kLoop, calls=%fused_computation.3 | loop fusion | flops 7864320 | bytes 9437184 | tf_op jit(solution)/shard_map/reduce_sum | solution.py:75
  432.7 90.5 %all-to-all-done.4 = bf16[128,2,4,4096]{3,2,1,0:T(4,128)(2,1)} async-done(((bf16[128,2,4,4096]{3,2,1,0:T(4,128)(2,1)}), bf16[128,2,4,4096]{3,2,1,0:T(4,128)(2,1)}, u32[]{:S(2)}, u32[]{:S(2)}) %all-to-all-start.4) | async-done | bytes 8388640 | tf_op jit(solution)/shard_map/all_to_all | solution.py:73
  523.1 8.5 %convert_reduce_fusion.1 = bf16[16,2,4,4096]{3,2,1,0:T(4,128)(2,1)S(1)} fusion(bf16[128,2,4,4096]{3,2,1,0:T(4,128)(2,1)} %all-to-all-done.4), kind=kLoop, calls=%fused_computation.4 | loop fusion | flops 7864320 | bytes 9437184 | tf_op jit(solution)/shard_map/reduce_sum | solution.py:76
  542.8 16.0 %bitcast_convert_fusion = bf16[2,256,4096]{2,1,0:T(8,128)(2,1)} fusion(bf16[128,2,4,4096]{3,2,1,0:T(4,128)(2,1)} %all-to-all-done.2, f32[128,2,4,256]{3,0,2,1:T(8,128)} %copy-done.5), kind=kOutput, calls=%fused_computation.5 | convolution fusion | flops 2150891520 | bytes 13631488 | tf_op jit(solution)/shard_map/seph,sepd->ehd/dot_general | solution.py:18
  558.8 9.6 %bitcast_convert_fusion.1 = bf16[2,4096,256]{2,1,0:T(8,128)(2,1)} fusion(bf16[128,2,4,4096]{0,3,2,1:T(8,128)(2,1)} %copy.103, bf16[128,2,4,256]{3,0,2,1:T(8,128)(2,1)S(1)} %copy-done.7), kind=kOutput, calls=%fused_computation.6 | convolution fusion | flops 2149580800 | bytes 13107200 | tf_op jit(solution)/shard_map/sepd,seph->edh/dot_general | solution.py:15
  576.3 140.2 %all-reduce.2.cloned.1.call-done = f32[4096,32]{0,1:T(8,128)} async-done(((f32[4096,32]{0,1:T(8,128)}), f32[4096,32]{0,1:T(8,128)}) %all-reduce.2.cloned.1.call-update) | async-done | bytes 524304 | tf_op jit(solution)/shard_map/psum | solution.py:92
  (71 shorter events, 54.3 us)
Async XLA Ops:
  7.2 2.1 copy-start
  7.2 8.4 %copy-start.2 = (bf16[32,4,4096]{2,1,0:T(4,128)(2,1)S(1)}, bf16[32,4,4096]{2,1,0:T(4,128)(2,1)}, u32[]{:S(2)}) copy-start(bf16[32,4,4096]{2,1,0:T(4,128)(2,1)} %param.9) | copy-start | bytes 3145732
  19.9 37.0 %copy-start.8 = (bf16[4096,32]{0,1:T(8,128)(2,1)S(1)}, bf16[4096,32]{0,1:T(8,128)(2,1)}, u32[]{:S(2)}) copy-start(bf16[4096,32]{0,1:T(8,128)(2,1)} %param.11) | copy-start | bytes 786436
  23.1 25.8 %all-to-all-start.1 = ((bf16[16,2,4,4096]{3,1,2,0:T(2,128)(2,1)}), bf16[16,2,4,4096]{3,1,2,0:T(2,128)(2,1)S(1)}, u32[]{:S(2)}, u32[]{:S(2)}) async-start(bf16[16,2,4,4096]{3,1,2,0:T(2,128)(2,1)} %copy.82), calls=%async_computation.1 | async-start | bytes 2097152 | tf_op jit(solution)/shard_map/all_to_all | solution.py:39
  48.9 21.8 %all-to-all-start = ((bf16[16,2,4,4096]{3,1,2,0:T(2,128)(2,1)}), bf16[16,2,4,4096]{3,1,2,0:T(2,128)(2,1)S(1)}, u32[]{:S(2)}, u32[]{:S(2)}) async-start(bf16[16,2,4,4096]{3,1,2,0:T(2,128)(2,1)} %copy.78), calls=%async_computation | async-start | bytes 2097152 | tf_op jit(solution)/shard_map/all_to_all | solution.py:40
  78.2 108.2 %all-to-all-start.3 = ((bf16[128,2,4,4096]{3,2,1,0:T(4,128)(2,1)}), bf16[128,2,4,4096]{3,2,1,0:T(4,128)(2,1)}, u32[]{:S(2)}, u32[]{:S(2)}) async-start(bf16[128,2,4,4096]{3,2,1,0:T(4,128)(2,1)} %bitcast.114), calls=%async_computation.3 | async-start | bytes 16777216 | tf_op jit(solution)/shard_map/all_to_all | solution.py:61
  193.9 110.3 %all-to-all-start.2 = ((bf16[128,2,4,4096]{3,2,1,0:T(4,128)(2,1)}), bf16[128,2,4,4096]{3,2,1,0:T(4,128)(2,1)}, u32[]{:S(2)}, u32[]{:S(2)}) async-start(bf16[128,2,4,4096]{3,2,1,0:T(4,128)(2,1)} %bitcast.115), calls=%async_computation.2 | async-start | bytes 16777216 | tf_op jit(solution)/shard_map/all_to_all | solution.py:62
  216.4 8.1 %copy-start.4 = (bf16[2,256,4096]{2,1,0:T(8,128)(2,1)S(1)}, bf16[2,256,4096]{2,1,0:T(8,128)(2,1)}, u32[]{:S(2)}) copy-start(bf16[2,256,4096]{2,1,0:T(8,128)(2,1)} %param.13) | copy-start | bytes 12582916
  224.5 88.0 %copy-start.5 = (f32[128,2,4,256]{3,0,2,1:T(8,128)}, f32[128,2,4,256]{3,0,2,1:T(8,128)S(1)}, u32[]{:S(2)}) copy-start(f32[128,2,4,256]{3,0,2,1:T(8,128)S(1)} %fusion.19) | copy-start | bytes 3145732
  304.1 109.7 %all-to-all-start.5 = ((bf16[128,2,4,4096]{3,2,1,0:T(4,128)(2,1)}), bf16[128,2,4,4096]{3,2,1,0:T(4,128)(2,1)}, u32[]{:S(2)}, u32[]{:S(2)}) async-start(bf16[128,2,4,4096]{3,2,1,0:T(4,128)(2,1)} %copy.94), calls=%async_computation.5 | async-start | bytes 16777216 | tf_op jit(solution)/shard_map/all_to_all | solution.py:72
  312.5 14.4 %copy-start.3 = (bf16[2,4096,256]{2,1,0:T(8,128)(2,1)S(1)}, bf16[2,4096,256]{2,1,0:T(8,128)(2,1)}, u32[]{:S(2)}) copy-start(bf16[2,4096,256]{2,1,0:T(8,128)(2,1)} %param.12) | copy-start | bytes 12582916
  326.9 2.6 copy-start.6
  413.8 109.3 %all-to-all-start.4 = ((bf16[128,2,4,4096]{3,2,1,0:T(4,128)(2,1)}), bf16[128,2,4,4096]{3,2,1,0:T(4,128)(2,1)}, u32[]{:S(2)}, u32[]{:S(2)}) async-start(bf16[128,2,4,4096]{3,2,1,0:T(4,128)(2,1)} %copy.90), calls=%async_computation.4 | async-start | bytes 16777216 | tf_op jit(solution)/shard_map/all_to_all | solution.py:73
  432.7 100.9 %copy-start.9 = (f32[4,32,32]{1,2,0:T(8,128)S(1)}, f32[4,32,32]{1,2,0:T(8,128)}, u32[]{:S(2)}) copy-start(f32[4,32,32]{1,2,0:T(8,128)} %fusion.14) | copy-start | bytes 49156
  538.2 31.3 %all-to-all-start.6 = ((bf16[16,2,4,4096]{3,1,2,0:T(2,128)(2,1)}), bf16[16,2,4,4096]{3,1,2,0:T(2,128)(2,1)S(1)}, u32[]{:S(2)}, u32[]{:S(2)}) async-start(bf16[16,2,4,4096]{3,1,2,0:T(2,128)(2,1)} %copy.99), calls=%async_computation.6 | async-start | bytes 2097152 | tf_op jit(solution)/shard_map/all_to_all | solution.py:93
  542.8 16.0 %copy-start.7 = (bf16[128,2,4,256]{3,0,2,1:T(8,128)(2,1)S(1)}, bf16[128,2,4,256]{3,0,2,1:T(8,128)(2,1)}, u32[]{:S(2)}) copy-start(bf16[128,2,4,256]{3,0,2,1:T(8,128)(2,1)} %copy-done.6) | copy-start | bytes 1572868
  542.8 173.7 %all-reduce.2.cloned.1.call-start = ((), (), s32[]{:S(2)}) async-start(), calls=%async_computation.7 | async-start | bytes 1048576 | tf_op jit(solution)/shard_map/psum | solution.py:92
  569.5 148.8 %copy-start.1 = (bf16[32,4,4096]{2,1,0:T(4,128)(2,1)S(1)}, bf16[32,4,4096]{2,1,0:T(4,128)(2,1)}, u32[]{:S(2)}) copy-start(bf16[32,4,4096]{2,1,0:T(4,128)(2,1)} %param.8) | copy-start | bytes 3145732
Sparse Core Ops, SparseCore 0:
  569.6 146.7 all-reduce.1
where the time goes:
time: 735 us; the launch traced here: 725 us
  waiting for transfers between devices  482 us (66%)
  local copies, waits for them, and re-layouts  98.7 us (13%)
  matrix products  60.6 us (8%)
  starting transfers between devices  48 us (7%)
  other arithmetic  21.3 us (3%)
  between operations  14.6 us (2%)
    psum x1, waiting for transfers between devices, shards(): grad_mixer = lax.psum(mixer_part, ('dp', 'expert'))  140 us
    all_to_all x1, waiting for transfers between devices, shards(): lax.all_to_all(spread_mixed, ('dp', 'expert'), split_axis=0, concat_axis=...  98.8 us
    all_to_all x1, waiting for transfers between devices, shards(): lax.all_to_all(part_grad, ('dp', 'expert'), split_axis=0, concat_axis=0,...  90.5 us
    all_to_all x1, waiting for transfers between devices, shards(): lax.all_to_all(part_out, ('dp', 'expert'), split_axis=0, concat_axis=0, t...  66.2 us
    all_to_all x1, waiting for transfers between devices, shards(): lax.all_to_all(spread_grad, ('dp', 'expert'), split_axis=0, concat_axis=0...  59.2 us
    convert_element_type x1, local copies, waits for them, and re-layouts, shards(): part_grad = jnp.einsum('seph,edh->sepd', slope, w_in, preferred_element_t...  18 us
    convert_element_type x1, local copies, waits for them, and re-layouts, shards(): part_out = jnp.einsum('seph,ehd->sepd', hidden, w_out, preferred_element_...  18 us
    dot_general x1, matrix products, expert_local(): jnp.einsum('seph,sepd->ehd', hidden, rows_grad, preferred_element_type=jn...  16 us
  transfers between devices with their start and end apart: 8, of which 7 were waited for; matrix products, arithmetic and copies ran while one was open for 18% of the time, Pallas kernels for 0%

commit v1 on v0

v1 whole, which is shorter than its diff:
```python
import jax
import jax.numpy as jnp
from jax import lax
from jax.sharding import Mesh
from jax.sharding import PartitionSpec as P

soft_cap = 15.0
f32 = jnp.float32
bf16 = jnp.bfloat16

axes = ("yh", "x", "core", "z", "b")
sizes = (2, 4, 2, 4, 2)
owners = ("yh", "x", "core")
same_core = ("yh", "x", "z", "b")
swap = [(0, 1), (1, 0)]


def mm(left, right, contract=((1,), (0,))):
    return lax.dot_general(left, right, (contract, ((), ())), preferred_element_type=f32)


def exchange(array, names):
    return lax.all_to_all(array, names, split_axis=0, concat_axis=0, tiled=True)


def split_high_low(value):
    high = lax.reduce_precision(value, 8, 7)
    return high.astype(bf16), (value - high).astype(bf16)


def weight_round(step):
    return [
        (s * 4 + z, (z // 2) * 4 + 2 * s + (z + step) % 2) for s in range(2) for z in range(4)
    ]


def back_round(step):
    return [(b, a) for a, b in weight_round(step)]


def shards(tokens, cotangent, group_of, mixer, w_in, w_out):
    seqs, positions, width = tokens.shape
    rows = seqs * positions
    core = lax.axis_index("core")
    first = core == 0
    even = lax.axis_index("z") % 2 == 0
    half = width // 2

    def pick(flag, one, other):
        return jnp.where(flag, one, other)

    home = group_of % 16
    earlier = jnp.arange(seqs)[:, None] > jnp.arange(seqs)[None, :]
    same = (home[:, None, :] == home[None, :, :]) & earlier[:, :, None]
    member = jnp.sum(same.astype(jnp.int32), axis=1)
    place = home * 8 + jnp.arange(positions, dtype=jnp.int32)[None, :] * 2 + member
    hot = (place.reshape(1, rows) == jnp.arange(rows, dtype=jnp.int32)[:, None]).astype(bf16)
    tok = mm(hot, tokens.reshape(rows, width)).astype(bf16).reshape(8, 1, 16, width)
    cot = mm(hot, cotangent.reshape(rows, width)).astype(bf16).reshape(8, 1, 16, width)
    sent = jnp.concatenate([tok, cot], axis=1).reshape(16, 16, width)
    held = exchange(sent, owners).reshape(256, width)

    weights_in, weights_out = [], []
    for step in range(2):
        flag = even if step == 0 else jnp.logical_not(even)
        weights_in.append(
            lax.ppermute(pick(flag, w_in[0], w_in[1]), ("core", "z"), weight_round(step))
        )
        weights_out.append(
            lax.ppermute(pick(flag, w_out[0], w_out[1]), ("core", "z"), weight_round(step))
        )

    mixer_t = mixer.T
    logits = mm(mixer_t, held, ((1,), (1,)))
    logits = pick(first, logits, lax.ppermute(logits, "core", swap))
    scaled = jnp.tanh(logits / soft_cap)
    exponent = jnp.exp(soft_cap * scaled)
    column = jnp.arange(256, dtype=jnp.int32) // 2 % 8
    mask = (column[None, :] == jnp.arange(8, dtype=jnp.int32)[:, None]).astype(f32)
    spread = exponent[:, None, :] * mask[None]
    spread = spread / jnp.sum(spread, axis=2, keepdims=True)
    spread_high, spread_low = split_high_low(spread)
    mix = mm(spread_high.reshape(256, 256), held) + mm(spread_low.reshape(256, 256), held)
    mix = mix.astype(bf16).reshape(32, 1, 8, width)
    mix = jnp.broadcast_to(mix, (32, 2, 8, width)).reshape(64, 8, width)
    own_rows = exchange(mix, same_core).reshape(512, width)
    other_rows = lax.ppermute(own_rows, "core", swap)
    mixed = pick(first, own_rows, other_rows)
    dmixed = pick(first, other_rows, own_rows)

    expert_in = jnp.concatenate(weights_in, axis=1)
    expert_out = jnp.concatenate(weights_out, axis=0)
    pre_act = mm(mixed, expert_in)
    sigma_pre = jax.nn.sigmoid(pre_act)
    hidden = (pre_act * sigma_pre).astype(bf16)
    back_hidden = mm(dmixed, expert_out, ((1,), (1,)))
    slope = (back_hidden * sigma_pre * (1.0 + pre_act * (1.0 - sigma_pre))).astype(bf16)
    part_out = mm(hidden, expert_out).astype(bf16)
    part_grad = mm(slope, expert_in, ((1,), (1,))).astype(bf16)
    kept = pick(first, part_grad, part_out)
    given = lax.ppermute(pick(first, part_out, part_grad), "core", swap)
    part = (kept.astype(f32) + given.astype(f32)).astype(bf16)
    back = exchange(part.reshape(64, 8, width), same_core).reshape(512, width)

    grads_in, grads_out = [], []
    for step in range(2):
        block = slice(256 * step, 256 * step + 256)
        grads_in.append(
            lax.ppermute(
                mm(mixed, slope[:, block], ((0,), (0,))).astype(bf16),
                ("core", "z"),
                back_round(step),
            )
        )
        grads_out.append(
            lax.ppermute(
                mm(hidden[:, block], dmixed, ((0,), (0,))).astype(bf16),
                ("core", "z"),
                back_round(step),
            )
        )
    grad_in = jnp.stack(
        [pick(even, grads_in[0], grads_in[1]), pick(even, grads_in[1], grads_in[0])]
    )
    grad_out = jnp.stack(
        [pick(even, grads_out[0], grads_out[1]), pick(even, grads_out[1], grads_out[0])]
    )

    back_half = pick(first, back[:, :half], lax.ppermute(back[:, half:], "core", swap))
    dots = mm(back, held, ((1,), (1,))).reshape(32, 2, 8, 256)
    dots = jnp.sum(dots * mask[None, None], axis=(1, 2))
    d_weights = dots + lax.ppermute(dots, "core", swap)
    weights = jnp.sum(spread, axis=1)
    column_sum = jnp.sum((weights * d_weights)[:, None, :] * mask[None], axis=2, keepdims=True)
    column_sum = jnp.sum(column_sum * mask[None], axis=1)
    d_logits = weights * (d_weights - column_sum) * (1.0 - scaled * scaled)
    d_high, d_low = split_high_low(d_logits)

    both_high = jnp.broadcast_to(spread_high[:, None], (32, 2, 8, 256)).reshape(512, 256)
    both_low = jnp.broadcast_to(spread_low[:, None], (32, 2, 8, 256)).reshape(512, 256)
    mixer_half = pick(first, mixer_t[:, :half], mixer_t[:, half:])
    down = ((0,), (0,))
    grad_rows = (
        mm(both_high, back_half, down)
        + mm(both_low, back_half, down)
        + mm(d_high, mixer_half, down)
        + mm(d_low, mixer_half, down)
    )
    grad_rows = exchange(grad_rows.astype(bf16).reshape(16, 16, half), owners)
    grad_rows = grad_rows.reshape(8, 2, 16, half)
    grad_tokens = jnp.concatenate(
        [mm(hot, grad_rows[:, side].reshape(rows, half), down).astype(bf16) for side in range(2)],
        axis=1,
    ).reshape(seqs, positions, width)

    mixer_part = mm(d_high, held) + mm(d_low, held)
    mixer_part = pick(first, mixer_part, jnp.zeros_like(mixer_part))
    pieces = exchange(mixer_part.reshape(128, 8, 128), axes)
    total = jnp.sum(pieces, axis=0, keepdims=True)
    whole = exchange(jnp.broadcast_to(total, (128, 8, 128)), axes)
    grad_mixer = whole.reshape(32, width).T
    return (grad_tokens, grad_mixer, grad_in, grad_out)


def solution(mesh):
    fine = Mesh(mesh.devices.reshape(sizes), axes)
    dp, expert = ("yh", "x", "core"), ("z", "b")
    every = dp + expert
    return jax.shard_map(
        shards,
        mesh=fine,
        in_specs=(
            P(every, None, None),
            P(every, None, None),
            P(every, None),
            P(),
            P(dp, None, expert),
            P(dp, expert, None),
        ),
        out_specs=(
            P(every, None, None),
            P(),
            P(dp, None, expert),
            P(dp, expert, None),
        ),
        check_vma=False,
    )
```

time: 735 us -> 439 us (0.60)
  waiting for transfers between devices: 482 us -> 268 us
  local copies, waits for them, and re-layouts: 98.7 us -> 15.7 us
  starting transfers between devices: 48 us -> 75.4 us
  matrix products: 60.6 us -> 39 us
  other arithmetic: 21.3 us -> 35.5 us
  between operations: 14.6 us -> 1.1 us
    all_to_all x7 -> x6, waiting for transfers between devices: 342 us -> 117 us  [exchange(): return lax.all_to_all(array, names, split_axis=0, concat_axis=0, tiled=True)]
    ppermute x0 -> x13, waiting for transfers between devices: none -> 151 us  [the longest x2 55.3 us: shards(): lax.ppermute(pick(flag, w_out[0], w_out[1]), ('core', 'z'), weight_round(...]
    psum x1 -> x0, waiting for transfers between devices: 140 us -> none  [shards(): grad_mixer = lax.psum(mixer_part, ('dp', 'expert'))]
    convert_element_type x2 -> x0, local copies, waits for them, and re-layouts: 36 us -> none  [the longest x1 18 us: shards(): part_grad = jnp.einsum('seph,edh->sepd', slope, w_in, preferred_element_t...]
    ppermute x0 -> x13, starting transfers between devices: none -> 28 us  [the longest x2 6.57 us: shards(): lax.ppermute(pick(flag, w_in[0], w_in[1]), ('core', 'z'), weight_round(st...]
    dot_general x14 -> x22, matrix products: 60.6 us -> 39 us  [mm(): lax.dot_general(left, right, (contract, ((), ())), preferred_element_type...]
    all_to_all x4 -> x0, local copies, waits for them, and re-layouts: 18.6 us -> none  [the longest x1 14.6 us: shards(): lax.all_to_all(spread_mixed, ('dp', 'expert'), split_axis=0, concat_axis=...]
    reduce_sum x2, other arithmetic: 17.1 us -> 0.35 us  [the longest x1 0.22 us: shards(): member = jnp.sum(same.astype(jnp.int32), axis=1)]
  transfers between devices with their start and end apart: 8 -> 19, of which waited for: 7 -> 13; matrix products, arithmetic and copies ran while one was open for 18% -> 13% of each run, Pallas kernels for 0% -> 0%
where the time goes in v1:
time: 439 us; the launch traced here: 435 us
  waiting for transfers between devices  268 us (61%)
  starting transfers between devices  75.4 us (17%)
  matrix products  39 us (9%)
  other arithmetic  35.5 us (8%)
  local copies, waits for them, and re-layouts  15.7 us (4%)
    all_to_all x6, waiting for transfers between devices, exchange(): return lax.all_to_all(array, names, split_axis=0, concat_axis=0, tiled=True)  117 us
    ppermute x2, waiting for transfers between devices, shards(): lax.ppermute(pick(flag, w_out[0], w_out[1]), ('core', 'z'), weight_round(...  55.3 us
    all_to_all x6, starting transfers between devices, exchange(): return lax.all_to_all(array, names, split_axis=0, concat_axis=0, tiled=True)  47.4 us
    dot_general x22, matrix products, mm(): lax.dot_general(left, right, (contract, ((), ())), preferred_element_type...  39 us
    ppermute x2, waiting for transfers between devices, shards(): lax.ppermute(mm(hidden[:, block], dmixed, ((0,), (0,))).astype(bf16), ('c...  36 us
    ppermute x2, waiting for transfers between devices, shards(): lax.ppermute(mm(mixed, slope[:, block], ((0,), (0,))).astype(bf16), ('cor...  30.5 us
    ppermute x2, waiting for transfers between devices, shards(): lax.ppermute(pick(flag, w_in[0], w_in[1]), ('core', 'z'), weight_round(st...  21.1 us
    select_n x3, other arithmetic, pick(): return jnp.where(flag, one, other)  9.56 us
  transfers between devices with their start and end apart: 19, of which 13 were waited for; matrix products, arithmetic and copies ran while one was open for 13% of the time, Pallas kernels for 0%

profile of v1, /device:TPU:1, one launch (start us, length us, event | category | flops | bytes accessed | tf_op | source)
XLA Modules:
  0.0 434.8 jit_solution(1705084181376195231)
XLA Ops:
  6.6 8.6 %all-to-all-start = ((bf16[16,16,4096]{2,1,0:T(8,128)(2,1)}), bf16[16,16,4096]{2,1,0:T(8,128)(2,1)S(1)}, u32[]{:S(2)}, u32[]{:S(2)}) async-start(bf16[16,16,4096]{2,1,0:T(8,128)(2,1)} %bitcast.87), calls=%async_computation | async-start | bytes 4194304 | tf_op jit(solution)/shard_map/all_to_all | solution.py:23
  15.2 28.6 %all-to-all-done = bf16[16,16,4096]{2,1,0:T(8,128)(2,1)S(1)} async-done(((bf16[16,16,4096]{2,1,0:T(8,128)(2,1)}), bf16[16,16,4096]{2,1,0:T(8,128)(2,1)S(1)}, u32[]{:S(2)}, u32[]{:S(2)}) %all-to-all-start) | async-done | bytes 2097184 | tf_op jit(solution)/shard_map/all_to_all | solution.py:23
  50.7 9.2 %all-to-all-start.1 = ((bf16[64,8,4096]{2,1,0:T(8,128)(2,1)}), bf16[64,8,4096]{2,1,0:T(8,128)(2,1)}, u32[]{:S(2)}, u32[]{:S(2)}) async-start(bf16[64,8,4096]{2,1,0:T(8,128)(2,1)} %bitcast.86), calls=%async_computation.1 | async-start | bytes 8388608 | tf_op jit(solution)/shard_map/all_to_all | solution.py:23
  59.9 4.5 %select_bitcast_fusion.4 = (bf16[4096,256]{1,0:T(8,128)(2,1)}, bf16[4096,256]{1,0:T(8,128)(2,1)}) fusion(pred[]{:T(512)S(6)} %not.3, bf16[2,4096,256]{2,1,0:T(8,128)(2,1)} %param.10, pred[]{:T(512)S(6)} %eq.90), kind=kLoop, calls=%fused_computation.34 | loop fusion | flops 2097152 | bytes 8388610 | tf_op jit(solution)/shard_map/jit(_where)/select_n | solution.py:50
  64.4 5.1 %collective-permute-start.4 = (bf16[4096,256]{1,0:T(8,128)(2,1)}, bf16[4096,256]{1,0:T(8,128)(2,1)}, u32[]{:S(2)}, u32[]{:S(2)}) collective-permute-start(bf16[4096,256]{1,0:T(8,128)(2,1)} %get-tuple-element.15), channel_id=1, source_target_pairs={{0,0},{2,2},{4,8},{6,10},{8,4},{10,6},{12,12},{14,14},{1,1},{3,3},... | collective-permute-start | bytes 6291464 | tf_op jit(solution)/shard_map/ppermute | solution.py:67
  69.6 43.5 %all-to-all-done.1 = bf16[64,8,4096]{2,1,0:T(8,128)(2,1)} async-done(((bf16[64,8,4096]{2,1,0:T(8,128)(2,1)}), bf16[64,8,4096]{2,1,0:T(8,128)(2,1)}, u32[]{:S(2)}, u32[]{:S(2)}) %all-to-all-start.1) | async-done | bytes 4194336 | tf_op jit(solution)/shard_map/all_to_all | solution.py:23
  124.3 21.1 %collective-permute-done.4 = bf16[4096,256]{1,0:T(8,128)(2,1)} collective-permute-done((bf16[4096,256]{1,0:T(8,128)(2,1)}, bf16[4096,256]{1,0:T(8,128)(2,1)}, u32[]{:S(2)}, u32[]{:S(2)}) %collective-permute-start.4) | collective-permute-done | bytes 2097184 | tf_op jit(solution)/shard_map/ppermute | solution.py:67
  147.1 43.1 %collective-permute-done.2 = bf16[256,4096]{1,0:T(8,128)(2,1)S(1)} collective-permute-done((bf16[256,4096]{1,0:T(8,128)(2,1)S(1)}, bf16[256,4096]{1,0:T(8,128)(2,1)S(1)}, u32[]{:S(2)}, u32[]{:S(2)}) %collective-permute-start.2) | collective-permute-done | bytes 2097184 | tf_op jit(solution)/shard_map/ppermute | solution.py:70
  190.6 12.2 %collective-permute-done.3 = bf16[256,4096]{1,0:T(8,128)(2,1)S(1)} collective-permute-done((bf16[256,4096]{1,0:T(8,128)(2,1)S(1)}, bf16[256,4096]{1,0:T(8,128)(2,1)S(1)}, u32[]{:S(2)}, u32[]{:S(2)}) %collective-permute-start.3) | collective-permute-done | bytes 2097184 | tf_op jit(solution)/shard_map/ppermute | solution.py:70
  216.5 7.3 %collective-permute-done.6 = bf16[512,4096]{1,0:T(8,128)(2,1)} collective-permute-done((bf16[512,4096]{1,0:T(8,128)(2,1)S(1)}, bf16[512,4096]{1,0:T(8,128)(2,1)}, u32[]{:S(2)}, u32[]{:S(2)}) %collective-permute-start.6) | collective-permute-done | bytes 4194336 | tf_op jit(solution)/shard_map/ppermute | solution.py:101
  223.8 6.6 %fusion.5 = bf16[64,8,4096]{2,1,0:T(8,128)(2,1)} fusion(bf16[512,4096]{1,0:T(8,128)(2,1)} %collective-permute-done.6, bf16[512,4096]{1,0:T(8,128)(2,1)S(1)} %convolution_convert_fusion.1, bf16[512,4096]{1,0:T(8,128)(2,1)S(1)} %get-tuple-element.25, pred[]{:T(512)S(6)} %eq.86), kind=kLoop, calls=%fused_computation.16 | loop fusion | flops 10485760 | bytes 16777216 | tf_op jit(solution)/shard_map/reshape | solution.py:103
  230.4 7.5 %all-to-all-start.2 = ((bf16[64,8,4096]{2,1,0:T(8,128)(2,1)}), bf16[64,8,4096]{2,1,0:T(8,128)(2,1)}, u32[]{:S(2)}, u32[]{:S(2)}) async-start(bf16[64,8,4096]{2,1,0:T(8,128)(2,1)} %fusion.5), calls=%async_computation.2 | async-start | bytes 8388608 | tf_op jit(solution)/shard_map/all_to_all | solution.py:23
  237.9 5.0 %convolution_convert_fusion.2 = bf16[256,4096]{1,0:T(8,128)(2,1)} fusion(bf16[512,4096]{1,0:T(8,128)(2,1)} %copy-done, bf16[512,512]{1,0:T(8,128)(2,1)S(1)} %get-tuple-element.22), kind=kOutput, calls=%fused_computation.7 | convolution fusion | flops 1074790400 | bytes 6553600 | tf_op jit(solution)/shard_map/dot_general | solution.py:19
  245.6 5.0 %collective-permute-start.11 = (bf16[256,4096]{1,0:T(8,128)(2,1)}, bf16[256,4096]{1,0:T(8,128)(2,1)}, u32[]{:S(2)}, u32[]{:S(2)}) collective-permute-start(bf16[256,4096]{1,0:T(8,128)(2,1)} %convolution_convert_fusion.3), channel_id=1, source_target_pairs={{0,0},{2,2},{8,4},{10,6},{4,8},{6,10},{12,12},{14,14},{1,1},{3,3},... | collective-permute-start | bytes 6291464 | tf_op jit(solution)/shard_map/ppermute | solution.py:116
  260.8 29.4 %all-to-all-done.2 = bf16[64,8,4096]{2,1,0:T(8,128)(2,1)} async-done(((bf16[64,8,4096]{2,1,0:T(8,128)(2,1)}), bf16[64,8,4096]{2,1,0:T(8,128)(2,1)}, u32[]{:S(2)}, u32[]{:S(2)}) %all-to-all-start.2) | async-done | bytes 4194336 | tf_op jit(solution)/shard_map/all_to_all | solution.py:23
  296.0 36.0 %collective-permute-done.11 = bf16[256,4096]{1,0:T(8,128)(2,1)} collective-permute-done((bf16[256,4096]{1,0:T(8,128)(2,1)}, bf16[256,4096]{1,0:T(8,128)(2,1)}, u32[]{:S(2)}, u32[]{:S(2)}) %collective-permute-start.11) | collective-permute-done | bytes 2097184 | tf_op jit(solution)/shard_map/ppermute | solution.py:116
  332.0 4.5 %select_bitcast_fusion.1 = (bf16[1,256,4096]{2,1,0:T(8,128)(2,1)}, bf16[1,256,4096]{2,1,0:T(8,128)(2,1)}) fusion(bf16[256,4096]{1,0:T(8,128)(2,1)} %collective-permute-done.11, bf16[256,4096]{1,0:T(8,128)(2,1)} %collective-permute-done.12, pred[]{:T(512)S(6)} %eq.90), kind=kLoop, calls=%fused_computation.31 | loop fusion | flops 2097152 | bytes 8388609 | tf_op jit(solution)/shard_map/stack | solution.py:125
  342.8 9.1 %all-to-all-start.4 = ((f32[128,8,128]{2,1,0:T(8,128)}), f32[128,8,128]{2,1,0:T(8,128)S(1)}, u32[]{:S(2)}, u32[]{:S(2)}) async-start(f32[128,8,128]{2,1,0:T(8,128)} %reshape.259), calls=%async_computation.4 | async-start | bytes 1048576 | tf_op jit(solution)/shard_map/all_to_all | solution.py:23
  351.9 30.3 %collective-permute-done.9 = bf16[4096,256]{1,0:T(8,128)(2,1)} collective-permute-done((bf16[4096,256]{1,0:T(8,128)(2,1)}, bf16[4096,256]{1,0:T(8,128)(2,1)}, u32[]{:S(2)}, u32[]{:S(2)}) %collective-permute-start.9) | collective-permute-done | bytes 2097184 | tf_op jit(solution)/shard_map/ppermute | solution.py:109
  382.4 4.5 %select_bitcast_fusion.3 = (bf16[1,4096,256]{2,1,0:T(8,128)(2,1)}, bf16[1,4096,256]{2,1,0:T(8,128)(2,1)}) fusion(bf16[4096,256]{1,0:T(8,128)(2,1)} %collective-permute-done.9, bf16[4096,256]{1,0:T(8,128)(2,1)} %collective-permute-done.10, pred[]{:T(512)S(6)} %eq.90), kind=kLoop, calls=%fused_computation.33 | loop fusion | flops 2097152 | bytes 8388609 | tf_op jit(solution)/shard_map/stack | solution.py:122
  388.3 8.2 %all-to-all-start.5 = ((f32[128,8,128]{2,1,0:T(8,128)}), f32[128,8,128]{2,1,0:T(8,128)S(1)}, u32[]{:S(2)}, u32[]{:S(2)}) async-start(f32[128,8,128]{2,1,0:T(8,128)} %broadcast_in_dim.17), calls=%async_computation.5 | async-start | bytes 1048576 | tf_op jit(solution)/shard_map/all_to_all | solution.py:23
  404.2 5.5 %all-to-all-done.5 = f32[128,8,128]{2,1,0:T(8,128)S(1)} async-done(((f32[128,8,128]{2,1,0:T(8,128)}), f32[128,8,128]{2,1,0:T(8,128)S(1)}, u32[]{:S(2)}, u32[]{:S(2)}) %all-to-all-start.5) | async-done | bytes 524320 | tf_op jit(solution)/shard_map/all_to_all | solution.py:23
  410.5 4.8 %all-to-all-start.3 = ((bf16[16,16,2048]{2,1,0:T(8,128)(2,1)}), bf16[16,16,2048]{2,1,0:T(8,128)(2,1)S(1)}, u32[]{:S(2)}, u32[]{:S(2)}) async-start(bf16[16,16,2048]{2,1,0:T(8,128)(2,1)} %bitcast.24), calls=%async_computation.3 | async-start | bytes 2097152 | tf_op jit(solution)/shard_map/all_to_all | solution.py:23
  422.7 10.0 %all-to-all-done.3 = bf16[16,16,2048]{2,1,0:T(8,128)(2,1)S(1)} async-done(((bf16[16,16,2048]{2,1,0:T(8,128)(2,1)}), bf16[16,16,2048]{2,1,0:T(8,128)(2,1)S(1)}, u32[]{:S(2)}, u32[]{:S(2)}) %all-to-all-start.3) | async-done | bytes 1048608 | tf_op jit(solution)/shard_map/all_to_all | solution.py:23
  (104 shorter events, 84.1 us)
Async XLA Ops:
  6.6 37.2 %copy-start.10 = (bf16[4096,32]{0,1:T(8,128)(2,1)S(1)}, bf16[4096,32]{0,1:T(8,128)(2,1)}, u32[]{:S(2)}) copy-start(bf16[4096,32]{0,1:T(8,128)(2,1)} %param.9) | copy-start | bytes 786436
  6.6 37.2 %all-to-all-start = ((bf16[16,16,4096]{2,1,0:T(8,128)(2,1)}), bf16[16,16,4096]{2,1,0:T(8,128)(2,1)S(1)}, u32[]{:S(2)}, u32[]{:S(2)}) async-start(bf16[16,16,4096]{2,1,0:T(8,128)(2,1)} %bitcast.87), calls=%async_computation | async-start | bytes 4194304 | tf_op jit(solution)/shard_map/all_to_all | solution.py:23
  44.5 1.6 collective-permute-start
  50.7 62.4 %all-to-all-start.1 = ((bf16[64,8,4096]{2,1,0:T(8,128)(2,1)}), bf16[64,8,4096]{2,1,0:T(8,128)(2,1)}, u32[]{:S(2)}, u32[]{:S(2)}) async-start(bf16[64,8,4096]{2,1,0:T(8,128)(2,1)} %bitcast.86), calls=%async_computation.1 | async-start | bytes 8388608 | tf_op jit(solution)/shard_map/all_to_all | solution.py:23
  64.4 80.9 %collective-permute-start.4 = (bf16[4096,256]{1,0:T(8,128)(2,1)}, bf16[4096,256]{1,0:T(8,128)(2,1)}, u32[]{:S(2)}, u32[]{:S(2)}) collective-permute-start(bf16[4096,256]{1,0:T(8,128)(2,1)} %get-tuple-element.15), channel_id=1, source_target_pairs={{0,0},{2,2},{4,8},{6,10},{8,4},{10,6},{12,12},{14,14},{1,1},{3,3},... | collective-permute-start | bytes 6291464 | tf_op jit(solution)/shard_map/ppermute | solution.py:67
  113.1 8.1 %copy-start.7 = (bf16[4096,256]{1,0:T(8,128)(2,1)S(1)}, bf16[4096,256]{1,0:T(8,128)(2,1)}, u32[]{:S(2)}) copy-start(bf16[4096,256]{1,0:T(8,128)(2,1)} %get-tuple-element.14) | copy-start | bytes 6291460
  113.1 89.9 %collective-permute-start.1 = (bf16[512,4096]{1,0:T(8,128)(2,1)}, bf16[512,4096]{1,0:T(8,128)(2,1)S(1)}, u32[]{:S(2)}, u32[]{:S(2)}) collective-permute-start(bf16[512,4096]{1,0:T(8,128)(2,1)} %bitcast.12), channel_id=1, source_target_pairs={{0,8},{8,0},{1,9},{9,1},{2,10},{10,2},{3,11},{11,3},{4,12},{12,4},... | collective-permute-start | bytes 12582920 | tf_op jit(solution)/shard_map/ppermute | solution.py:87
  117.6 72.6 %collective-permute-start.2 = (bf16[256,4096]{1,0:T(8,128)(2,1)S(1)}, bf16[256,4096]{1,0:T(8,128)(2,1)S(1)}, u32[]{:S(2)}, u32[]{:S(2)}) collective-permute-start(bf16[256,4096]{1,0:T(8,128)(2,1)S(1)} %get-tuple-element.13), channel_id=1, source_target_pairs={{0,0},{2,2},{4,8},{6,10},{8,4},{10,6},{12,12},{14,14},{1,1},{3,3},... | collective-permute-start | bytes 6291464 | tf_op jit(solution)/shard_map/ppermute | solution.py:70
  121.2 69.2 %collective-permute-start.5 = (bf16[4096,256]{1,0:T(8,128)(2,1)S(1)}, bf16[4096,256]{1,0:T(8,128)(2,1)S(1)}, u32[]{:S(2)}, u32[]{:S(2)}) collective-permute-start(bf16[4096,256]{1,0:T(8,128)(2,1)S(1)} %copy-done.7), channel_id=1, source_target_pairs={{0,2},{2,0},{4,10},{6,8},{8,6},{10,4},{12,14},{14,12},{1,3},{3,1},... | collective-permute-start | bytes 6291464 | tf_op jit(solution)/shard_map/ppermute | solution.py:67
  122.7 80.1 %collective-permute-start.3 = (bf16[256,4096]{1,0:T(8,128)(2,1)S(1)}, bf16[256,4096]{1,0:T(8,128)(2,1)S(1)}, u32[]{:S(2)}, u32[]{:S(2)}) collective-permute-start(bf16[256,4096]{1,0:T(8,128)(2,1)S(1)} %get-tuple-element.12), channel_id=1, source_target_pairs={{0,2},{2,0},{4,10},{6,8},{8,6},{10,4},{12,14},{14,12},{1,3},{3,1},... | collective-permute-start | bytes 6291464 | tf_op jit(solution)/shard_map/ppermute | solution.py:70
  216.4 7.4 %collective-permute-start.6 = (bf16[512,4096]{1,0:T(8,128)(2,1)S(1)}, bf16[512,4096]{1,0:T(8,128)(2,1)}, u32[]{:S(2)}, u32[]{:S(2)}) collective-permute-start(bf16[512,4096]{1,0:T(8,128)(2,1)S(1)} %get-tuple-element.24), channel_id=1, source_target_pairs={{0,8},{8,0},{1,9},{9,1},{2,10},{10,2},{3,11},{11,3},{4,12},{12,4},... | collective-permute-start | bytes 12582920 | tf_op jit(solution)/shard_map/ppermute | solution.py:101
  230.4 59.9 %all-to-all-start.2 = ((bf16[64,8,4096]{2,1,0:T(8,128)(2,1)}), bf16[64,8,4096]{2,1,0:T(8,128)(2,1)}, u32[]{:S(2)}, u32[]{:S(2)}) async-start(bf16[64,8,4096]{2,1,0:T(8,128)(2,1)} %fusion.5), calls=%async_computation.2 | async-start | bytes 8388608 | tf_op jit(solution)/shard_map/all_to_all | solution.py:23
  242.9 8.3 %copy-start.6 = (bf16[512,4096]{1,0:T(8,128)(2,1)S(1)}, bf16[512,4096]{1,0:T(8,128)(2,1)}, u32[]{:S(2)}) copy-start(bf16[512,4096]{1,0:T(8,128)(2,1)} %copy-done.5) | copy-start | bytes 12582916
  242.9 8.3 %copy-start.13 = (bf16[512,512]{1,0:T(8,128)(2,1)S(1)}, bf16[512,512]{1,0:T(8,128)(2,1)}, u32[]{:S(2)}) copy-start(bf16[512,512]{1,0:T(8,128)(2,1)} %copy-done.12) | copy-start | bytes 1572868
  245.6 86.4 %collective-permute-start.11 = (bf16[256,4096]{1,0:T(8,128)(2,1)}, bf16[256,4096]{1,0:T(8,128)(2,1)}, u32[]{:S(2)}, u32[]{:S(2)}) collective-permute-start(bf16[256,4096]{1,0:T(8,128)(2,1)} %convolution_convert_fusion.3), channel_id=1, source_target_pairs={{0,0},{2,2},{8,4},{10,6},{4,8},{6,10},{12,12},{14,14},{1,1},{3,3},... | collective-permute-start | bytes 6291464 | tf_op jit(solution)/shard_map/ppermute | solution.py:116
  250.6 81.4 %collective-permute-start.12 = (bf16[256,4096]{1,0:T(8,128)(2,1)}, bf16[256,4096]{1,0:T(8,128)(2,1)}, u32[]{:S(2)}, u32[]{:S(2)}) collective-permute-start(bf16[256,4096]{1,0:T(8,128)(2,1)} %convolution_convert_fusion.2), channel_id=1, source_target_pairs={{2,0},{0,2},{10,4},{8,6},{6,8},{4,10},{14,12},{12,14},{3,1},{1,3},... | collective-permute-start | bytes 6291464 | tf_op jit(solution)/shard_map/ppermute | solution.py:116
  253.8 128.4 %collective-permute-start.9 = (bf16[4096,256]{1,0:T(8,128)(2,1)}, bf16[4096,256]{1,0:T(8,128)(2,1)}, u32[]{:S(2)}, u32[]{:S(2)}) collective-permute-start(bf16[4096,256]{1,0:T(8,128)(2,1)} %convolution_convert_fusion.5), channel_id=1, source_target_pairs={{0,0},{2,2},{8,4},{10,6},{4,8},{6,10},{12,12},{14,14},{1,1},{3,3},... | collective-permute-start | bytes 6291464 | tf_op jit(solution)/shard_map/ppermute | solution.py:109
  260.2 122.2 %collective-permute-start.10 = (bf16[4096,256]{1,0:T(8,128)(2,1)}, bf16[4096,256]{1,0:T(8,128)(2,1)}, u32[]{:S(2)}, u32[]{:S(2)}) collective-permute-start(bf16[4096,256]{1,0:T(8,128)(2,1)} %convolution_convert_fusion.4), channel_id=1, source_target_pairs={{2,0},{0,2},{10,4},{8,6},{6,8},{4,10},{14,12},{12,14},{3,1},{1,3},... | collective-permute-start | bytes 6291464 | tf_op jit(solution)/shard_map/ppermute | solution.py:109
  293.7 47.0 %collective-permute-start.8 = (f32[32,256]{1,0:T(8,128)S(1)}, f32[32,256]{1,0:T(8,128)S(1)}, u32[]{:S(2)}, u32[]{:S(2)}) collective-permute-start(f32[32,256]{1,0:T(8,128)S(1)} %fusion.11), channel_id=1, source_target_pairs={{0,8},{8,0},{1,9},{9,1},{2,10},{10,2},{3,11},{11,3},{4,12},{12,4},... | collective-permute-start | bytes 98312 | tf_op jit(solution)/shard_map/ppermute | solution.py:132
  339.6 56.9 %collective-permute-start.7 = (bf16[512,2048]{1,0:T(8,128)(2,1)}, bf16[512,2048]{1,0:T(8,128)(2,1)}, u32[]{:S(2)}, u32[]{:S(2)}) collective-permute-start(bf16[512,2048]{1,0:T(8,128)(2,1)} %slice.61), channel_id=1, source_target_pairs={{0,8},{8,0},{1,9},{9,1},{2,10},{10,2},{3,11},{11,3},{4,12},{12,4},... | collective-permute-start | bytes 6291464 | tf_op jit(solution)/shard_map/ppermute | solution.py:129
  342.8 44.6 %all-to-all-start.4 = ((f32[128,8,128]{2,1,0:T(8,128)}), f32[128,8,128]{2,1,0:T(8,128)S(1)}, u32[]{:S(2)}, u32[]{:S(2)}) async-start(f32[128,8,128]{2,1,0:T(8,128)} %reshape.259), calls=%async_computation.4 | async-start | bytes 1048576 | tf_op jit(solution)/shard_map/all_to_all | solution.py:23
  388.3 21.4 %all-to-all-start.5 = ((f32[128,8,128]{2,1,0:T(8,128)}), f32[128,8,128]{2,1,0:T(8,128)S(1)}, u32[]{:S(2)}, u32[]{:S(2)}) async-start(f32[128,8,128]{2,1,0:T(8,128)} %broadcast_in_dim.17), calls=%async_computation.5 | async-start | bytes 1048576 | tf_op jit(solution)/shard_map/all_to_all | solution.py:23
  402.7 12.6 %copy-start.2 = (bf16[1,256,4096]{2,1,0:T(8,128)(2,1)S(1)}, bf16[1,256,4096]{2,1,0:T(8,128)(2,1)}, u32[]{:S(2)}) copy-start(bf16[1,256,4096]{2,1,0:T(8,128)(2,1)} %get-tuple-element.8) | copy-start | bytes 6291460
  410.5 22.2 %all-to-all-start.3 = ((bf16[16,16,2048]{2,1,0:T(8,128)(2,1)}), bf16[16,16,2048]{2,1,0:T(8,128)(2,1)S(1)}, u32[]{:S(2)}, u32[]{:S(2)}) async-start(bf16[16,16,2048]{2,1,0:T(8,128)(2,1)} %bitcast.24), calls=%async_computation.3 | async-start | bytes 2097152 | tf_op jit(solution)/shard_map/all_to_all | solution.py:23
  (9 other events, 28.2 us)

commit v2 on v1

v2 whole, which is shorter than its diff:
```python
import functools

import jax
import jax.numpy as jnp
from jax import lax
from jax.experimental import pallas as pl
from jax.experimental.pallas import tpu as pltpu
from jax.sharding import Mesh
from jax.sharding import PartitionSpec as P

soft_cap = 15.0
f32 = jnp.float32
bf16 = jnp.bfloat16

axes = ("yh", "x", "core", "z", "b")
sizes = (2, 4, 2, 4, 2)
owners = ("yh", "x", "core")
planes = ("yh", "x", "z")
column = ("core", "z")
swap = [(0, 1), (1, 0)]
NN = ((1,), (0,))
NT = ((1,), (1,))
TN = ((0,), (0,))

any_spec = pl.BlockSpec(memory_space=pl.ANY)
vmem_spec = pl.BlockSpec(memory_space=pltpu.VMEM)
smem_spec = pl.BlockSpec(memory_space=pltpu.SMEM)
roomy = pltpu.CompilerParams(vmem_limit_bytes=48 * 1024 * 1024)


def mm(left, right, contract=NN):
    return lax.dot_general(left, right, (contract, ((), ())), preferred_element_type=f32)


def exchange(array, names):
    return lax.all_to_all(array, names, split_axis=0, concat_axis=0, tiled=True)


def split_high_low(value):
    high = lax.reduce_precision(value, 8, 7)
    return high.astype(bf16), (value - high).astype(bf16)


def weight_round(step):
    pairs = []
    for s in range(2):
        for z in range(4):
            q = (z + step) % 4
            pairs.append((s * 4 + z, (q % 2) * 4 + 2 * s + q // 2))
    return pairs


def back_round(step):
    return [(b, a) for a, b in weight_round(step)]


def piece_copies(piece, w_in, w_out, packed, sem, back):
    expert = piece // 2
    if piece % 2 == 1:
        pairs = [(w_out.at[expert], packed)]
    else:
        pairs = [
            (
                w_in.at[expert, pl.ds(256 * a, 256), :],
                packed.at[:, pl.ds(256 * a, 256)],
            )
            for a in range(16)
        ]
    for one, two in pairs:
        source, target = (two, one) if back else (one, two)
        pltpu.make_async_copy(source, target, sem).start()


def pack_body(z_ref, w_in, w_out, p0, p1, p2, p3, sems):
    packed = (p0, p1, p2, p3)
    for step in range(4):
        for piece in range(4):
            @pl.when((z_ref[0] + step) % 4 == piece)
            def _():
                piece_copies(piece, w_in, w_out, packed[step], sems.at[step], False)
    for step in range(4):
        pltpu.make_async_copy(w_out.at[0], packed[step], sems.at[step]).wait()


def pack(z, w_in, w_out):
    shape = jax.ShapeDtypeStruct((256, 4096), bf16)
    return pl.pallas_call(
        pack_body,
        out_shape=(shape,) * 4,
        in_specs=[smem_spec, any_spec, any_spec],
        out_specs=(any_spec,) * 4,
        scratch_shapes=[pltpu.SemaphoreType.DMA((4,))],
        cost_estimate=pl.CostEstimate(flops=0, bytes_accessed=16 << 20, transcendentals=0),
    )(z, w_in, w_out)


def unpack_body(z_ref, p0, p1, p2, p3, w_in, w_out, sems):
    packed = (p0, p1, p2, p3)
    for step in range(4):
        for piece in range(4):
            @pl.when((z_ref[0] + step) % 4 == piece)
            def _():
                piece_copies(piece, w_in, w_out, packed[step], sems.at[step], True)
    for step in range(4):
        pltpu.make_async_copy(packed[step], w_out.at[0], sems.at[step]).wait()


def unpack(z, pieces):
    return pl.pallas_call(
        unpack_body,
        out_shape=(
            jax.ShapeDtypeStruct((2, 4096, 256), bf16),
            jax.ShapeDtypeStruct((2, 256, 4096), bf16),
        ),
        in_specs=[smem_spec] + [any_spec] * 4,
        out_specs=(any_spec, any_spec),
        scratch_shapes=[pltpu.SemaphoreType.DMA((4,))],
        cost_estimate=pl.CostEstimate(flops=0, bytes_accessed=16 << 20, transcendentals=0),
    )(z, *pieces)


def load_weights(core, weights, held, sems):
    for slot in range(4):
        @pl.when(core == 0)
        def _():
            pltpu.make_async_copy(weights[slot], held.at[slot], sems.at[slot]).start()

        @pl.when(core == 1)
        def _():
            pltpu.make_async_copy(weights[(slot + 1) % 4], held.at[slot], sems.at[slot]).start()


def wait_weights(slot, weights, held, sems):
    pltpu.make_async_copy(weights[0], held.at[slot], sems.at[slot]).wait()


def up_body(core_ref, r00, r01, r10, r11, w0, w1, w2, w3, pre_ref, send_ref, held, sems):
    core = core_ref[0]
    weights = (w0, w1, w2, w3)
    load_weights(core, weights, held, sems)

    def slot_step(slot, carry):
        wait_weights(slot, weights, held, sems)
        for block, (low, high) in enumerate(((r00, r01), (r10, r11))):
            here = pl.ds(256 * block, 256)

            @pl.when(core == 0)
            def _():
                total = jnp.zeros((256, 256), f32)
                for a in range(16):
                    rows = (low if a < 8 else high)[:, 256 * (a % 8) : 256 * (a % 8) + 256]
                    total += mm(rows, held[slot, :, 256 * a : 256 * a + 256])
                pre_ref[slot, here, :] = total
                send_ref[slot, here, :] = (total * jax.nn.sigmoid(total)).astype(bf16)

            @pl.when(core == 1)
            def _():
                total = mm(low[...], held[slot, :, :2048], NT) + mm(high[...], held[slot, :, 2048:], NT)
                send_ref[slot, here, :] = total.astype(bf16)

        return carry

    lax.fori_loop(0, 4, slot_step, 0)


def up(core, rows, weights):
    return pl.pallas_call(
        up_body,
        out_shape=(
            jax.ShapeDtypeStruct((4, 512, 256), f32),
            jax.ShapeDtypeStruct((4, 512, 256), bf16),
        ),
        in_specs=[smem_spec] + [vmem_spec] * 4 + [any_spec] * 4,
        out_specs=(vmem_spec, vmem_spec),
        scratch_shapes=[pltpu.VMEM((4, 256, 4096), bf16), pltpu.SemaphoreType.DMA((4,))],
        compiler_params=roomy,
        cost_estimate=pl.CostEstimate(flops=2 * 512 * 4096 * 1024, bytes_accessed=15 << 20, transcendentals=512 * 1024),
    )(core, *rows, *weights)


def down_body(core_ref, pre_ref, got_ref, w0, w1, w2, w3, o00, o01, o10, o11, q_ref, held, sems):
    core = core_ref[0]
    weights = (w0, w1, w2, w3)
    load_weights(core, weights, held, sems)

    @pl.when(core == 0)
    def _():
        for slot in range(4):
            pre_act = pre_ref[slot]
            sigma_pre = jax.nn.sigmoid(pre_act)
            slope = got_ref[slot].astype(f32) * sigma_pre * (1.0 + pre_act * (1.0 - sigma_pre))
            q_ref[slot] = slope.astype(bf16)

    @pl.when(core == 1)
    def _():
        q_ref[...] = got_ref[...]

    for slot in range(4):
        wait_weights(slot, weights, held, sems)
    for half, (own, other) in enumerate(((o00, o10), (o01, o11))):
        def part_step(a, carry):
            there = pl.ds(pl.multiple_of(256 * a + 2048 * half, 256), 256)
            here = pl.ds(pl.multiple_of(256 * a, 256), 256)
            for block, target in enumerate((own, other)):
                rows = pl.ds(256 * block, 256)

                @pl.when(core == 0)
                def _():
                    total = jnp.zeros((256, 256), f32)
                    for slot in range(4):
                        total += mm(q_ref[slot, rows, :], held[slot, :, there], NT)
                    target[:, here] = total.astype(bf16)

                @pl.when(core == 1)
                def _():
                    total = jnp.zeros((256, 256), f32)
                    for slot in range(4):
                        total += mm(q_ref[slot, rows, :], held[slot, :, there])
                    target[:, here] = total.astype(bf16)

            return carry

        lax.fori_loop(0, 8, part_step, 0)


def down(core, pre_act, got, weights):
    piece = jax.ShapeDtypeStruct((256, 2048), bf16)
    return pl.pallas_call(
        down_body,
        out_shape=(piece,) * 4 + (jax.ShapeDtypeStruct((4, 512, 256), bf16),),
        in_specs=[smem_spec] + [vmem_spec] * 2 + [any_spec] * 4,
        out_specs=(vmem_spec,) * 5,
        scratch_shapes=[pltpu.VMEM((4, 256, 4096), bf16), pltpu.SemaphoreType.DMA((4,))],
        compiler_params=roomy,
        cost_estimate=pl.CostEstimate(flops=2 * 512 * 4096 * 1024, bytes_accessed=16 << 20, transcendentals=512 * 1024),
    )(core, pre_act, got, *weights)


def grads_body(core_ref, r00, r01, r10, r11, q_ref, g0, g1, g2, g3, held, sems):
    core = core_ref[0]
    grads = (g0, g1, g2, g3)

    @pl.when(core == 0)
    def _():
        for half, (own, other) in enumerate(((r00, r10), (r01, r11))):
            def token_step(a, carry):
                here = pl.ds(pl.multiple_of(256 * a, 256), 256)
                there = pl.ds(pl.multiple_of(256 * a + 2048 * half, 256), 256)
                for slot in range(4):
                    total = mm(own[:, here], q_ref[slot, :256, :], TN)
                    total += mm(other[:, here], q_ref[slot, 256:, :], TN)
                    held[slot, :, there] = total.astype(bf16)
                return carry

            lax.fori_loop(0, 8, token_step, 0)

    @pl.when(core == 1)
    def _():
        for half, (own, other) in enumerate(((r00, r10), (r01, r11))):
            def grad_step(a, carry):
                here = pl.ds(pl.multiple_of(256 * a, 256), 256)
                there = pl.ds(pl.multiple_of(256 * a + 2048 * half, 256), 256)
                for slot in range(4):
                    total = mm(q_ref[slot, :256, :], own[:, here], TN)
                    total += mm(q_ref[slot, 256:, :], other[:, here], TN)
                    held[slot, :, there] = total.astype(bf16)
                return carry

            lax.fori_loop(0, 8, grad_step, 0)

    for slot in range(4):
        @pl.when(core == 0)
        def _():
            pltpu.make_async_copy(held.at[slot], grads[slot], sems.at[slot]).start()

        @pl.when(core == 1)
        def _():
            pltpu.make_async_copy(held.at[slot], grads[(slot + 1) % 4], sems.at[slot]).start()

    for slot in range(4):
        pltpu.make_async_copy(held.at[slot], grads[0], sems.at[slot]).wait()


def weight_grads(core, rows, units):
    shape = jax.ShapeDtypeStruct((256, 4096), bf16)
    return pl.pallas_call(
        grads_body,
        out_shape=(shape,) * 4,
        in_specs=[smem_spec] + [vmem_spec] * 5,
        out_specs=(any_spec,) * 4,
        scratch_shapes=[pltpu.VMEM((4, 256, 4096), bf16), pltpu.SemaphoreType.DMA((4,))],
        compiler_params=roomy,
        cost_estimate=pl.CostEstimate(flops=2 * 512 * 4096 * 1024, bytes_accessed=13 << 20, transcendentals=0),
    )(core, *rows, units)


def shards(tokens, cotangent, group_of, mixer, w_in, w_out):
    seqs, positions, width = tokens.shape
    rows = seqs * positions
    core = lax.axis_index("core")
    first = core == 0
    half = width // 2
    core_at = core.astype(jnp.int32).reshape(1)
    z_at = lax.axis_index("z").astype(jnp.int32).reshape(1)
    tie = lax.optimization_barrier

    weights = [
        lax.ppermute(piece, column, weight_round(step))
        for step, piece in enumerate(pack(z_at, w_in, w_out))
    ]

    home = group_of % 16
    earlier = jnp.arange(seqs)[:, None] > jnp.arange(seqs)[None, :]
    same = (home[:, None, :] == home[None, :, :]) & earlier[:, :, None]
    member = jnp.sum(same.astype(jnp.int32), axis=1)
    place = home * 8 + jnp.arange(positions, dtype=jnp.int32)[None, :] * 2 + member
    hot = (place.reshape(1, rows) == jnp.arange(rows, dtype=jnp.int32)[:, None]).astype(bf16)
    tok = mm(hot, tokens.reshape(rows, width)).astype(bf16).reshape(8, 1, 16, width)
    cot = mm(hot, cotangent.reshape(rows, width)).astype(bf16).reshape(8, 1, 16, width)
    sent = jnp.concatenate([tok, cot], axis=1).reshape(16, 16, width)
    held = exchange(sent, owners).reshape(256, width)

    mixer_t = mixer.T
    logits = mm(mixer_t, held, NT)
    logits = jnp.where(first, logits, lax.ppermute(logits, "core", swap))
    scaled = jnp.tanh(logits / soft_cap)
    exponent = jnp.exp(soft_cap * scaled)
    column_of = jnp.arange(256, dtype=jnp.int32) // 2 % 8
    mask = (column_of[None, :] == jnp.arange(8, dtype=jnp.int32)[:, None]).astype(f32)
    spread = exponent[:, None, :] * mask[None]
    spread = spread / jnp.sum(spread, axis=2, keepdims=True)
    spread_high, spread_low = split_high_low(spread)
    flat_high, flat_low = spread_high.reshape(256, 256), spread_low.reshape(256, 256)

    def mix(side):
        part = held[:, half * side : half * side + half]
        return (mm(flat_high, part) + mm(flat_low, part)).astype(bf16).reshape(32, 8, half)

    mix_0, weights[0], weights[1] = tie((mix(0), weights[0], weights[1]))
    own_0 = exchange(mix_0, planes).reshape(256, half)
    other_0 = lax.ppermute(own_0, "b", swap)
    own_1 = exchange(mix(1), planes).reshape(256, half)
    own_1, weights[2], weights[3] = tie((own_1, weights[2], weights[3]))
    other_1 = lax.ppermute(own_1, "b", swap)
    expert_rows = (own_0, own_1, other_0, other_1)

    pre_act, given = up(core_at, expert_rows, weights)
    got = lax.ppermute(given, "core", swap)
    part_0, part_1, away_0, away_1, units = down(core_at, pre_act, got, weights)

    def home_sum(part, away):
        come = lax.ppermute(away, "b", swap)
        total = (part.astype(f32) + come.astype(f32)).astype(bf16)
        return exchange(total.reshape(32, 8, half), planes).reshape(256, half)

    back_0 = home_sum(part_0, away_0)
    back_1 = home_sum(part_1, away_1)

    grads = [
        lax.ppermute(piece, column, back_round(step))
        for step, piece in enumerate(weight_grads(core_at, expert_rows, units))
    ]

    back_half = jnp.where(first, back_1, lax.ppermute(back_0, "core", swap))
    dots = mm(back_0, held[:, :half], NT) + mm(back_1, held[:, half:], NT)
    dots = jnp.sum(dots.reshape(32, 8, 256) * mask[None], axis=1)
    d_weights = dots + lax.ppermute(dots, "core", swap)
    mixing = jnp.sum(spread, axis=1)
    column_sum = jnp.sum((mixing * d_weights)[:, None, :] * mask[None], axis=2, keepdims=True)
    column_sum = jnp.sum(column_sum * mask[None], axis=1)
    d_logits = mixing * (d_weights - column_sum) * (1.0 - scaled * scaled)
    d_high, d_low = split_high_low(d_logits)

    mixer_part = mm(d_high, held) + mm(d_low, held)
    mixer_part = jnp.where(first, mixer_part, jnp.zeros_like(mixer_part))
    pieces = exchange(mixer_part.reshape(128, 8, 128), axes)
    total = jnp.sum(pieces, axis=0, keepdims=True)

    mixer_half = jnp.where(first, mixer_t[:, half:], mixer_t[:, :half])
    grad_rows = (
        mm(flat_high, back_half, TN)
        + mm(flat_low, back_half, TN)
        + mm(d_high, mixer_half, TN)
        + mm(d_low, mixer_half, TN)
    )
    grad_rows = exchange(grad_rows.astype(bf16).reshape(16, 16, half), owners)
    grad_rows, grads[0], grads[1], grads[2], grads[3] = tie((grad_rows, *grads))
    grad_in, grad_out = unpack(z_at, grads)
    grad_rows = grad_rows.reshape(8, 2, 16, half)
    grad_tokens = jnp.concatenate(
        [mm(hot, grad_rows[:, 1 - side].reshape(rows, half), TN).astype(bf16) for side in range(2)],
        axis=1,
    ).reshape(seqs, positions, width)

    whole = exchange(jnp.broadcast_to(total, (128, 8, 128)), axes)
    grad_mixer = whole.reshape(32, width).T
    return (grad_tokens, grad_mixer, grad_in, grad_out)


def solution(mesh):
    fine = Mesh(mesh.devices.reshape(sizes), axes)
    dp, expert = ("yh", "x", "core"), ("z", "b")
    every = dp + expert
    return jax.shard_map(
        shards,
        mesh=fine,
        in_specs=(
            P(every, None, None),
            P(every, None, None),
            P(every, None),
            P(),
            P(dp, None, expert),
            P(dp, expert, None),
        ),
        out_specs=(
            P(every, None, None),
            P(),
            P(dp, None, expert),
            P(dp, expert, None),
        ),
        check_vma=False,
    )
```

time: 439 us -> 977 us (2.23)
  Pallas kernels: 0 us -> 548 us
  starting transfers between devices: 75.4 us -> 138 us
  other arithmetic: 35.5 us -> 8.93 us
  matrix products: 39 us -> 18.3 us
  waiting for transfers between devices: 268 us -> 248 us
    pallas_call x0 -> x5, Pallas kernels: none -> 548 us  [the longest x1 255 us: pack(): pl.pallas_call(pack_body, out_shape=(shape,) * 4, in_specs=[smem_spec, an...]
    ppermute x12 -> x15, starting transfers between devices: 25.7 us -> 55.8 us  [the longest x4 25.7 us: shards(): lax.ppermute(piece, column, back_round(step))]
    all_to_all x6 -> x8, starting transfers between devices: 47.4 us -> 77.2 us  [exchange(): return lax.all_to_all(array, names, split_axis=0, concat_axis=0, tiled=True)]
    all_to_all x6 -> x8, waiting for transfers between devices: 117 us -> 95.5 us  [exchange(): return lax.all_to_all(array, names, split_axis=0, concat_axis=0, tiled=True)]
    dot_general x22 -> x17, matrix products: 39 us -> 18.3 us  [mm(): lax.dot_general(left, right, (contract, ((), ())), preferred_element_type...]
    another operation x4 -> x0, other arithmetic: 15.5 us -> none  [the longest x2 8.62 us: shards(): jnp.stack([pick(even, grads_out[0], grads_out[1]), pick(even, grads_out[1...]
    ppermute x12 -> x15, waiting for transfers between devices: 151 us -> 152 us  [the longest x4 65.8 us: shards(): lax.ppermute(piece, column, weight_round(step))]
  transfers between devices with their start and end apart: 19 -> 24, of which waited for: 13 -> 13; matrix products, arithmetic and copies ran while one was open for 13% -> 2% of each run, Pallas kernels for 0% -> 27%
where the time goes in v2:
time: 977 us; the launch traced here: 974 us
  Pallas kernels  548 us (56%)
  waiting for transfers between devices  248 us (25%)
  starting transfers between devices  138 us (14%)
  matrix products  18.3 us (2%)
  local copies, waits for them, and re-layouts  11.3 us (1%)
    pallas_call x1, Pallas kernels, pack(): pl.pallas_call(pack_body, out_shape=(shape,) * 4, in_specs=[smem_spec, an...  255 us
    pallas_call x1, Pallas kernels, unpack(): pl.pallas_call(unpack_body, out_shape=(jax.ShapeDtypeStruct((2, 4096, 256...  255 us
    all_to_all x8, waiting for transfers between devices, exchange(): return lax.all_to_all(array, names, split_axis=0, concat_axis=0, tiled=True)  95.5 us
    all_to_all x8, starting transfers between devices, exchange(): return lax.all_to_all(array, names, split_axis=0, concat_axis=0, tiled=True)  77.2 us
    ppermute x4, waiting for transfers between devices, shards(): lax.ppermute(piece, column, weight_round(step))  65.8 us
    ppermute x2, waiting for transfers between devices, home_sum(): come = lax.ppermute(away, 'b', swap)  41.6 us
    ppermute x4, starting transfers between devices, shards(): lax.ppermute(piece, column, back_round(step))  25.7 us
    ppermute x4, starting transfers between devices, shards(): lax.ppermute(piece, column, weight_round(step))  24.8 us
  transfers between devices with their start and end apart: 24, of which 13 were waited for; matrix products, arithmetic and copies ran while one was open for 2% of the time, Pallas kernels for 27%

profile of v2, /device:TPU:1, one launch (start us, length us, event | category | flops | bytes accessed | tf_op | source)
XLA Modules:
  0.0 973.9 jit_solution(10804747119797869574)
XLA Ops:
  6.6 8.4 all-to-all-start
  15.1 255.3 %shard_map.93 = (bf16[256,4096]{1,0:T(8,128)(2,1)}, bf16[256,4096]{1,0:T(8,128)(2,1)}, bf16[256,4096]{1,0:T(8,128)(2,1)}, bf16[256,4096]{1,0:T(8,128)(2,1)}) custom-call(s32[1]{0:T(128)} %bitcast.10.z_ref, bf16[2,4096,256]{2,1,0:T(8,128)(2,1)} %w_in.1, bf16[2,256,4096]{2,1,0:T(8,128)(2,1)} %w_out.1), custom_call_target="tpu_custom_call" | custom-call | bytes 16777216 | tf_op jit(solution)/shard_map/pallas_call | solution.py:87
  281.4 13.8 %collective-permute-start.2 = (bf16[256,4096]{1,0:T(8,128)(2,1)}, bf16[256,4096]{1,0:T(8,128)(2,1)}, u32[]{:S(2)}, u32[]{:S(2)}) collective-permute-start(bf16[256,4096]{1,0:T(8,128)(2,1)} %get-tuple-element.33), channel_id=1, source_target_pairs={{0,8},{2,2},{4,10},{6,0},{8,12},{10,6},{12,14},{14,4},{1,9},{3,3},... | collective-permute-start | bytes 6291464 | tf_op jit(solution)/shard_map/ppermute | solution.py:308
  302.1 7.6 all-to-all-start.2
  311.7 65.8 %collective-permute-done.1.w0 = bf16[256,4096]{1,0:T(8,128)(2,1)} collective-permute-done((bf16[256,4096]{1,0:T(8,128)(2,1)}, bf16[256,4096]{1,0:T(8,128)(2,1)}, u32[]{:S(2)}, u32[]{:S(2)}) %collective-permute-start.1) | collective-permute-done | bytes 2097184 | tf_op jit(solution)/shard_map/ppermute | solution.py:308
  377.5 11.0 %all-to-all-start.1 = ((bf16[32,8,2048]{2,1,0:T(8,128)(2,1)}), bf16[32,8,2048]{2,1,0:T(8,128)(2,1)S(1)}, u32[]{:S(2)}, u32[]{:S(2)}) async-start(bf16[32,8,2048]{2,1,0:T(8,128)(2,1)} %fusion.7), calls=%async_computation.1 | async-start | bytes 2097152 | tf_op jit(solution)/shard_map/all_to_all | solution.py:36
  389.0 15.9 %all-to-all-done.1 = bf16[32,8,2048]{2,1,0:T(8,128)(2,1)S(1)} async-done(((bf16[32,8,2048]{2,1,0:T(8,128)(2,1)}), bf16[32,8,2048]{2,1,0:T(8,128)(2,1)S(1)}, u32[]{:S(2)}, u32[]{:S(2)}) %all-to-all-start.1) | async-done | bytes 1048608 | tf_op jit(solution)/shard_map/all_to_all | solution.py:36
  405.3 17.1 %collective-permute-done.6.r11 = bf16[256,2048]{1,0:T(8,128)(2,1)S(1)} collective-permute-done((bf16[256,2048]{1,0:T(8,128)(2,1)S(1)}, bf16[256,2048]{1,0:T(8,128)(2,1)S(1)}, u32[]{:S(2)}, u32[]{:S(2)}) %collective-permute-start.6) | collective-permute-done | bytes 1048608 | tf_op jit(solution)/shard_map/ppermute | solution.py:344
  422.4 22.5 %collective-permute-done.5.r10 = bf16[256,2048]{1,0:T(8,128)(2,1)S(1)} collective-permute-done((bf16[256,2048]{1,0:T(8,128)(2,1)S(1)}, bf16[256,2048]{1,0:T(8,128)(2,1)S(1)}, u32[]{:S(2)}, u32[]{:S(2)}) %collective-permute-start.5) | collective-permute-done | bytes 1048608 | tf_op jit(solution)/shard_map/ppermute | solution.py:341
  444.9 9.3 shard_map.94
  459.2 16.7 %shard_map.95 = (bf16[256,2048]{1,0:T(8,128)(2,1)S(1)}, bf16[256,2048]{1,0:T(8,128)(2,1)S(1)}, bf16[256,2048]{1,0:T(8,128)(2,1)}, bf16[256,2048]{1,0:T(8,128)(2,1)S(1)}, bf16[4,512,256]{2,1,0:T(8,128)(2,1)S(1)}) custom-call(s32[1]{0:T(128)} %bitcast.8.core_ref, f32[4,512,256]{2,1,0:T(8,128)} %get-tuple-element.42.pre_ref, bf16[4,512,256]{2,1,0:T(8,128)(2,1)} %copy-done.10, ...), custom_call_target="tpu_custom_call" | custom-call | flops 4294967296 | bytes 16777216 | tf_op jit(solution)/shard_map/pallas_call | solution.py:228
  478.4 22.1 %collective-permute-done.8 = bf16[256,2048]{1,0:T(8,128)(2,1)S(1)} collective-permute-done((bf16[256,2048]{1,0:T(8,128)(2,1)S(1)}, bf16[256,2048]{1,0:T(8,128)(2,1)S(1)}, u32[]{:S(2)}, u32[]{:S(2)}) %collective-permute-start.8) | collective-permute-done | bytes 1048608 | tf_op jit(solution)/shard_map/ppermute | solution.py:352
  501.8 10.0 %all-to-all-start.3 = ((bf16[32,8,2048]{2,1,0:T(8,128)(2,1)}), bf16[32,8,2048]{2,1,0:T(8,128)(2,1)}, u32[]{:S(2)}, u32[]{:S(2)}) async-start(bf16[32,8,2048]{2,1,0:T(8,128)(2,1)} %fusion.12), calls=%async_computation.3 | async-start | bytes 2097152 | tf_op jit(solution)/shard_map/all_to_all | solution.py:36
  511.9 19.6 %collective-permute-done.9 = bf16[256,2048]{1,0:T(8,128)(2,1)} collective-permute-done((bf16[256,2048]{1,0:T(8,128)(2,1)}, bf16[256,2048]{1,0:T(8,128)(2,1)}, u32[]{:S(2)}, u32[]{:S(2)}) %collective-permute-start.9) | collective-permute-done | bytes 1048608 | tf_op jit(solution)/shard_map/ppermute | solution.py:352
  537.8 6.3 all-to-all-start.4
  546.1 11.7 %all-to-all-done.4 = bf16[32,8,2048]{2,1,0:T(8,128)(2,1)} async-done(((bf16[32,8,2048]{2,1,0:T(8,128)(2,1)}), bf16[32,8,2048]{2,1,0:T(8,128)(2,1)}, u32[]{:S(2)}, u32[]{:S(2)}) %all-to-all-start.4) | async-done | bytes 1048608 | tf_op jit(solution)/shard_map/all_to_all | solution.py:36
  577.6 11.3 %shard_map.96 = (bf16[256,4096]{1,0:T(8,128)(2,1)}, bf16[256,4096]{1,0:T(8,128)(2,1)}, bf16[256,4096]{1,0:T(8,128)(2,1)}, bf16[256,4096]{1,0:T(8,128)(2,1)}) custom-call(s32[1]{0:T(128)} %bitcast.8.core_ref, bf16[256,2048]{1,0:T(8,128)(2,1)S(1)} %bitcast.70, bf16[256,2048]{1,0:T(8,128)(2,1)S(1)} %bitcast.67, bf16[256,2048]{1,0:T(8,128)(2,1)S(1)} %copy-done.3, ...), custom_call_target="tpu_custom_call" | custom-call | flops 4294967296 | bytes 13631488 | tf_op jit(solution)/shard_map/pallas_call | solution.py:286
  592.7 16.5 %collective-permute-start.13 = (bf16[256,4096]{1,0:T(8,128)(2,1)}, bf16[256,4096]{1,0:T(8,128)(2,1)}, u32[]{:S(2)}, u32[]{:S(2)}) collective-permute-start(bf16[256,4096]{1,0:T(8,128)(2,1)} %get-tuple-element.50), channel_id=1, source_target_pairs={{8,0},{2,2},{10,4},{0,6},{12,8},{6,10},{14,12},{4,14},{9,1},{3,3},... | collective-permute-start | bytes 6291464 | tf_op jit(solution)/shard_map/ppermute | solution.py:360
  609.3 5.4 collective-permute-start.15
  617.1 21.2 %all-to-all-start.7 = ((f32[128,8,128]{2,1,0:T(8,128)}), f32[128,8,128]{2,1,0:T(8,128)S(1)}, u32[]{:S(2)}, u32[]{:S(2)}) async-start(f32[128,8,128]{2,1,0:T(8,128)} %broadcast_in_dim.5), calls=%async_computation.7 | async-start | bytes 1048576 | tf_op jit(solution)/shard_map/all_to_all | solution.py:36
  644.0 47.6 %all-to-all-done.7 = f32[128,8,128]{2,1,0:T(8,128)S(1)} async-done(((f32[128,8,128]{2,1,0:T(8,128)}), f32[128,8,128]{2,1,0:T(8,128)S(1)}, u32[]{:S(2)}, u32[]{:S(2)}) %all-to-all-start.7) | async-done | bytes 524320 | tf_op jit(solution)/shard_map/all_to_all | solution.py:36
  691.7 7.4 all-to-all-start.5
  700.0 16.4 %all-to-all-done.5 = bf16[16,16,2048]{2,1,0:T(8,128)(2,1)S(1)} async-done(((bf16[16,16,2048]{2,1,0:T(8,128)(2,1)}), bf16[16,16,2048]{2,1,0:T(8,128)(2,1)S(1)}, u32[]{:S(2)}, u32[]{:S(2)}) %all-to-all-start.5) | async-done | bytes 1048608 | tf_op jit(solution)/shard_map/all_to_all | solution.py:36
  718.5 255.2 %shard_map.97 = (bf16[2,4096,256]{2,1,0:T(8,128)(2,1)}, bf16[2,256,4096]{2,1,0:T(8,128)(2,1)}) custom-call(s32[1]{0:T(128)} %bitcast.10.z_ref, bf16[256,4096]{1,0:T(8,128)(2,1)} %collective-permute-done.12.p0, bf16[256,4096]{1,0:T(8,128)(2,1)} %collective-permute-done.13.p1, bf16[256,4096]{1,0:T(8,128)(2,1)} %collective-permute-done.14.p2, ...), custom_call_target="tpu_custom_call" | custom-call | bytes 16777216 | tf_op jit(solution)/shard_map/pallas_call | solution.py:109
  (96 shorter events, 78.5 us)
Async XLA Ops:
  6.6 288.5 %all-to-all-start = ((bf16[16,16,4096]{2,1,0:T(8,128)(2,1)}), bf16[16,16,4096]{2,1,0:T(8,128)(2,1)S(1)}, u32[]{:S(2)}, u32[]{:S(2)}) async-start(bf16[16,16,4096]{2,1,0:T(8,128)(2,1)} %bitcast.80), calls=%async_computation | async-start | bytes 4194304 | tf_op jit(solution)/shard_map/all_to_all | solution.py:36
  270.4 118.2 %collective-permute-start.3 = (bf16[256,4096]{1,0:T(8,128)(2,1)}, bf16[256,4096]{1,0:T(8,128)(2,1)}, u32[]{:S(2)}, u32[]{:S(2)}) collective-permute-start(bf16[256,4096]{1,0:T(8,128)(2,1)} %get-tuple-element.35), channel_id=1, source_target_pairs={{0,2},{2,10},{4,0},{6,8},{8,6},{10,14},{12,4},{14,12},{1,3},{3,11}... | collective-permute-start | bytes 6291464 | tf_op jit(solution)/shard_map/ppermute | solution.py:308
  274.3 114.2 %collective-permute-start.4 = (bf16[256,4096]{1,0:T(8,128)(2,1)}, bf16[256,4096]{1,0:T(8,128)(2,1)}, u32[]{:S(2)}, u32[]{:S(2)}) collective-permute-start(bf16[256,4096]{1,0:T(8,128)(2,1)} %get-tuple-element.36), channel_id=1, source_target_pairs={{0,10},{2,0},{4,8},{6,2},{8,14},{10,4},{12,12},{14,6},{1,11},{3,1}... | collective-permute-start | bytes 6291464 | tf_op jit(solution)/shard_map/ppermute | solution.py:308
  276.3 101.2 %collective-permute-start.1 = (bf16[256,4096]{1,0:T(8,128)(2,1)}, bf16[256,4096]{1,0:T(8,128)(2,1)}, u32[]{:S(2)}, u32[]{:S(2)}) collective-permute-start(bf16[256,4096]{1,0:T(8,128)(2,1)} %get-tuple-element.32), channel_id=1, source_target_pairs={{0,0},{2,8},{4,2},{6,10},{8,4},{10,12},{12,6},{14,14},{1,1},{3,9},... | collective-permute-start | bytes 6291464 | tf_op jit(solution)/shard_map/ppermute | solution.py:308
  281.4 96.2 %collective-permute-start.2 = (bf16[256,4096]{1,0:T(8,128)(2,1)}, bf16[256,4096]{1,0:T(8,128)(2,1)}, u32[]{:S(2)}, u32[]{:S(2)}) collective-permute-start(bf16[256,4096]{1,0:T(8,128)(2,1)} %get-tuple-element.33), channel_id=1, source_target_pairs={{0,8},{2,2},{4,10},{6,0},{8,12},{10,6},{12,14},{14,4},{1,9},{3,3},... | collective-permute-start | bytes 6291464 | tf_op jit(solution)/shard_map/ppermute | solution.py:308
  295.9 4.0 collective-permute-start
  302.1 75.5 %all-to-all-start.2 = ((bf16[32,8,2048]{2,1,0:T(8,128)(2,1)}), bf16[32,8,2048]{2,1,0:T(8,128)(2,1)S(1)}, u32[]{:S(2)}, u32[]{:S(2)}) async-start(bf16[32,8,2048]{2,1,0:T(8,128)(2,1)} %fusion.6), calls=%async_computation.2 | async-start | bytes 2097152 | tf_op jit(solution)/shard_map/all_to_all | solution.py:36
  377.5 27.4 %all-to-all-start.1 = ((bf16[32,8,2048]{2,1,0:T(8,128)(2,1)}), bf16[32,8,2048]{2,1,0:T(8,128)(2,1)S(1)}, u32[]{:S(2)}, u32[]{:S(2)}) async-start(bf16[32,8,2048]{2,1,0:T(8,128)(2,1)} %fusion.7), calls=%async_computation.1 | async-start | bytes 2097152 | tf_op jit(solution)/shard_map/all_to_all | solution.py:36
  388.5 33.9 %collective-permute-start.6 = (bf16[256,2048]{1,0:T(8,128)(2,1)S(1)}, bf16[256,2048]{1,0:T(8,128)(2,1)S(1)}, u32[]{:S(2)}, u32[]{:S(2)}) collective-permute-start(bf16[256,2048]{1,0:T(8,128)(2,1)S(1)} %bitcast.65), channel_id=1, source_target_pairs={{0,1},{1,0},{2,3},{3,2},{4,5},{5,4},{6,7},{7,6},{8,9},{9,8},{10,11... | collective-permute-start | bytes 3145736 | tf_op jit(solution)/shard_map/ppermute | solution.py:344
  404.9 39.9 %collective-permute-start.5 = (bf16[256,2048]{1,0:T(8,128)(2,1)S(1)}, bf16[256,2048]{1,0:T(8,128)(2,1)S(1)}, u32[]{:S(2)}, u32[]{:S(2)}) collective-permute-start(bf16[256,2048]{1,0:T(8,128)(2,1)S(1)} %bitcast.68), channel_id=1, source_target_pairs={{0,1},{1,0},{2,3},{3,2},{4,5},{5,4},{6,7},{7,6},{8,9},{9,8},{10,11... | collective-permute-start | bytes 3145736 | tf_op jit(solution)/shard_map/ppermute | solution.py:341
  454.2 4.1 collective-permute-start.7
  476.9 23.5 %collective-permute-start.8 = (bf16[256,2048]{1,0:T(8,128)(2,1)S(1)}, bf16[256,2048]{1,0:T(8,128)(2,1)S(1)}, u32[]{:S(2)}, u32[]{:S(2)}) collective-permute-start(bf16[256,2048]{1,0:T(8,128)(2,1)S(1)} %get-tuple-element.45), channel_id=1, source_target_pairs={{0,1},{1,0},{2,3},{3,2},{4,5},{5,4},{6,7},{7,6},{8,9},{9,8},{10,11... | collective-permute-start | bytes 3145736 | tf_op jit(solution)/shard_map/ppermute | solution.py:352
  478.0 53.5 %collective-permute-start.9 = (bf16[256,2048]{1,0:T(8,128)(2,1)}, bf16[256,2048]{1,0:T(8,128)(2,1)}, u32[]{:S(2)}, u32[]{:S(2)}) collective-permute-start(bf16[256,2048]{1,0:T(8,128)(2,1)} %get-tuple-element.47), channel_id=1, source_target_pairs={{0,1},{1,0},{2,3},{3,2},{4,5},{5,4},{6,7},{7,6},{8,9},{9,8},{10,11... | collective-permute-start | bytes 3145736 | tf_op jit(solution)/shard_map/ppermute | solution.py:352
  501.8 36.0 %all-to-all-start.3 = ((bf16[32,8,2048]{2,1,0:T(8,128)(2,1)}), bf16[32,8,2048]{2,1,0:T(8,128)(2,1)}, u32[]{:S(2)}, u32[]{:S(2)}) async-start(bf16[32,8,2048]{2,1,0:T(8,128)(2,1)} %fusion.12), calls=%async_computation.3 | async-start | bytes 2097152 | tf_op jit(solution)/shard_map/all_to_all | solution.py:36
  537.8 20.1 %all-to-all-start.4 = ((bf16[32,8,2048]{2,1,0:T(8,128)(2,1)}), bf16[32,8,2048]{2,1,0:T(8,128)(2,1)}, u32[]{:S(2)}, u32[]{:S(2)}) async-start(bf16[32,8,2048]{2,1,0:T(8,128)(2,1)} %fusion.13), calls=%async_computation.4 | async-start | bytes 2097152 | tf_op jit(solution)/shard_map/all_to_all | solution.py:36
  560.0 6.0 collective-permute-start.11
  565.4 72.9 %collective-permute-start.10 = (bf16[256,2048]{1,0:T(8,128)(2,1)}, bf16[256,2048]{1,0:T(8,128)(2,1)}, u32[]{:S(2)}, u32[]{:S(2)}) collective-permute-start(bf16[256,2048]{1,0:T(8,128)(2,1)} %bitcast.17), channel_id=1, source_target_pairs={{0,8},{8,0},{1,9},{9,1},{2,10},{10,2},{3,11},{11,3},{4,12},{12,4},... | collective-permute-start | bytes 3145736 | tf_op jit(solution)/shard_map/ppermute | solution.py:364
  570.0 45.1 %all-to-all-start.6 = ((f32[128,8,128]{2,1,0:T(8,128)}), f32[128,8,128]{2,1,0:T(8,128)}, u32[]{:S(2)}, u32[]{:S(2)}) async-start(f32[128,8,128]{2,1,0:T(8,128)} %reshape.175), calls=%async_computation.6 | async-start | bytes 1048576 | tf_op jit(solution)/shard_map/all_to_all | solution.py:36
  588.9 111.1 %collective-permute-start.12 = (bf16[256,4096]{1,0:T(8,128)(2,1)}, bf16[256,4096]{1,0:T(8,128)(2,1)}, u32[]{:S(2)}, u32[]{:S(2)}) collective-permute-start(bf16[256,4096]{1,0:T(8,128)(2,1)} %get-tuple-element.49), channel_id=1, source_target_pairs={{0,0},{8,2},{2,4},{10,6},{4,8},{12,10},{6,12},{14,14},{1,1},{9,3},... | collective-permute-start | bytes 6291464 | tf_op jit(solution)/shard_map/ppermute | solution.py:360
  592.7 107.3 %collective-permute-start.13 = (bf16[256,4096]{1,0:T(8,128)(2,1)}, bf16[256,4096]{1,0:T(8,128)(2,1)}, u32[]{:S(2)}, u32[]{:S(2)}) collective-permute-start(bf16[256,4096]{1,0:T(8,128)(2,1)} %get-tuple-element.50), channel_id=1, source_target_pairs={{8,0},{2,2},{10,4},{0,6},{12,8},{6,10},{14,12},{4,14},{9,1},{3,3},... | collective-permute-start | bytes 6291464 | tf_op jit(solution)/shard_map/ppermute | solution.py:360
  609.2 90.8 %collective-permute-start.14 = (bf16[256,4096]{1,0:T(8,128)(2,1)}, bf16[256,4096]{1,0:T(8,128)(2,1)}, u32[]{:S(2)}, u32[]{:S(2)}) collective-permute-start(bf16[256,4096]{1,0:T(8,128)(2,1)} %get-tuple-element.51), channel_id=1, source_target_pairs={{2,0},{10,2},{0,4},{8,6},{6,8},{14,10},{4,12},{12,14},{3,1},{11,3}... | collective-permute-start | bytes 6291464 | tf_op jit(solution)/shard_map/ppermute | solution.py:360
  609.3 90.7 %collective-permute-start.15 = (bf16[256,4096]{1,0:T(8,128)(2,1)}, bf16[256,4096]{1,0:T(8,128)(2,1)}, u32[]{:S(2)}, u32[]{:S(2)}) collective-permute-start(bf16[256,4096]{1,0:T(8,128)(2,1)} %get-tuple-element.52), channel_id=1, source_target_pairs={{10,0},{0,2},{8,4},{2,6},{14,8},{4,10},{12,12},{6,14},{11,1},{1,3}... | collective-permute-start | bytes 6291464 | tf_op jit(solution)/shard_map/ppermute | solution.py:360
  617.1 74.5 %all-to-all-start.7 = ((f32[128,8,128]{2,1,0:T(8,128)}), f32[128,8,128]{2,1,0:T(8,128)S(1)}, u32[]{:S(2)}, u32[]{:S(2)}) async-start(f32[128,8,128]{2,1,0:T(8,128)} %broadcast_in_dim.5), calls=%async_computation.7 | async-start | bytes 1048576 | tf_op jit(solution)/shard_map/all_to_all | solution.py:36
  691.7 24.8 %all-to-all-start.5 = ((bf16[16,16,2048]{2,1,0:T(8,128)(2,1)}), bf16[16,16,2048]{2,1,0:T(8,128)(2,1)S(1)}, u32[]{:S(2)}, u32[]{:S(2)}) async-start(bf16[16,16,2048]{2,1,0:T(8,128)(2,1)} %bitcast.20), calls=%async_computation.5 | async-start | bytes 2097152 | tf_op jit(solution)/shard_map/all_to_all | solution.py:36
  (11 other events, 360.8 us)

commit v3 on v1

v3 whole, which is shorter than its diff:
```python
import functools

import jax
import jax.numpy as jnp
from jax import lax
from jax.experimental import pallas as pl
from jax.experimental.pallas import tpu as pltpu
from jax.sharding import Mesh
from jax.sharding import PartitionSpec as P

soft_cap = 15.0
f32 = jnp.float32
bf16 = jnp.bfloat16

axes = ("yh", "x", "core", "z", "b")
sizes = (2, 4, 2, 4, 2)
owners = ("yh", "x", "core")
near = ("yh", "x", "b")
column = ("core", "z")
swap = [(0, 1), (1, 0)]
NN = ((1,), (0,))
NT = ((1,), (1,))
TN = ((0,), (0,))

any_spec = pl.BlockSpec(memory_space=pl.ANY)
vmem_spec = pl.BlockSpec(memory_space=pltpu.VMEM)
smem_spec = pl.BlockSpec(memory_space=pltpu.SMEM)
roomy = pltpu.CompilerParams(vmem_limit_bytes=48 * 1024 * 1024)


def mm(left, right, contract=NN):
    return lax.dot_general(left, right, (contract, ((), ())), preferred_element_type=f32)


def exchange(array, names):
    return lax.all_to_all(array, names, split_axis=0, concat_axis=0, tiled=True)


def split_high_low(value):
    high = lax.reduce_precision(value, 8, 7)
    return high.astype(bf16), (value - high).astype(bf16)


def piece_of(step, z):
    return ((z + 1 + step // 2) % 2) * 2 + (step + z // 2) % 2


def weight_round(step):
    pairs = []
    for s in range(2):
        for z in range(4):
            q = piece_of(step, z)
            pairs.append((s * 4 + z, (q % 2) * 4 + 2 * s + q // 2))
    return [(a, b) for a, b in pairs if a != b]


def own_step(core, z):
    table = [-1] * 8
    for step in range(4):
        sending = [a for a, _ in weight_round(step)]
        for at in range(8):
            if at not in sending:
                table[at] = step
    return jnp.array(table, jnp.int32)[core * 4 + z]


def back_round(step):
    return [(b, a) for a, b in weight_round(step)]


def piece_copies(piece, w_in, w_out, packed):
    expert = piece // 2
    if piece % 2 == 1:
        return [(w_out.at[expert], packed)]
    return [
        (w_in.at[expert, pl.ds(256 * a, 256), :], packed.at[:, pl.ds(256 * a, 256)])
        for a in range(16)
    ]


def sort_body(
    at_ref, place_ref, tokens, cotangent, w_in, w_out, sent, p0, p1, p2, p3, held, taken, put
):
    packed = (p0, p1, p2, p3)
    for step in range(4):
        for piece in range(4):
            @pl.when(at_ref[2 + step] == piece)
            def _():
                for source, target in piece_copies(piece, w_in, w_out, held.at[step]):
                    pltpu.make_async_copy(source, target, taken.at[step]).start()
    rows = tokens.shape[0]
    hot = (lax.broadcasted_iota(jnp.int32, (rows, rows), 0) == place_ref[...]).astype(bf16)
    for start in range(0, tokens.shape[1], 512):
        here = pl.ds(start, 512)
        sent[:, 0, :, here] = mm(hot, tokens[:, here]).astype(bf16).reshape(8, 16, 512)
        sent[:, 1, :, here] = mm(hot, cotangent[:, here]).astype(bf16).reshape(8, 16, 512)
    for step in range(4):
        pltpu.make_async_copy(w_out.at[0], held.at[step], taken.at[step]).wait()
        pltpu.make_async_copy(held.at[step], packed[step], put.at[step]).start()
    for step in range(4):
        pltpu.make_async_copy(held.at[step], packed[step], put.at[step]).wait()


def sort_and_pack(at, place, tokens, cotangent, w_in, w_out):
    shape = jax.ShapeDtypeStruct((256, 4096), bf16)
    return pl.pallas_call(
        sort_body,
        out_shape=(jax.ShapeDtypeStruct((8, 2, 16, 4096), bf16),) + (shape,) * 4,
        in_specs=[smem_spec] + [vmem_spec] * 3 + [any_spec] * 2,
        out_specs=(vmem_spec,) + (any_spec,) * 4,
        scratch_shapes=[
            pltpu.VMEM((4, 256, 4096), bf16),
            pltpu.SemaphoreType.DMA((4,)),
            pltpu.SemaphoreType.DMA((4,)),
        ],
        compiler_params=roomy,
        cost_estimate=pl.CostEstimate(flops=0, bytes_accessed=20 << 20, transcendentals=0),
    )(at, place, tokens, cotangent, w_in, w_out)


def unpack_body(
    at_ref, p0, p1, p2, p3, q0, q1, q2, q3, w_in, w_out, held, taken, put
):
    come, made = (p0, p1, p2, p3), (q0, q1, q2, q3)
    for step in range(4):
        @pl.when(at_ref[1] == step)
        def _():
            pltpu.make_async_copy(made[step], held.at[step], taken.at[step]).start()

        @pl.when(at_ref[1] != step)
        def _():
            pltpu.make_async_copy(come[step], held.at[step], taken.at[step]).start()
    for step in range(4):
        pltpu.make_async_copy(come[step], held.at[step], taken.at[step]).wait()
        for piece in range(4):
            @pl.when(at_ref[2 + step] == piece)
            def _():
                for target, source in piece_copies(piece, w_in, w_out, held.at[step]):
                    pltpu.make_async_copy(source, target, put.at[step]).start()
    for step in range(4):
        pltpu.make_async_copy(held.at[step], w_out.at[0], put.at[step]).wait()


def unpack(at, come, made):
    return pl.pallas_call(
        unpack_body,
        out_shape=(
            jax.ShapeDtypeStruct((2, 4096, 256), bf16),
            jax.ShapeDtypeStruct((2, 256, 4096), bf16),
        ),
        in_specs=[smem_spec] + [any_spec] * 8,
        out_specs=(any_spec, any_spec),
        scratch_shapes=[
            pltpu.VMEM((4, 256, 4096), bf16),
            pltpu.SemaphoreType.DMA((4,)),
            pltpu.SemaphoreType.DMA((4,)),
        ],
        compiler_params=roomy,
        cost_estimate=pl.CostEstimate(flops=0, bytes_accessed=16 << 20, transcendentals=0),
    )(at, *come, *made)


def load_weights(at_ref, weights, packed, tall, wide, sems):
    def load_tall(slot, array):
        for a in range(16):
            block = pl.ds(256 * a, 256)
            target = tall.at[block, pl.ds(256 * slot, 256)]
            pltpu.make_async_copy(array.at[:, block], target, sems.at[slot]).start()

    def load_wide(slot, array):
        target = wide.at[pl.ds(256 * slot, 256), :]
        pltpu.make_async_copy(array, target, sems.at[slot]).start()

    core, own = at_ref[0], at_ref[1]
    for slot in range(4):
        for here, step, load in ((0, slot, load_tall), (1, slot ^ 1, load_wide)):
            @pl.when((core == here) & (own == step))
            def _():
                load(slot, packed[step])

            @pl.when((core == here) & (own != step))
            def _():
                load(slot, weights[step])


def wait_weights(slot, weights, wide, sems):
    pltpu.make_async_copy(weights[0], wide.at[pl.ds(256 * slot, 256), :], sems.at[slot]).wait()


def up_body(
    at_ref, rows_in, w0, w1, w2, w3, p0, p1, p2, p3,
    pre_ref, send_ref, rows, tall, wide, row_sem, sems,
):
    core = at_ref[0]
    weights = (w0, w1, w2, w3)
    pltpu.make_async_copy(rows_in, rows, row_sem).start()
    load_weights(at_ref, weights, (p0, p1, p2, p3), tall, wide, sems)
    pltpu.make_async_copy(rows_in, rows, row_sem).wait()

    @pl.when(core == 0)
    def _():
        for slot in range(4):
            wait_weights(slot, weights, wide, sems)
            here = slice(256 * slot, 256 * slot + 256)
            pre_act = mm(rows[...], tall[:, here])
            pre_ref[:, here] = pre_act
            send_ref[:, here] = (pre_act * jax.nn.sigmoid(pre_act)).astype(bf16)

    @pl.when(core == 1)
    def _():
        for slot in range(4):
            wait_weights(slot, weights, wide, sems)
            here = slice(256 * slot, 256 * slot + 256)
            send_ref[:, here] = mm(rows[...], wide[here, :], NT).astype(bf16)


def up(at, rows, weights, packed):
    return pl.pallas_call(
        up_body,
        out_shape=(
            jax.ShapeDtypeStruct((512, 1024), f32),
            jax.ShapeDtypeStruct((512, 1024), bf16),
        ),
        in_specs=[smem_spec] + [any_spec] * 9,
        out_specs=(vmem_spec, vmem_spec),
        scratch_shapes=[
            pltpu.VMEM((512, 4096), bf16),
            pltpu.VMEM((4096, 1024), bf16),
            pltpu.VMEM((1024, 4096), bf16),
            pltpu.SemaphoreType.DMA,
            pltpu.SemaphoreType.DMA((4,)),
        ],
        compiler_params=roomy,
        cost_estimate=pl.CostEstimate(
            flops=2 * 512 * 4096 * 1024, bytes_accessed=15 << 20, transcendentals=512 * 1024
        ),
    )(at, rows, *weights, *packed)


def down_body(
    at_ref, pre_ref, got_ref, w0, w1, w2, w3, p0, p1, p2, p3,
    part_ref, q_ref, tall, wide, sems,
):
    core = at_ref[0]
    weights = (w0, w1, w2, w3)
    load_weights(at_ref, weights, (p0, p1, p2, p3), tall, wide, sems)

    @pl.when(core == 0)
    def _():
        for slot in range(4):
            here = slice(256 * slot, 256 * slot + 256)
            pre_act = pre_ref[:, here]
            sigma_pre = jax.nn.sigmoid(pre_act)
            slope = got_ref[:, here].astype(f32) * sigma_pre * (1.0 + pre_act * (1.0 - sigma_pre))
            q_ref[:, here] = slope.astype(bf16)

    @pl.when(core == 1)
    def _():
        q_ref[...] = got_ref[...]

    for slot in range(4):
        wait_weights(slot, weights, wide, sems)

    @pl.when(core == 0)
    def _():
        for index in range(8):
            here = slice(512 * index, 512 * index + 512)
            part_ref[:, here] = mm(q_ref[...], tall[here, :], NT).astype(bf16)

    @pl.when(core == 1)
    def _():
        for index in range(8):
            here = slice(512 * index, 512 * index + 512)
            part_ref[:, here] = mm(q_ref[...], wide[:, here]).astype(bf16)


def down(at, pre_act, got, weights, packed):
    return pl.pallas_call(
        down_body,
        out_shape=(
            jax.ShapeDtypeStruct((512, 4096), bf16),
            jax.ShapeDtypeStruct((512, 1024), bf16),
        ),
        in_specs=[smem_spec] + [vmem_spec] * 2 + [any_spec] * 8,
        out_specs=(vmem_spec,) * 2,
        scratch_shapes=[
            pltpu.VMEM((4096, 1024), bf16),
            pltpu.VMEM((1024, 4096), bf16),
            pltpu.SemaphoreType.DMA((4,)),
        ],
        compiler_params=roomy,
        cost_estimate=pl.CostEstimate(
            flops=2 * 512 * 4096 * 1024, bytes_accessed=16 << 20, transcendentals=512 * 1024
        ),
    )(at, pre_act, got, *weights, *packed)


def grads_body(at_ref, rows, q_ref, g0, g1, g2, g3, tall, wide, sems):
    core = at_ref[0]
    grads = (g0, g1, g2, g3)

    @pl.when(core == 0)
    def _():
        for slot in range(4):
            here = slice(256 * slot, 256 * slot + 256)
            tall[:, here] = mm(rows[...], q_ref[:, here], TN).astype(bf16)
            for a in range(16):
                block = pl.ds(256 * a, 256)
                source = tall.at[block, pl.ds(256 * slot, 256)]
                pltpu.make_async_copy(source, grads[slot].at[:, block], sems.at[slot]).start()

    @pl.when(core == 1)
    def _():
        for slot in range(4):
            here = slice(256 * slot, 256 * slot + 256)
            wide[here, :] = mm(q_ref[:, here], rows[...], TN).astype(bf16)
            source = wide.at[pl.ds(256 * slot, 256), :]
            pltpu.make_async_copy(source, grads[slot ^ 1], sems.at[slot]).start()

    for slot in range(4):
        pltpu.make_async_copy(wide.at[pl.ds(0, 256), :], grads[0], sems.at[slot]).wait()


def weight_grads(at, rows, units):
    shape = jax.ShapeDtypeStruct((256, 4096), bf16)
    return pl.pallas_call(
        grads_body,
        out_shape=(shape,) * 4,
        in_specs=[smem_spec] + [vmem_spec] * 2,
        out_specs=(any_spec,) * 4,
        scratch_shapes=[
            pltpu.VMEM((4096, 1024), bf16),
            pltpu.VMEM((1024, 4096), bf16),
            pltpu.SemaphoreType.DMA((4,)),
        ],
        compiler_params=roomy,
        cost_estimate=pl.CostEstimate(
            flops=2 * 512 * 4096 * 1024, bytes_accessed=13 << 20, transcendentals=0
        ),
    )(at, rows, units)


def shards(tokens, cotangent, group_of, mixer, w_in, w_out):
    seqs, positions, width = tokens.shape
    rows = seqs * positions
    core = lax.axis_index("core")
    first = core == 0
    half = width // 2
    plane = lax.axis_index("z")
    at = jnp.stack(
        [core, own_step(core, plane)] + [piece_of(step, plane) for step in range(4)]
    ).astype(jnp.int32)
    tie = lax.optimization_barrier

    home = group_of % 16
    earlier = jnp.arange(seqs)[:, None] > jnp.arange(seqs)[None, :]
    same = (home[:, None, :] == home[None, :, :]) & earlier[:, :, None]
    member = jnp.sum(same.astype(jnp.int32), axis=1)
    place = home * 8 + jnp.arange(positions, dtype=jnp.int32)[None, :] * 2 + member
    place = place.reshape(1, rows)
    sent, *packed = sort_and_pack(
        at, place, tokens.reshape(rows, width), cotangent.reshape(rows, width), w_in, w_out
    )
    hot = (place == jnp.arange(rows, dtype=jnp.int32)[:, None]).astype(bf16)
    held = exchange(sent.reshape(16, 16, width), owners).reshape(256, width)

    def send_weights(step, piece):
        return lax.ppermute(piece, column, weight_round(step))

    weights = [send_weights(0, packed[0]), send_weights(1, packed[1])]

    planes = [(plane + d) % 4 for d in range(4)]
    mixer_e = mixer.T.reshape(8, 4, width)
    mixer_t = jnp.concatenate(
        [lax.dynamic_index_in_dim(mixer_e, p, 1, keepdims=False) for p in planes], axis=0
    )
    logits = mm(mixer_t, held, NT)
    logits = jnp.where(first, logits, lax.ppermute(logits, "core", swap))
    scaled = jnp.tanh(logits / soft_cap)
    exponent = jnp.exp(soft_cap * scaled)
    column_of = jnp.arange(256, dtype=jnp.int32) // 2 % 8
    mask = (column_of[None, :] == jnp.arange(8, dtype=jnp.int32)[:, None]).astype(f32)
    spread = exponent[:, None, :] * mask[None]
    spread = spread / jnp.sum(spread, axis=2, keepdims=True)
    spread_high, spread_low = split_high_low(spread)
    flat_high, flat_low = spread_high.reshape(256, 256), spread_low.reshape(256, 256)

    def shift(by):
        return [(s, (s + by) % 4) for s in range(4)]

    mix = (mm(flat_high, held) + mm(flat_low, held)).astype(bf16)
    blocks = {}
    for d in (2, 1, 3, 0):
        block = mix[64 * d : 64 * d + 64]
        blocks[d] = lax.ppermute(block, "z", shift(d)) if d else block
    blocks[2], weights[0], weights[1], *later = tie(
        (blocks[2], weights[0], weights[1], *packed[2:])
    )
    weights += [send_weights(step + 2, piece) for step, piece in enumerate(later)]
    sent = jnp.stack([blocks[d].reshape(8, 8, width) for d in range(4)], axis=1)
    sent = jnp.broadcast_to(sent[:, None], (8, 2, 4, 8, width)).reshape(16, 32, width)
    expert_rows = exchange(sent, near).reshape(512, width)

    pre_act, given = up(at, expert_rows, weights, packed)
    got = lax.ppermute(given, "core", swap)
    part, units = down(at, pre_act, got, weights, packed)
    made = weight_grads(at, expert_rows, units)
    back = exchange(part.reshape(16, 32, width), near)

    def send_grads(step, piece):
        return lax.ppermute(piece, column, back_round(step))

    grads = [send_grads(step, made[step]) for step in range(2)]
    back, grads[0], grads[1] = tie((back, grads[0], grads[1]))
    back = jnp.sum(back.reshape(8, 2, 4, 8, width).astype(f32), axis=1).astype(bf16)
    blocks = {}
    for d in (2, 1, 3, 0):
        block = back[:, d].reshape(64, width)
        blocks[d] = lax.ppermute(block, "z", shift(-d)) if d else block
    blocks[2], *later = tie((blocks[2], *made[2:]))
    grads += [send_grads(step + 2, piece) for step, piece in enumerate(later)]
    dots, halves = [], []
    for d in range(4):
        block = blocks[d]
        dots.append(jnp.sum(mm(block, held, NT).reshape(8, 8, 256) * mask[None], axis=1))
        come = lax.ppermute(block[:, :half], "core", swap)
        halves.append(jnp.where(first, block[:, half:], come))
    dots = jnp.concatenate(dots, axis=0)
    back_half = jnp.concatenate(halves, axis=0)
    d_weights = dots + lax.ppermute(dots, "core", swap)
    mixing = jnp.sum(spread, axis=1)
    column_sum = jnp.sum((mixing * d_weights)[:, None, :] * mask[None], axis=2, keepdims=True)
    column_sum = jnp.sum(column_sum * mask[None], axis=1)
    d_logits = mixing * (d_weights - column_sum) * (1.0 - scaled * scaled)
    d_high, d_low = split_high_low(d_logits)

    mixer_half = jnp.where(first, mixer_t[:, half:], mixer_t[:, :half])
    grad_rows = (
        mm(flat_high, back_half, TN)
        + mm(flat_low, back_half, TN)
        + mm(d_high, mixer_half, TN)
        + mm(d_low, mixer_half, TN)
    )
    grad_rows = exchange(grad_rows.astype(bf16).reshape(16, 16, half), owners)

    here_yh, here_x = lax.axis_index("yh"), lax.axis_index("x")
    steps = jnp.arange(32, dtype=jnp.int32)
    far_x, far_yh, far_z = steps // 8, steps // 4 % 2, steps % 4
    at_x, at_yh = (here_x + far_x) % 4, (here_yh + far_yh) % 2
    take = far_z * 8 + at_yh * 4 + at_x
    turn = (take[:, None] == steps[None, :]).astype(bf16)
    part = mm(mm(turn, d_high).astype(bf16), held) + mm(mm(turn, d_low).astype(bf16), held)
    come = lax.ppermute(part[:, half:], "core", [(0, 1)])
    part = jnp.where(first, part[:, :half], come)
    low_b = lax.axis_index("b") == 0
    left, right = part[:, : half // 2], part[:, half // 2 :]
    part = jnp.where(low_b, left, right)
    part += lax.ppermute(jnp.where(low_b, right, left), "b", swap)
    part = part.reshape(4, 2, 4, half // 2)
    part = sum(
        [lax.ppermute(part[d], "x", shift(d)) for d in range(1, 4)], start=part[0]
    )
    part = part[0] + lax.ppermute(part[1], "yh", swap)
    part, grad_rows, grads[2], grads[3] = tie((part, grad_rows, grads[2], grads[3]))
    part = sum(
        [lax.ppermute(part[d : d + 1], "z", shift(d)) for d in range(1, 4)], start=part[:1]
    )
    part = jnp.concatenate(
        [part] + [lax.ppermute(part, "z", shift(-d)) for d in range(1, 4)], axis=0
    )
    part = jnp.stack([part, lax.ppermute(part, "yh", swap)], axis=0)
    part = jnp.stack([part] + [lax.ppermute(part, "x", shift(-d)) for d in range(1, 4)], axis=0)
    part = part.reshape(32, half // 2)
    come = lax.ppermute(part, "b", swap)
    part = jnp.concatenate([jnp.where(low_b, part, come), jnp.where(low_b, come, part)], axis=1)
    come = lax.ppermute(part, "core", swap)
    part = jnp.concatenate([jnp.where(first, part, come), jnp.where(first, come, part)], axis=1)
    expert_at = (at_yh * 4 + at_x) * 4 + (plane + far_z) % 4
    turn = (expert_at[:, None] == steps[None, :]).astype(f32)
    grad_mixer = lax.dot_general(
        part, turn, (TN, ((), ())), precision=lax.Precision.HIGHEST, preferred_element_type=f32
    )

    grad_in, grad_out = unpack(at, grads, made)
    grad_rows = grad_rows.reshape(8, 2, 16, half)
    grad_tokens = jnp.concatenate(
        [mm(hot, grad_rows[:, 1 - side].reshape(rows, half), TN).astype(bf16) for side in range(2)],
        axis=1,
    ).reshape(seqs, positions, width)
    return (grad_tokens, grad_mixer, grad_in, grad_out)


def solution(mesh):
    fine = Mesh(mesh.devices.reshape(sizes), axes)
    dp, expert = ("yh", "x", "core"), ("z", "b")
    every = dp + expert
    return jax.shard_map(
        shards,
        mesh=fine,
        in_specs=(
            P(every, None, None),
            P(every, None, None),
            P(every, None),
            P(),
            P(dp, None, expert),
            P(dp, expert, None),
        ),
        out_specs=(
            P(every, None, None),
            P(),
            P(dp, None, expert),
            P(dp, expert, None),
        ),
        check_vma=False,
    )
```

time: 439 us -> 409 us (0.932)
  waiting for transfers between devices: 268 us -> 189 us
  Pallas kernels: 0 us -> 47.5 us
  starting transfers between devices: 75.4 us -> 95 us
  other arithmetic: 35.5 us -> 16.2 us
  matrix products: 39 us -> 28.9 us
  local copies, waits for them, and re-layouts: 15.7 us -> 22.7 us
    all_to_all x6 -> x4, waiting for transfers between devices: 117 us -> 32.6 us  [exchange(): return lax.all_to_all(array, names, split_axis=0, concat_axis=0, tiled=True)]
    pallas_call x0 -> x5, Pallas kernels: none -> 47.5 us  [the longest x1 12.8 us: up(): pl.pallas_call(up_body, out_shape=(jax.ShapeDtypeStruct((512, 1024), f32)...]
    ppermute x12 -> x38, starting transfers between devices: 25.7 us -> 67 us  [the longest x4 10.9 us: send_grads(): return lax.ppermute(piece, column, back_round(step))]
    all_to_all x6 -> x4, starting transfers between devices: 47.4 us -> 26.7 us  [exchange(): return lax.all_to_all(array, names, split_axis=0, concat_axis=0, tiled=True)]
    another operation x4, other arithmetic: 15.5 us -> 0.33 us  [the longest x1 0.26 us: shards(): sent = jnp.stack([blocks[d].reshape(8, 8, width) for d in range(4)], axis=1)]
    dot_general x22 -> x15, matrix products: 39 us -> 27.6 us  [mm(): lax.dot_general(left, right, (contract, ((), ())), preferred_element_type...]
    reshape x1 -> x0, other arithmetic: 6.59 us -> none  [shards(): back = exchange(part.reshape(64, 8, width), same_core).reshape(512, width)]
    ppermute x12 -> x38, waiting for transfers between devices: 151 us -> 156 us  [the longest x4 65.3 us: send_weights(): return lax.ppermute(piece, column, weight_round(step))]
  transfers between devices with their start and end apart: 19 -> 43, of which waited for: 13 -> 25; matrix products, arithmetic and copies ran while one was open for 13% -> 10% of each run, Pallas kernels for 0% -> 4%
where the time goes in v3:
time: 409 us; the launch traced here: 401 us
  waiting for transfers between devices  189 us (46%)
  starting transfers between devices  95 us (23%)
  Pallas kernels  47.5 us (12%)
  matrix products  28.9 us (7%)
  local copies, waits for them, and re-layouts  22.7 us (6%)
  other arithmetic  16.2 us (4%)
    ppermute x4, waiting for transfers between devices, send_weights(): return lax.ppermute(piece, column, weight_round(step))  65.3 us
    ppermute x4, waiting for transfers between devices, send_grads(): return lax.ppermute(piece, column, back_round(step))  45.7 us
    all_to_all x4, waiting for transfers between devices, exchange(): return lax.all_to_all(array, names, split_axis=0, concat_axis=0, tiled=True)  32.6 us
    dot_general x15, matrix products, mm(): lax.dot_general(left, right, (contract, ((), ())), preferred_element_type...  27.6 us
    all_to_all x4, starting transfers between devices, exchange(): return lax.all_to_all(array, names, split_axis=0, concat_axis=0, tiled=True)  26.7 us
    pallas_call x1, Pallas kernels, up(): pl.pallas_call(up_body, out_shape=(jax.ShapeDtypeStruct((512, 1024), f32)...  12.8 us
    ppermute x3, waiting for transfers between devices, shards(): blocks[d] = lax.ppermute(block, 'z', shift(-d)) if d else block  12.6 us
    pallas_call x1, Pallas kernels, down(): pl.pallas_call(down_body, out_shape=(jax.ShapeDtypeStruct((512, 4096), bf...  11.1 us
  transfers between devices with their start and end apart: 43, of which 25 were waited for; matrix products, arithmetic and copies ran while one was open for 10% of the time, Pallas kernels for 4%

profile of v3, /device:TPU:1, one launch (start us, length us, event | category | flops | bytes accessed | tf_op | source)
XLA Modules:
  0.0 401.2 jit_solution(7308140351431916383)
XLA Ops:
  6.4 8.4 %shard_map.102 = (bf16[8,2,16,4096]{3,2,1,0:T(8,128)(2,1)S(1)}, bf16[256,4096]{1,0:T(8,128)(2,1)}, bf16[256,4096]{1,0:T(8,128)(2,1)}, bf16[256,4096]{1,0:T(8,128)(2,1)}, bf16[256,4096]{1,0:T(8,128)(2,1)}) custom-call(s32[6]{0:T(128)S(1)} %stack.50.at_ref, s32[1,128]{1,0:T(1,128)S(1)} %reshape.298.place_ref, bf16[128,4096]{1,0:T(8,128)(2,1)S(1)} %reshape.299.tokens, ...), custom_call_target="tpu_custom_call" | custom-call | bytes 20971520 | tf_op jit(solution)/shard_map/pallas_call | solution.py:106
  16.1 8.6 %all-to-all-start = ((bf16[16,16,4096]{2,1,0:T(8,128)(2,1)}), bf16[16,16,4096]{2,1,0:T(8,128)(2,1)}, u32[]{:S(2)}, u32[]{:S(2)}) async-start(bf16[16,16,4096]{2,1,0:T(8,128)(2,1)} %bitcast.100), calls=%async_computation | async-start | bytes 4194304 | tf_op jit(solution)/shard_map/all_to_all | solution.py:36
  29.2 24.2 %all-to-all-done = bf16[16,16,4096]{2,1,0:T(8,128)(2,1)} async-done(((bf16[16,16,4096]{2,1,0:T(8,128)(2,1)}), bf16[16,16,4096]{2,1,0:T(8,128)(2,1)}, u32[]{:S(2)}, u32[]{:S(2)}) %all-to-all-start) | async-done | bytes 2097184 | tf_op jit(solution)/shard_map/all_to_all | solution.py:36
  69.0 20.6 %collective-permute-done.4.w1 = bf16[256,4096]{1,0:T(8,128)(2,1)} collective-permute-done((bf16[256,4096]{1,0:T(8,128)(2,1)}, bf16[256,4096]{1,0:T(8,128)(2,1)}, u32[]{:S(2)}, u32[]{:S(2)}) %collective-permute-start.4) | collective-permute-done | bytes 2097184 | tf_op jit(solution)/shard_map/ppermute | solution.py:368
  92.2 4.0 collective-permute-done.5
  99.4 6.9 %all-to-all-start.1 = ((bf16[16,32,4096]{2,1,0:T(8,128)(2,1)}), bf16[16,32,4096]{2,1,0:T(8,128)(2,1)}, u32[]{:S(2)}, u32[]{:S(2)}) async-start(bf16[16,32,4096]{2,1,0:T(8,128)(2,1)} %bitcast.101), calls=%async_computation.1 | async-start | bytes 8388608 | tf_op jit(solution)/shard_map/all_to_all | solution.py:36
  110.0 25.7 %collective-permute-done.6.w2 = bf16[256,4096]{1,0:T(8,128)(2,1)} collective-permute-done((bf16[256,4096]{1,0:T(8,128)(2,1)}, bf16[256,4096]{1,0:T(8,128)(2,1)}, u32[]{:S(2)}, u32[]{:S(2)}) %collective-permute-start.6) | collective-permute-done | bytes 2097184 | tf_op jit(solution)/shard_map/ppermute | solution.py:368
  135.7 19.0 %collective-permute-done.7.w3 = bf16[256,4096]{1,0:T(8,128)(2,1)} collective-permute-done((bf16[256,4096]{1,0:T(8,128)(2,1)}, bf16[256,4096]{1,0:T(8,128)(2,1)}, u32[]{:S(2)}, u32[]{:S(2)}) %collective-permute-start.7) | collective-permute-done | bytes 2097184 | tf_op jit(solution)/shard_map/ppermute | solution.py:368
  154.7 8.4 %all-to-all-done.1 = bf16[16,32,4096]{2,1,0:T(8,128)(2,1)} async-done(((bf16[16,32,4096]{2,1,0:T(8,128)(2,1)}), bf16[16,32,4096]{2,1,0:T(8,128)(2,1)}, u32[]{:S(2)}, u32[]{:S(2)}) %all-to-all-start.1) | async-done | bytes 4194336 | tf_op jit(solution)/shard_map/all_to_all | solution.py:36
  163.1 12.8 %shard_map.103 = (f32[512,1024]{1,0:T(8,128)S(1)}, bf16[512,1024]{1,0:T(8,128)(2,1)S(1)}) custom-call(s32[6]{0:T(128)S(1)} %stack.50.at_ref, bf16[512,4096]{1,0:T(8,128)(2,1)} %bitcast.19.rows_in.rows, bf16[256,4096]{1,0:T(8,128)(2,1)S(1)} %collective-permute-done.3.w0, bf16[256,4096]{1,0:T(8,128)(2,1)} %collective-permute-done.4.w1, ...), custom_call_target="tpu_custom_call" | custom-call | flops 4294967296 | bytes 15728640 | tf_op jit(solution)/shard_map/pallas_call | solution.py:218
  179.2 11.1 %shard_map.104 = (bf16[512,4096]{1,0:T(8,128)(2,1)}, bf16[512,1024]{1,0:T(8,128)(2,1)S(1)}) custom-call(s32[6]{0:T(128)S(1)} %stack.50.at_ref, f32[512,1024]{1,0:T(8,128)S(1)} %get-tuple-element.44.pre_ref, bf16[512,1024]{1,0:T(8,128)(2,1)S(1)} %collective-permute-done.8.got_ref, bf16[256,4096]{1,0:T(8,128)(2,1)} %copy-done, ...), custom_call_target="tpu_custom_call" | custom-call | flops 4294967296 | bytes 16777216 | tf_op jit(solution)/shard_map/pallas_call | solution.py:278
  190.3 4.6 %all-to-all-start.2 = ((bf16[16,32,4096]{2,1,0:T(8,128)(2,1)}), bf16[16,32,4096]{2,1,0:T(8,128)(2,1)}, u32[]{:S(2)}, u32[]{:S(2)}) async-start(bf16[16,32,4096]{2,1,0:T(8,128)(2,1)} %bitcast.102), calls=%async_computation.2 | async-start | bytes 8388608 | tf_op jit(solution)/shard_map/all_to_all | solution.py:36
  194.9 9.1 %shard_map.105 = (bf16[256,4096]{1,0:T(8,128)(2,1)S(1)}, bf16[256,4096]{1,0:T(8,128)(2,1)S(1)}, bf16[256,4096]{1,0:T(8,128)(2,1)}, bf16[256,4096]{1,0:T(8,128)(2,1)}) custom-call(s32[6]{0:T(128)S(1)} %stack.50.at_ref, bf16[512,4096]{1,0:T(8,128)(2,1)} %bitcast.19.rows_in.rows, bf16[512,1024]{1,0:T(8,128)(2,1)S(1)} %get-tuple-element.47.q_ref), custom_call_target="tpu_custom_call" | custom-call | flops 4294967296 | bytes 13631488 | tf_op jit(solution)/shard_map/pallas_call | solution.py:326
  206.3 4.1 %collective-permute-start.9 = (bf16[256,4096]{1,0:T(8,128)(2,1)S(1)}, bf16[256,4096]{1,0:T(8,128)(2,1)S(1)}, u32[]{:S(2)}, u32[]{:S(2)}) collective-permute-start(bf16[256,4096]{1,0:T(8,128)(2,1)S(1)} %get-tuple-element.48.q0), channel_id=1, source_target_pairs={{2,0},{0,2},{10,4},{8,6},{6,8},{4,10},{14,12},{12,14},{3,1},{1,3},... | collective-permute-start | bytes 6291464 | tf_op jit(solution)/shard_map/ppermute | solution.py:411
  210.4 38.8 %collective-permute-done.10.p1 = bf16[256,4096]{1,0:T(8,128)(2,1)S(1)} collective-permute-done((bf16[256,4096]{1,0:T(8,128)(2,1)S(1)}, bf16[256,4096]{1,0:T(8,128)(2,1)S(1)}, u32[]{:S(2)}, u32[]{:S(2)}) %collective-permute-start.10) | collective-permute-done | bytes 2097184 | tf_op jit(solution)/shard_map/ppermute | solution.py:411
  250.5 4.4 %collective-permute-done.9.p0 = bf16[256,4096]{1,0:T(8,128)(2,1)S(1)} collective-permute-done((bf16[256,4096]{1,0:T(8,128)(2,1)S(1)}, bf16[256,4096]{1,0:T(8,128)(2,1)S(1)}, u32[]{:S(2)}, u32[]{:S(2)}) %collective-permute-start.9) | collective-permute-done | bytes 2097184 | tf_op jit(solution)/shard_map/ppermute | solution.py:411
  256.2 5.1 %reduce_sum.96 = bf16[8,4,8,4096]{3,2,1,0:T(8,128)(2,1)} reduce(bf16[8,2,4,8,4096]{4,3,2,1,0:T(8,128)(2,1)} %bitcast.21, bf16[]{:T(256)} %constant.217.clone.1), dimensions={1}, to_apply=%region_3.4 | reduce | flops 1048576 | bytes 6291458 | tf_op jit(solution)/shard_map/reduce_sum | solution.py:415
  264.0 3.7 collective-permute-start.12
  280.1 11.3 %collective-permute-done.11 = bf16[64,4096]{1,0:T(8,128)(2,1)S(1)} collective-permute-done((bf16[64,4096]{1,0:T(8,128)(2,1)S(1)}, bf16[64,4096]{1,0:T(8,128)(2,1)S(1)}, u32[]{:S(2)}, u32[]{:S(2)}) %collective-permute-start.11) | collective-permute-done | bytes 524320 | tf_op jit(solution)/shard_map/ppermute | solution.py:419
  302.0 4.5 %collective-permute-start.25 = (bf16[256,4096]{1,0:T(8,128)(2,1)S(1)}, bf16[256,4096]{1,0:T(8,128)(2,1)}, u32[]{:S(2)}, u32[]{:S(2)}) collective-permute-start(bf16[256,4096]{1,0:T(8,128)(2,1)S(1)} %copy-done.8), channel_id=1, source_target_pairs={{8,4},{10,6},{4,8},{6,10},{9,5},{11,7},{5,9},{7,11},{24,20},{26,22... | collective-permute-start | bytes 6291464 | tf_op jit(solution)/shard_map/ppermute | solution.py:411
  324.0 6.7 %all-to-all-start.3 = ((bf16[16,16,2048]{2,1,0:T(8,128)(2,1)}), bf16[16,16,2048]{2,1,0:T(8,128)(2,1)S(1)}, u32[]{:S(2)}, u32[]{:S(2)}) async-start(bf16[16,16,2048]{2,1,0:T(8,128)(2,1)} %bitcast.35), calls=%async_computation.3 | async-start | bytes 2097152 | tf_op jit(solution)/shard_map/all_to_all | solution.py:36
  335.7 9.0 %collective-permute-done.19 = f32[2,4,1024]{2,1,0:T(4,128)S(1)} collective-permute-done((f32[2,4,1024]{2,1,0:T(4,128)S(1)}, f32[2,4,1024]{2,1,0:T(4,128)S(1)}, u32[]{:S(2)}, u32[]{:S(2)}) %collective-permute-start.19) | collective-permute-done | bytes 32800 | tf_op jit(solution)/shard_map/ppermute | solution.py:461
  381.9 7.8 %collective-permute-start.38 = (f32[32,2048]{1,0:T(8,128)}, f32[32,2048]{1,0:T(8,128)}, u32[]{:S(2)}, u32[]{:S(2)}) collective-permute-start(f32[32,2048]{1,0:T(8,128)} %pad_maximum_fusion.4), channel_id=1, source_target_pairs={{0,8},{8,0},{1,9},{9,1},{2,10},{10,2},{3,11},{11,3},{4,12},{12,4},... | collective-permute-start | bytes 786440 | tf_op jit(solution)/shard_map/ppermute | solution.py:476
  392.5 6.0 %shard_map.106 = (bf16[2,4096,256]{2,1,0:T(8,128)(2,1)}, bf16[2,256,4096]{2,1,0:T(8,128)(2,1)}) custom-call(s32[6]{0:T(128)S(1)} %stack.50.at_ref, bf16[256,4096]{1,0:T(8,128)(2,1)S(1)} %copy-done.6, bf16[256,4096]{1,0:T(8,128)(2,1)S(1)} %copy-done.4, bf16[256,4096]{1,0:T(8,128)(2,1)} %collective-permute-done.25.p2, ...), custom_call_target="tpu_custom_call" | custom-call | bytes 16777216 | tf_op jit(solution)/shard_map/pallas_call | solution.py:145
  (204 shorter events, 134.7 us)
Async XLA Ops:
  16.1 37.3 %all-to-all-start = ((bf16[16,16,4096]{2,1,0:T(8,128)(2,1)}), bf16[16,16,4096]{2,1,0:T(8,128)(2,1)}, u32[]{:S(2)}, u32[]{:S(2)}) async-start(bf16[16,16,4096]{2,1,0:T(8,128)(2,1)} %bitcast.100), calls=%async_computation | async-start | bytes 4194304 | tf_op jit(solution)/shard_map/all_to_all | solution.py:36
  24.7 44.3 %collective-permute-start.3 = (bf16[256,4096]{1,0:T(8,128)(2,1)}, bf16[256,4096]{1,0:T(8,128)(2,1)S(1)}, u32[]{:S(2)}, u32[]{:S(2)}) collective-permute-start(bf16[256,4096]{1,0:T(8,128)(2,1)} %get-tuple-element.35.p0), channel_id=1, source_target_pairs={{0,2},{2,0},{4,10},{6,8},{8,6},{10,4},{12,14},{14,12},{1,3},{3,1},... | collective-permute-start | bytes 6291464 | tf_op jit(solution)/shard_map/ppermute | solution.py:368
  28.1 61.5 %collective-permute-start.4 = (bf16[256,4096]{1,0:T(8,128)(2,1)}, bf16[256,4096]{1,0:T(8,128)(2,1)}, u32[]{:S(2)}, u32[]{:S(2)}) collective-permute-start(bf16[256,4096]{1,0:T(8,128)(2,1)} %get-tuple-element.36.p1), channel_id=1, source_target_pairs={{0,10},{2,8},{4,2},{6,0},{8,14},{10,12},{12,6},{14,4},{1,11},{3,9}... | collective-permute-start | bytes 6291464 | tf_op jit(solution)/shard_map/ppermute | solution.py:368
  63.1 29.1 %collective-permute-start.2 = (bf16[64,4096]{1,0:T(8,128)(2,1)S(1)}, bf16[64,4096]{1,0:T(8,128)(2,1)S(1)}, u32[]{:S(2)}, u32[]{:S(2)}) collective-permute-start(bf16[64,4096]{1,0:T(8,128)(2,1)S(1)} %get-tuple-element.70), channel_id=1, source_target_pairs={{0,4},{2,6},{4,0},{6,2},{1,5},{3,7},{5,1},{7,3},{8,12},{10,14},{12... | collective-permute-start | bytes 1572872 | tf_op jit(solution)/shard_map/ppermute | solution.py:395
  66.3 25.9 %collective-permute-start.1 = (bf16[64,4096]{1,0:T(8,128)(2,1)S(1)}, bf16[64,4096]{1,0:T(8,128)(2,1)S(1)}, u32[]{:S(2)}, u32[]{:S(2)}) collective-permute-start(bf16[64,4096]{1,0:T(8,128)(2,1)S(1)} %get-tuple-element.71), channel_id=1, source_target_pairs={{0,2},{2,4},{4,6},{6,0},{1,3},{3,5},{5,7},{7,1},{8,10},{10,12},{12... | collective-permute-start | bytes 1572872 | tf_op jit(solution)/shard_map/ppermute | solution.py:395
  67.0 29.2 %collective-permute-start.5 = (bf16[64,4096]{1,0:T(8,128)(2,1)S(1)}, bf16[64,4096]{1,0:T(8,128)(2,1)S(1)}, u32[]{:S(2)}, u32[]{:S(2)}) collective-permute-start(bf16[64,4096]{1,0:T(8,128)(2,1)S(1)} %get-tuple-element.69), channel_id=1, source_target_pairs={{0,6},{2,0},{4,2},{6,4},{1,7},{3,1},{5,3},{7,5},{8,14},{10,8},{12,... | collective-permute-start | bytes 1572872 | tf_op jit(solution)/shard_map/ppermute | solution.py:395
  99.4 63.8 %all-to-all-start.1 = ((bf16[16,32,4096]{2,1,0:T(8,128)(2,1)}), bf16[16,32,4096]{2,1,0:T(8,128)(2,1)}, u32[]{:S(2)}, u32[]{:S(2)}) async-start(bf16[16,32,4096]{2,1,0:T(8,128)(2,1)} %bitcast.101), calls=%async_computation.1 | async-start | bytes 8388608 | tf_op jit(solution)/shard_map/all_to_all | solution.py:36
  106.2 29.5 %collective-permute-start.6 = (bf16[256,4096]{1,0:T(8,128)(2,1)}, bf16[256,4096]{1,0:T(8,128)(2,1)}, u32[]{:S(2)}, u32[]{:S(2)}) collective-permute-start(bf16[256,4096]{1,0:T(8,128)(2,1)} %get-tuple-element.42.p2), channel_id=1, source_target_pairs={{4,8},{6,10},{8,4},{10,6},{5,9},{7,11},{9,5},{11,7},{20,24},{22,26... | collective-permute-start | bytes 6291464 | tf_op jit(solution)/shard_map/ppermute | solution.py:368
  109.0 45.7 %collective-permute-start.7 = (bf16[256,4096]{1,0:T(8,128)(2,1)}, bf16[256,4096]{1,0:T(8,128)(2,1)}, u32[]{:S(2)}, u32[]{:S(2)}) collective-permute-start(bf16[256,4096]{1,0:T(8,128)(2,1)} %get-tuple-element.43.p3), channel_id=1, source_target_pairs={{0,8},{2,10},{4,0},{6,2},{8,12},{10,14},{12,4},{14,6},{1,9},{3,11}... | collective-permute-start | bytes 6291464 | tf_op jit(solution)/shard_map/ppermute | solution.py:368
  190.3 65.9 %all-to-all-start.2 = ((bf16[16,32,4096]{2,1,0:T(8,128)(2,1)}), bf16[16,32,4096]{2,1,0:T(8,128)(2,1)}, u32[]{:S(2)}, u32[]{:S(2)}) async-start(bf16[16,32,4096]{2,1,0:T(8,128)(2,1)} %bitcast.102), calls=%async_computation.2 | async-start | bytes 8388608 | tf_op jit(solution)/shard_map/all_to_all | solution.py:36
  204.1 45.1 %collective-permute-start.10 = (bf16[256,4096]{1,0:T(8,128)(2,1)S(1)}, bf16[256,4096]{1,0:T(8,128)(2,1)S(1)}, u32[]{:S(2)}, u32[]{:S(2)}) collective-permute-start(bf16[256,4096]{1,0:T(8,128)(2,1)S(1)} %get-tuple-element.49.q1), channel_id=1, source_target_pairs={{10,0},{8,2},{2,4},{0,6},{14,8},{12,10},{6,12},{4,14},{11,1},{9,3}... | collective-permute-start | bytes 6291464 | tf_op jit(solution)/shard_map/ppermute | solution.py:411
  206.3 48.6 %collective-permute-start.9 = (bf16[256,4096]{1,0:T(8,128)(2,1)S(1)}, bf16[256,4096]{1,0:T(8,128)(2,1)S(1)}, u32[]{:S(2)}, u32[]{:S(2)}) collective-permute-start(bf16[256,4096]{1,0:T(8,128)(2,1)S(1)} %get-tuple-element.48.q0), channel_id=1, source_target_pairs={{2,0},{0,2},{10,4},{8,6},{6,8},{4,10},{14,12},{12,14},{3,1},{1,3},... | collective-permute-start | bytes 6291464 | tf_op jit(solution)/shard_map/ppermute | solution.py:411
  264.0 13.7 %collective-permute-start.12 = (bf16[64,4096]{1,0:T(8,128)(2,1)}, bf16[64,4096]{1,0:T(8,128)(2,1)S(1)}, u32[]{:S(2)}, u32[]{:S(2)}) collective-permute-start(bf16[64,4096]{1,0:T(8,128)(2,1)} %get-tuple-element.66), channel_id=1, source_target_pairs={{0,4},{2,6},{4,0},{6,2},{1,5},{3,7},{5,1},{7,3},{8,12},{10,14},{12... | collective-permute-start | bytes 1572872 | tf_op jit(solution)/shard_map/ppermute | solution.py:419
  269.0 22.4 %collective-permute-start.11 = (bf16[64,4096]{1,0:T(8,128)(2,1)S(1)}, bf16[64,4096]{1,0:T(8,128)(2,1)S(1)}, u32[]{:S(2)}, u32[]{:S(2)}) collective-permute-start(bf16[64,4096]{1,0:T(8,128)(2,1)S(1)} %get-tuple-element.67), channel_id=1, source_target_pairs={{0,6},{2,0},{4,2},{6,4},{1,7},{3,1},{5,3},{7,5},{8,14},{10,8},{12,... | collective-permute-start | bytes 1572872 | tf_op jit(solution)/shard_map/ppermute | solution.py:419
  270.8 27.7 %collective-permute-start.21 = (bf16[64,2048]{1,0:T(8,128)(2,1)S(1)}, bf16[64,2048]{1,0:T(8,128)(2,1)S(1)}, u32[]{:S(2)}, u32[]{:S(2)}) collective-permute-start(bf16[64,2048]{1,0:T(8,128)(2,1)S(1)} %slice.159), channel_id=1, source_target_pairs={{0,8},{8,0},{1,9},{9,1},{2,10},{10,2},{3,11},{11,3},{4,12},{12,4},... | collective-permute-start | bytes 786440 | tf_op jit(solution)/shard_map/ppermute | solution.py:426
  272.2 22.4 %collective-permute-start.13 = (bf16[64,4096]{1,0:T(8,128)(2,1)}, bf16[64,4096]{1,0:T(8,128)(2,1)S(1)}, u32[]{:S(2)}, u32[]{:S(2)}) collective-permute-start(bf16[64,4096]{1,0:T(8,128)(2,1)} %get-tuple-element.65), channel_id=1, source_target_pairs={{0,2},{2,4},{4,6},{6,0},{1,3},{3,5},{5,7},{7,1},{8,10},{10,12},{12... | collective-permute-start | bytes 1572872 | tf_op jit(solution)/shard_map/ppermute | solution.py:419
  300.7 13.7 %collective-permute-start.22 = (bf16[64,2048]{1,0:T(8,128)(2,1)}, bf16[64,2048]{1,0:T(8,128)(2,1)}, u32[]{:S(2)}, u32[]{:S(2)}) collective-permute-start(bf16[64,2048]{1,0:T(8,128)(2,1)} %slice.161), channel_id=1, source_target_pairs={{0,8},{8,0},{1,9},{9,1},{2,10},{10,2},{3,11},{11,3},{4,12},{12,4},... | collective-permute-start | bytes 786440 | tf_op jit(solution)/shard_map/ppermute | solution.py:426
  300.8 16.0 %collective-permute-start.23 = (bf16[64,2048]{1,0:T(8,128)(2,1)}, bf16[64,2048]{1,0:T(8,128)(2,1)}, u32[]{:S(2)}, u32[]{:S(2)}) collective-permute-start(bf16[64,2048]{1,0:T(8,128)(2,1)} %slice.129), channel_id=1, source_target_pairs={{0,8},{8,0},{1,9},{9,1},{2,10},{10,2},{3,11},{11,3},{4,12},{12,4},... | collective-permute-start | bytes 786440 | tf_op jit(solution)/shard_map/ppermute | solution.py:426
  302.0 15.8 %collective-permute-start.24 = (bf16[64,2048]{1,0:T(8,128)(2,1)}, bf16[64,2048]{1,0:T(8,128)(2,1)}, u32[]{:S(2)}, u32[]{:S(2)}) collective-permute-start(bf16[64,2048]{1,0:T(8,128)(2,1)} %slice.163), channel_id=1, source_target_pairs={{0,8},{8,0},{1,9},{9,1},{2,10},{10,2},{3,11},{11,3},{4,12},{12,4},... | collective-permute-start | bytes 786440 | tf_op jit(solution)/shard_map/ppermute | solution.py:426
  302.0 49.0 %collective-permute-start.25 = (bf16[256,4096]{1,0:T(8,128)(2,1)S(1)}, bf16[256,4096]{1,0:T(8,128)(2,1)}, u32[]{:S(2)}, u32[]{:S(2)}) collective-permute-start(bf16[256,4096]{1,0:T(8,128)(2,1)S(1)} %copy-done.8), channel_id=1, source_target_pairs={{8,4},{10,6},{4,8},{6,10},{9,5},{11,7},{5,9},{7,11},{24,20},{26,22... | collective-permute-start | bytes 6291464 | tf_op jit(solution)/shard_map/ppermute | solution.py:411
  306.5 46.9 %collective-permute-start.26 = (bf16[256,4096]{1,0:T(8,128)(2,1)}, bf16[256,4096]{1,0:T(8,128)(2,1)}, u32[]{:S(2)}, u32[]{:S(2)}) collective-permute-start(bf16[256,4096]{1,0:T(8,128)(2,1)} %get-tuple-element.55.q3), channel_id=1, source_target_pairs={{8,0},{10,2},{0,4},{2,6},{12,8},{14,10},{4,12},{6,14},{9,1},{11,3}... | collective-permute-start | bytes 6291464 | tf_op jit(solution)/shard_map/ppermute | solution.py:411
  324.0 26.9 %all-to-all-start.3 = ((bf16[16,16,2048]{2,1,0:T(8,128)(2,1)}), bf16[16,16,2048]{2,1,0:T(8,128)(2,1)S(1)}, u32[]{:S(2)}, u32[]{:S(2)}) async-start(bf16[16,16,2048]{2,1,0:T(8,128)(2,1)} %bitcast.35), calls=%async_computation.3 | async-start | bytes 2097152 | tf_op jit(solution)/shard_map/all_to_all | solution.py:36
  331.7 13.0 %collective-permute-start.19 = (f32[2,4,1024]{2,1,0:T(4,128)S(1)}, f32[2,4,1024]{2,1,0:T(4,128)S(1)}, u32[]{:S(2)}, u32[]{:S(2)}) collective-permute-start(f32[2,4,1024]{2,1,0:T(4,128)S(1)} %squeeze.38), channel_id=1, source_target_pairs={{0,48},{16,0},{32,16},{48,32},{1,49},{17,1},{33,17},{49,33},{2,50}... | collective-permute-start | bytes 98312 | tf_op jit(solution)/shard_map/ppermute | solution.py:461
  381.9 16.6 %collective-permute-start.38 = (f32[32,2048]{1,0:T(8,128)}, f32[32,2048]{1,0:T(8,128)}, u32[]{:S(2)}, u32[]{:S(2)}) collective-permute-start(f32[32,2048]{1,0:T(8,128)} %pad_maximum_fusion.4), channel_id=1, source_target_pairs={{0,8},{8,0},{1,9},{9,1},{2,10},{10,2},{3,11},{11,3},{4,12},{12,4},... | collective-permute-start | bytes 786440 | tf_op jit(solution)/shard_map/ppermute | solution.py:476
  (46 other events, 413.5 us)

commit v4 on v3

--- a/solution.py
+++ b/solution.py
@@ -16,6 +16,7 @@
 sizes = (2, 4, 2, 4, 2)
 owners = ("yh", "x", "core")
 near = ("yh", "x", "b")
+same_core = ("yh", "x", "z", "b")
 column = ("core", "z")
 swap = [(0, 1), (1, 0)]
 NN = ((1,), (0,))
@@ -26,6 +27,10 @@
 vmem_spec = pl.BlockSpec(memory_space=pltpu.VMEM)
 smem_spec = pl.BlockSpec(memory_space=pltpu.SMEM)
 roomy = pltpu.CompilerParams(vmem_limit_bytes=48 * 1024 * 1024)
+
+
+def block_at(index, size):
+    return pl.ds(pl.multiple_of(index * size, size), size)
 
 
 def mm(left, right, contract=NN):
@@ -90,10 +95,14 @@
                     pltpu.make_async_copy(source, target, taken.at[step]).start()
     rows = tokens.shape[0]
     hot = (lax.broadcasted_iota(jnp.int32, (rows, rows), 0) == place_ref[...]).astype(bf16)
-    for start in range(0, tokens.shape[1], 512):
-        here = pl.ds(start, 512)
+
+    def step(index, carry):
+        here = block_at(index, 512)
         sent[:, 0, :, here] = mm(hot, tokens[:, here]).astype(bf16).reshape(8, 16, 512)
         sent[:, 1, :, here] = mm(hot, cotangent[:, here]).astype(bf16).reshape(8, 16, 512)
+        return carry
+
+    lax.fori_loop(0, tokens.shape[1] // 512, step, 0)
     for step in range(4):
         pltpu.make_async_copy(w_out.at[0], held.at[step], taken.at[step]).wait()
         pltpu.make_async_copy(held.at[step], packed[step], put.at[step]).start()
@@ -118,46 +127,61 @@
     )(at, place, tokens, cotangent, w_in, w_out)
 
 
-def unpack_body(
-    at_ref, p0, p1, p2, p3, q0, q1, q2, q3, w_in, w_out, held, taken, put
-):
-    come, made = (p0, p1, p2, p3), (q0, q1, q2, q3)
-    for step in range(4):
+def unpack_body(steps, at_ref, *refs):
+    count = len(steps)
+    come, made = refs[:count], refs[count : 2 * count]
+    w_in, w_out, held, taken, put = refs[-5:]
+    for slot, step in enumerate(steps):
         @pl.when(at_ref[1] == step)
         def _():
-            pltpu.make_async_copy(made[step], held.at[step], taken.at[step]).start()
+            pltpu.make_async_copy(made[slot], held.at[slot], taken.at[slot]).start()
 
         @pl.when(at_ref[1] != step)
         def _():
-            pltpu.make_async_copy(come[step], held.at[step], taken.at[step]).start()
-    for step in range(4):
-        pltpu.make_async_copy(come[step], held.at[step], taken.at[step]).wait()
+            pltpu.make_async_copy(come[slot], held.at[slot], taken.at[slot]).start()
+    for slot, step in enumerate(steps):
+        pltpu.make_async_copy(come[slot], held.at[slot], taken.at[slot]).wait()
         for piece in range(4):
             @pl.when(at_ref[2 + step] == piece)
             def _():
-                for target, source in piece_copies(piece, w_in, w_out, held.at[step]):
-                    pltpu.make_async_copy(source, target, put.at[step]).start()
-    for step in range(4):
-        pltpu.make_async_copy(held.at[step], w_out.at[0], put.at[step]).wait()
-
-
-def unpack(at, come, made):
+                for target, source in piece_copies(piece, w_in, w_out, held.at[slot]):
+                    pltpu.make_async_copy(source, target, put.at[slot]).start()
+    for slot in range(count):
+        pltpu.make_async_copy(held.at[slot], w_out.at[0], put.at[slot]).wait()
+
+
+def unpack(steps, at, come, made, into=()):
+    count = len(steps)
     return pl.pallas_call(
-        unpack_body,
+        functools.partial(unpack_body, steps),
         out_shape=(
             jax.ShapeDtypeStruct((2, 4096, 256), bf16),
             jax.ShapeDtypeStruct((2, 256, 4096), bf16),
         ),
-        in_specs=[smem_spec] + [any_spec] * 8,
+        in_specs=[smem_spec] + [any_spec] * (2 * count + len(into)),
         out_specs=(any_spec, any_spec),
         scratch_shapes=[
-            pltpu.VMEM((4, 256, 4096), bf16),
-            pltpu.SemaphoreType.DMA((4,)),
-            pltpu.SemaphoreType.DMA((4,)),
+            pltpu.VMEM((count, 256, 4096), bf16),
+            pltpu.SemaphoreType.DMA((count,)),
+            pltpu.SemaphoreType.DMA((count,)),
         ],
+        input_output_aliases={1 + 2 * count + k: k for k in range(len(into))},
         compiler_params=roomy,
-        cost_estimate=pl.CostEstimate(flops=0, bytes_accessed=16 << 20, transcendentals=0),
-    )(at, *come, *made)
+        cost_estimate=pl.CostEstimate(
+            flops=0, bytes_accessed=count << 22, transcendentals=0
+        ),
+    )(at, *[come[k] for k in steps], *[made[k] for k in steps], *into)
+
+
+def row_copies(at_ref, rows_in, rows, sem):
+    copies = []
+    for d in range(4):
+        at_z = lax.rem(at_ref[6] + 4 - d, 4)
+        for b in range(2):
+            copies.append(
+                pltpu.make_async_copy(rows_in.at[:, b, d], rows.at[:, at_z, b], sem)
+            )
+    return copies
 
 
 def load_weights(at_ref, weights, packed, tall, wide, sems):
@@ -193,25 +217,32 @@
 ):
     core = at_ref[0]
     weights = (w0, w1, w2, w3)
-    pltpu.make_async_copy(rows_in, rows, row_sem).start()
+    for copy in row_copies(at_ref, rows_in, rows, row_sem):
+        copy.start()
     load_weights(at_ref, weights, (p0, p1, p2, p3), tall, wide, sems)
-    pltpu.make_async_copy(rows_in, rows, row_sem).wait()
+    pltpu.make_async_copy(rows, rows, row_sem).wait()
 
     @pl.when(core == 0)
     def _():
-        for slot in range(4):
+        def slot_step(slot, carry):
             wait_weights(slot, weights, wide, sems)
-            here = slice(256 * slot, 256 * slot + 256)
-            pre_act = mm(rows[...], tall[:, here])
+            here = block_at(slot, 256)
+            pre_act = mm(rows[...].reshape(512, 4096), tall[:, here])
             pre_ref[:, here] = pre_act
             send_ref[:, here] = (pre_act * jax.nn.sigmoid(pre_act)).astype(bf16)
+            return carry
+
+        lax.fori_loop(0, 4, slot_step, 0)
 
     @pl.when(core == 1)
     def _():
-        for slot in range(4):
+        def slot_step(slot, carry):
             wait_weights(slot, weights, wide, sems)
-            here = slice(256 * slot, 256 * slot + 256)
-            send_ref[:, here] = mm(rows[...], wide[here, :], NT).astype(bf16)
+            here = block_at(slot, 256)
+            send_ref[:, here] = mm(rows[...].reshape(512, 4096), wide[here, :], NT).astype(bf16)
+            return carry
+
+        lax.fori_loop(0, 4, slot_step, 0)
 
 
 def up(at, rows, weights, packed):
@@ -224,7 +255,7 @@
         in_specs=[smem_spec] + [any_spec] * 9,
         out_specs=(vmem_spec, vmem_spec),
         scratch_shapes=[
-            pltpu.VMEM((512, 4096), bf16),
+            pltpu.VMEM((8, 4, 2, 8, 4096), bf16),
             pltpu.VMEM((4096, 1024), bf16),
             pltpu.VMEM((1024, 4096), bf16),
             pltpu.SemaphoreType.DMA,
@@ -295,27 +326,43 @@
     )(at, pre_act, got, *weights, *packed)
 
 
-def grads_body(at_ref, rows, q_ref, g0, g1, g2, g3, tall, wide, sems):
+def grads_body(at_ref, rows_in, q_ref, g0, g1, g2, g3, rows, tall, wide, row_sem, sems):
     core = at_ref[0]
     grads = (g0, g1, g2, g3)
+    for copy in row_copies(at_ref, rows_in, rows, row_sem):
+        copy.start()
+    pltpu.make_async_copy(rows, rows, row_sem).wait()
 
     @pl.when(core == 0)
     def _():
-        for slot in range(4):
-            here = slice(256 * slot, 256 * slot + 256)
-            tall[:, here] = mm(rows[...], q_ref[:, here], TN).astype(bf16)
-            for a in range(16):
-                block = pl.ds(256 * a, 256)
-                source = tall.at[block, pl.ds(256 * slot, 256)]
-                pltpu.make_async_copy(source, grads[slot].at[:, block], sems.at[slot]).start()
+        def slot_step(at, carry):
+            here = block_at(at, 256)
+            tall[:, here] = mm(rows[...].reshape(512, 4096), q_ref[:, here], TN).astype(bf16)
+            for slot in range(4):
+                @pl.when(at == slot)
+                def _():
+                    for a in range(16):
+                        block = pl.ds(256 * a, 256)
+                        source = tall.at[block, pl.ds(256 * slot, 256)]
+                        target = grads[slot].at[:, block]
+                        pltpu.make_async_copy(source, target, sems.at[slot]).start()
+            return carry
+
+        lax.fori_loop(0, 4, slot_step, 0)
 
     @pl.when(core == 1)
     def _():
-        for slot in range(4):
-            here = slice(256 * slot, 256 * slot + 256)
-            wide[here, :] = mm(q_ref[:, here], rows[...], TN).astype(bf16)
-            source = wide.at[pl.ds(256 * slot, 256), :]
-            pltpu.make_async_copy(source, grads[slot ^ 1], sems.at[slot]).start()
+        def slot_step(at, carry):
+            here = block_at(at, 256)
+            wide[here, :] = mm(q_ref[:, here], rows[...].reshape(512, 4096), TN).astype(bf16)
+            for slot in range(4):
+                @pl.when(at == slot)
+                def _():
+                    source = wide.at[pl.ds(256 * slot, 256), :]
+                    pltpu.make_async_copy(source, grads[slot ^ 1], sems.at[slot]).start()
+            return carry
+
+        lax.fori_loop(0, 4, slot_step, 0)
 
     for slot in range(4):
         pltpu.make_async_copy(wide.at[pl.ds(0, 256), :], grads[0], sems.at[slot]).wait()
@@ -326,11 +373,13 @@
     return pl.pallas_call(
         grads_body,
         out_shape=(shape,) * 4,
-        in_specs=[smem_spec] + [vmem_spec] * 2,
+        in_specs=[smem_spec, any_spec, vmem_spec],
         out_specs=(any_spec,) * 4,
         scratch_shapes=[
+            pltpu.VMEM((8, 4, 2, 8, 4096), bf16),
             pltpu.VMEM((4096, 1024), bf16),
             pltpu.VMEM((1024, 4096), bf16),
+            pltpu.SemaphoreType.DMA,
             pltpu.SemaphoreType.DMA((4,)),
         ],
         compiler_params=roomy,
@@ -338,6 +387,92 @@
             flops=2 * 512 * 4096 * 1024, bytes_accessed=13 << 20, transcendentals=0
         ),
     )(at, rows, units)
+
+
+def group_mask():
+    column = lax.broadcasted_iota(jnp.int32, (8, 256), 1) // 2 % 8
+    return (column == lax.broadcasted_iota(jnp.int32, (8, 256), 0)).astype(f32)
+
+
+def dots_body(back_ref, held_ref, low_ref, high_ref, dots_ref):
+    total = jnp.zeros((256, 256), f32)
+    for start in range(0, 4096, 512):
+        here = slice(start, start + 512)
+        one, two = back_ref[:, 0, :, here], back_ref[:, 1, :, here]
+        both = (one.astype(f32) + two.astype(f32)).astype(bf16).reshape(256, 512)
+        target, at = (low_ref, start) if start < 2048 else (high_ref, start - 2048)
+        target[:, at : at + 512] = both
+        total += mm(both, held_ref[:, here], NT)
+    dots_ref[...] = jnp.sum(total.reshape(32, 8, 256) * group_mask()[None], axis=1)
+
+
+def sum_and_dots(back, held):
+    piece = jax.ShapeDtypeStruct((256, 2048), bf16)
+    return pl.pallas_call(
+        dots_body,
+        out_shape=(piece, piece, jax.ShapeDtypeStruct((32, 256), f32)),
+        in_specs=[vmem_spec] * 2,
+        out_specs=(vmem_spec,) * 3,
+        compiler_params=roomy,
+        cost_estimate=pl.CostEstimate(flops=1 << 29, bytes_accessed=8 << 20, transcendentals=0),
+    )(back, held)
+
+
+def token_body(
+    at_ref, dots_ref, other_ref, spread_ref, scaled_ref, high_ref, come_ref, mixer_ref, held_ref,
+    rows_ref, part_ref, value,
+):
+    core = at_ref[0]
+    mask = group_mask()[None]
+    spread, scaled = spread_ref[...], scaled_ref[...]
+    d_weights = dots_ref[...] + other_ref[...]
+    mixing = jnp.sum(spread, axis=1)
+    column_sum = jnp.sum((mixing * d_weights)[:, None, :] * mask, axis=2, keepdims=True)
+    column_sum = jnp.sum(column_sum * mask, axis=1)
+    d_logits = mixing * (d_weights - column_sum) * (1.0 - scaled * scaled)
+    d_high = d_logits.astype(bf16)
+    d_low = (d_logits - d_high.astype(f32)).astype(bf16)
+    flat = spread.reshape(256, 256)
+    flat_high = flat.astype(bf16)
+    flat_low = (flat - flat_high.astype(f32)).astype(bf16)
+    left = jnp.concatenate([flat_high, flat_low, d_high, d_low], axis=0)
+
+    def token_rows(half_ref, offset):
+        for start in range(0, 2048, 512):
+            here = slice(start, start + 512)
+            half, mixer = half_ref[:, here], mixer_ref[:, offset + start : offset + start + 512]
+            right = jnp.concatenate([half, half, mixer, mixer], axis=0)
+            rows_ref[:, here] = mm(left, right, TN).astype(bf16)
+
+    @pl.when(core == 0)
+    def _():
+        token_rows(high_ref, 2048)
+        for start in range(0, 4096, 512):
+            here = slice(start, start + 512)
+            value[:, here] = mm(d_high, held_ref[:, here]) + mm(d_low, held_ref[:, here])
+        for row in range(4):
+            for at in range(32):
+                part_ref[32 * row + at] = value[8 * row : 8 * row + 8, 128 * at : 128 * at + 128]
+
+    @pl.when(core == 1)
+    def _():
+        token_rows(come_ref, 0)
+        part_ref[...] = jnp.zeros_like(part_ref)
+
+
+def token_grads(at, *arrays):
+    return pl.pallas_call(
+        token_body,
+        out_shape=(
+            jax.ShapeDtypeStruct((256, 2048), bf16),
+            jax.ShapeDtypeStruct((128, 8, 128), f32),
+        ),
+        in_specs=[smem_spec] + [vmem_spec] * 8,
+        out_specs=(vmem_spec,) * 2,
+        scratch_shapes=[pltpu.VMEM((32, 4096), f32)],
+        compiler_params=roomy,
+        cost_estimate=pl.CostEstimate(flops=1 << 29, bytes_accessed=6 << 20, transcendentals=0),
+    )(at, *arrays)
 
 
 def shards(tokens, cotangent, group_of, mixer, w_in, w_out):
@@ -348,7 +483,7 @@
     half = width // 2
     plane = lax.axis_index("z")
     at = jnp.stack(
-        [core, own_step(core, plane)] + [piece_of(step, plane) for step in range(4)]
+        [core, own_step(core, plane)] + [piece_of(step, plane) for step in range(4)] + [plane]
     ).astype(jnp.int32)
     tie = lax.optimization_barrier
 
@@ -399,89 +534,48 @@
     weights += [send_weights(step + 2, piece) for step, piece in enumerate(later)]
     sent = jnp.stack([blocks[d].reshape(8, 8, width) for d in range(4)], axis=1)
     sent = jnp.broadcast_to(sent[:, None], (8, 2, 4, 8, width)).reshape(16, 32, width)
-    expert_rows = exchange(sent, near).reshape(512, width)
+    expert_rows = exchange(sent, near).reshape(8, 2, 4, 8, width)
 
     pre_act, given = up(at, expert_rows, weights, packed)
     got = lax.ppermute(given, "core", swap)
     part, units = down(at, pre_act, got, weights, packed)
     made = weight_grads(at, expert_rows, units)
-    back = exchange(part.reshape(16, 32, width), near)
+    back = exchange(part.reshape(64, 8, width), same_core)
 
     def send_grads(step, piece):
         return lax.ppermute(piece, column, back_round(step))
 
-    grads = [send_grads(step, made[step]) for step in range(2)]
-    back, grads[0], grads[1] = tie((back, grads[0], grads[1]))
-    back = jnp.sum(back.reshape(8, 2, 4, 8, width).astype(f32), axis=1).astype(bf16)
-    blocks = {}
-    for d in (2, 1, 3, 0):
-        block = back[:, d].reshape(64, width)
-        blocks[d] = lax.ppermute(block, "z", shift(-d)) if d else block
-    blocks[2], *later = tie((blocks[2], *made[2:]))
-    grads += [send_grads(step + 2, piece) for step, piece in enumerate(later)]
-    dots, halves = [], []
-    for d in range(4):
-        block = blocks[d]
-        dots.append(jnp.sum(mm(block, held, NT).reshape(8, 8, 256) * mask[None], axis=1))
-        come = lax.ppermute(block[:, :half], "core", swap)
-        halves.append(jnp.where(first, block[:, half:], come))
-    dots = jnp.concatenate(dots, axis=0)
-    back_half = jnp.concatenate(halves, axis=0)
-    d_weights = dots + lax.ppermute(dots, "core", swap)
-    mixing = jnp.sum(spread, axis=1)
-    column_sum = jnp.sum((mixing * d_weights)[:, None, :] * mask[None], axis=2, keepdims=True)
-    column_sum = jnp.sum(column_sum * mask[None], axis=1)
-    d_logits = mixing * (d_weights - column_sum) * (1.0 - scaled * scaled)
-    d_high, d_low = split_high_low(d_logits)
-
-    mixer_half = jnp.where(first, mixer_t[:, half:], mixer_t[:, :half])
-    grad_rows = (
-        mm(flat_high, back_half, TN)
-        + mm(flat_low, back_half, TN)
-        + mm(d_high, mixer_half, TN)
-        + mm(d_low, mixer_half, TN)
+    grads = [send_grads(0, made[0]), send_grads(1, made[1])]
+    back, *later = tie((back, *made[2:]))
+
+    def whole_order(array):
+        split = array.reshape(4, 8, *array.shape[1:])
+        order = [
+            lax.dynamic_index_in_dim(split, (e - plane) % 4, 0, keepdims=False) for e in range(4)
+        ]
+        return jnp.stack(order, axis=1).reshape(array.shape)
+
+    spread_e, scaled_e = whole_order(spread), whole_order(scaled)
+    low, high, dots = sum_and_dots(back.reshape(32, 2, 8, width), held)
+    come = lax.ppermute(low, "core", swap)
+    dots_other = lax.ppermute(dots, "core", swap)
+    grad_rows, mixer_part = token_grads(
+        at, dots, dots_other, spread_e, scaled_e, high, come, mixer.T, held
     )
-    grad_rows = exchange(grad_rows.astype(bf16).reshape(16, 16, half), owners)
-
-    here_yh, here_x = lax.axis_index("yh"), lax.axis_index("x")
-    steps = jnp.arange(32, dtype=jnp.int32)
-    far_x, far_yh, far_z = steps // 8, steps // 4 % 2, steps % 4
-    at_x, at_yh = (here_x + far_x) % 4, (here_yh + far_yh) % 2
-    take = far_z * 8 + at_yh * 4 + at_x
-    turn = (take[:, None] == steps[None, :]).astype(bf16)
-    part = mm(mm(turn, d_high).astype(bf16), held) + mm(mm(turn, d_low).astype(bf16), held)
-    come = lax.ppermute(part[:, half:], "core", [(0, 1)])
-    part = jnp.where(first, part[:, :half], come)
-    low_b = lax.axis_index("b") == 0
-    left, right = part[:, : half // 2], part[:, half // 2 :]
-    part = jnp.where(low_b, left, right)
-    part += lax.ppermute(jnp.where(low_b, right, left), "b", swap)
-    part = part.reshape(4, 2, 4, half // 2)
-    part = sum(
-        [lax.ppermute(part[d], "x", shift(d)) for d in range(1, 4)], start=part[0]
+    grads.append(send_grads(2, later[0]))
+    grad_rows = exchange(grad_rows.reshape(16, 16, half), owners)
+    grad_rows, mixer_part, grads[0], grads[1], last = tie(
+        (grad_rows, mixer_part, grads[0], grads[1], later[1])
     )
-    part = part[0] + lax.ppermute(part[1], "yh", swap)
-    part, grad_rows, grads[2], grads[3] = tie((part, grad_rows, grads[2], grads[3]))
-    part = sum(
-        [lax.ppermute(part[d : d + 1], "z", shift(d)) for d in range(1, 4)], start=part[:1]
-    )
-    part = jnp.concatenate(
-        [part] + [lax.ppermute(part, "z", shift(-d)) for d in range(1, 4)], axis=0
-    )
-    part = jnp.stack([part, lax.ppermute(part, "yh", swap)], axis=0)
-    part = jnp.stack([part] + [lax.ppermute(part, "x", shift(-d)) for d in range(1, 4)], axis=0)
-    part = part.reshape(32, half // 2)
-    come = lax.ppermute(part, "b", swap)
-    part = jnp.concatenate([jnp.where(low_b, part, come), jnp.where(low_b, come, part)], axis=1)
-    come = lax.ppermute(part, "core", swap)
-    part = jnp.concatenate([jnp.where(first, part, come), jnp.where(first, come, part)], axis=1)
-    expert_at = (at_yh * 4 + at_x) * 4 + (plane + far_z) % 4
-    turn = (expert_at[:, None] == steps[None, :]).astype(f32)
-    grad_mixer = lax.dot_general(
-        part, turn, (TN, ((), ())), precision=lax.Precision.HIGHEST, preferred_element_type=f32
-    )
-
-    grad_in, grad_out = unpack(at, grads, made)
+    pieces = exchange(mixer_part, axes)
+    grads.append(send_grads(3, last))
+    pieces, grads[2] = tie((pieces, grads[2]))
+    total = jnp.sum(pieces, axis=0, keepdims=True)
+    whole = exchange(jnp.broadcast_to(total, (128, 8, 128)), axes)
+    grad_mixer = whole.reshape(4, 32, 8, 128).transpose(1, 3, 0, 2).reshape(width, 32)
+
+    most = unpack((0, 1, 2), at, grads, made)
+    grad_in, grad_out = unpack((3,), at, grads, made, most)
     grad_rows = grad_rows.reshape(8, 2, 16, half)
     grad_tokens = jnp.concatenate(
         [mm(hot, grad_rows[:, 1 - side].reshape(rows, half), TN).astype(bf16) for side in range(2)],

time: 409 us -> 371 us (0.907); the launches traced: 401 us -> 370 us
  waiting for transfers between devices: 189 us -> 222 us
  matrix products: 28.9 us -> 3.72 us
  starting transfers between devices: 95 us -> 71.2 us
  other arithmetic: 16.2 us -> 4.63 us
  local copies, waits for them, and re-layouts: 22.7 us -> 15.3 us
  Pallas kernels: 47.5 us -> 52.5 us
    all_to_all x4 -> x6, waiting for transfers between devices: 32.6 us -> 98.6 us  [exchange(): return lax.all_to_all(array, names, split_axis=0, concat_axis=0, tiled=True)]
    ppermute x26 -> x2, starting transfers between devices: 42.7 us -> 2.45 us  [the longest x1 2.14 us: shards(): come = lax.ppermute(low, 'core', swap)]
    ppermute x26 -> x2, waiting for transfers between devices: 35.6 us -> 1.88 us  [the longest x1 1.72 us: shards(): dots_other = lax.ppermute(dots, 'core', swap)]
    dot_general x15 -> x5, matrix products: 27.6 us -> 3.72 us  [mm(): lax.dot_general(left, right, (contract, ((), ())), preferred_element_type...]
    all_to_all x4 -> x6, starting transfers between devices: 26.7 us -> 46.9 us  [exchange(): return lax.all_to_all(array, names, split_axis=0, concat_axis=0, tiled=True)]
    pallas_call x2 -> x5, Pallas kernels: 15.1 us -> 24.8 us  [the longest x1 9.21 us: weight_grads(): pl.pallas_call(grads_body, out_shape=(shape,) * 4, in_specs=[smem_spec, a...]
    ppermute x4, waiting for transfers between devices: 65.3 us -> 72.1 us  [send_weights(): return lax.ppermute(piece, column, weight_round(step))]
    select_n x8 -> x0, other arithmetic: 5.46 us -> none  [the longest x4 3.72 us: shards(): halves.append(jnp.where(first, block[:, half:], come))]
  transfers between devices with their start and end apart: 43 -> 21, of which waited for: 25 -> 16; matrix products, arithmetic and copies ran while one was open for 10% -> 3% of each run, Pallas kernels for 4% -> 6%
where the time goes in v4:
time: 371 us; the launch traced here: 370 us
  waiting for transfers between devices  222 us (60%)
  starting transfers between devices  71.2 us (19%)
  Pallas kernels  52.5 us (14%)
  local copies, waits for them, and re-layouts  15.3 us (4%)
  other arithmetic  4.63 us (1%)
  matrix products  3.72 us (1%)
    all_to_all x6, waiting for transfers between devices, exchange(): return lax.all_to_all(array, names, split_axis=0, concat_axis=0, tiled=True)  98.6 us
    ppermute x4, waiting for transfers between devices, send_weights(): return lax.ppermute(piece, column, weight_round(step))  72.1 us
    all_to_all x6, starting transfers between devices, exchange(): return lax.all_to_all(array, names, split_axis=0, concat_axis=0, tiled=True)  46.9 us
    ppermute x4, waiting for transfers between devices, send_grads(): return lax.ppermute(piece, column, back_round(step))  40.5 us
    pallas_call x1, Pallas kernels, down(): pl.pallas_call(down_body, out_shape=(jax.ShapeDtypeStruct((512, 4096), bf...  10.7 us
    pallas_call x1, Pallas kernels, up(): pl.pallas_call(up_body, out_shape=(jax.ShapeDtypeStruct((512, 1024), f32)...  9.75 us
    pallas_call x1, Pallas kernels, weight_grads(): pl.pallas_call(grads_body, out_shape=(shape,) * 4, in_specs=[smem_spec, a...  9.21 us
    pallas_call x2, Pallas kernels, unpack(): pl.pallas_call(functools.partial(unpack_body, steps), out_shape=(jax.Shap...  8.81 us
  transfers between devices with their start and end apart: 21, of which 16 were waited for; matrix products, arithmetic and copies ran while one was open for 3% of the time, Pallas kernels for 6%

profile of v4, /device:TPU:1, one launch (start us, length us, event | category | flops | bytes accessed | tf_op | source)
XLA Modules:
  0.0 370.2 jit_solution(3259996684454441342)
XLA Ops:
  5.8 7.2 %shard_map.102 = (bf16[8,2,16,4096]{3,2,1,0:T(8,128)(2,1)S(1)}, bf16[256,4096]{1,0:T(8,128)(2,1)}, bf16[256,4096]{1,0:T(8,128)(2,1)}, bf16[256,4096]{1,0:T(8,128)(2,1)}, bf16[256,4096]{1,0:T(8,128)(2,1)}) custom-call(s32[7]{0:T(128)S(1)} %stack.60.at_ref, s32[1,128]{1,0:T(1,128)S(1)} %reshape.218.place_ref, bf16[128,4096]{1,0:T(8,128)(2,1)S(1)} %reshape.219.tokens, ...), custom_call_target="tpu_custom_call" | custom-call | bytes 20971520 | tf_op jit(solution)/shard_map/pallas_call | solution.py:115
  14.3 8.6 %all-to-all-start = ((bf16[16,16,4096]{2,1,0:T(8,128)(2,1)}), bf16[16,16,4096]{2,1,0:T(8,128)(2,1)S(1)}, u32[]{:S(2)}, u32[]{:S(2)}) async-start(bf16[16,16,4096]{2,1,0:T(8,128)(2,1)} %bitcast.64), calls=%async_computation | async-start | bytes 4194304 | tf_op jit(solution)/shard_map/all_to_all | solution.py:41
  27.4 24.1 %all-to-all-done = bf16[16,16,4096]{2,1,0:T(8,128)(2,1)S(1)} async-done(((bf16[16,16,4096]{2,1,0:T(8,128)(2,1)}), bf16[16,16,4096]{2,1,0:T(8,128)(2,1)S(1)}, u32[]{:S(2)}, u32[]{:S(2)}) %all-to-all-start) | async-done | bytes 2097184 | tf_op jit(solution)/shard_map/all_to_all | solution.py:41
  61.6 27.2 %collective-permute-done.4.w1 = bf16[256,4096]{1,0:T(8,128)(2,1)} collective-permute-done((bf16[256,4096]{1,0:T(8,128)(2,1)}, bf16[256,4096]{1,0:T(8,128)(2,1)}, u32[]{:S(2)}, u32[]{:S(2)}) %collective-permute-start.4) | collective-permute-done | bytes 2097184 | tf_op jit(solution)/shard_map/ppermute | solution.py:503
  90.3 4.0 %collective-permute-done.5 = bf16[64,4096]{1,0:T(8,128)(2,1)S(1)} collective-permute-done((bf16[64,4096]{1,0:T(8,128)(2,1)S(1)}, bf16[64,4096]{1,0:T(8,128)(2,1)S(1)}, u32[]{:S(2)}, u32[]{:S(2)}) %collective-permute-start.5) | collective-permute-done | bytes 524320 | tf_op jit(solution)/shard_map/ppermute | solution.py:530
  97.4 6.9 %all-to-all-start.1 = ((bf16[16,32,4096]{2,1,0:T(8,128)(2,1)}), bf16[16,32,4096]{2,1,0:T(8,128)(2,1)}, u32[]{:S(2)}, u32[]{:S(2)}) async-start(bf16[16,32,4096]{2,1,0:T(8,128)(2,1)} %bitcast.69), calls=%async_computation.1 | async-start | bytes 8388608 | tf_op jit(solution)/shard_map/all_to_all | solution.py:41
  108.2 25.6 %collective-permute-done.6.w2 = bf16[256,4096]{1,0:T(8,128)(2,1)} collective-permute-done((bf16[256,4096]{1,0:T(8,128)(2,1)}, bf16[256,4096]{1,0:T(8,128)(2,1)}, u32[]{:S(2)}, u32[]{:S(2)}) %collective-permute-start.6) | collective-permute-done | bytes 2097184 | tf_op jit(solution)/shard_map/ppermute | solution.py:503
  133.8 19.2 %collective-permute-done.7.w3 = bf16[256,4096]{1,0:T(8,128)(2,1)} collective-permute-done((bf16[256,4096]{1,0:T(8,128)(2,1)}, bf16[256,4096]{1,0:T(8,128)(2,1)}, u32[]{:S(2)}, u32[]{:S(2)}) %collective-permute-start.7) | collective-permute-done | bytes 2097184 | tf_op jit(solution)/shard_map/ppermute | solution.py:503
  153.0 8.2 %all-to-all-done.1 = bf16[16,32,4096]{2,1,0:T(8,128)(2,1)} async-done(((bf16[16,32,4096]{2,1,0:T(8,128)(2,1)}), bf16[16,32,4096]{2,1,0:T(8,128)(2,1)}, u32[]{:S(2)}, u32[]{:S(2)}) %all-to-all-start.1) | async-done | bytes 4194336 | tf_op jit(solution)/shard_map/all_to_all | solution.py:41
  161.2 9.8 %shard_map.103 = (f32[512,1024]{1,0:T(8,128)S(1)}, bf16[512,1024]{1,0:T(8,128)(2,1)S(1)}) custom-call(s32[7]{0:T(128)S(1)} %stack.60.at_ref, bf16[8,2,4,8,4096]{4,3,2,1,0:T(8,128)(2,1)} %bitcast.20.rows_in, bf16[256,4096]{1,0:T(8,128)(2,1)} %collective-permute-done.3.w0, bf16[256,4096]{1,0:T(8,128)(2,1)} %collective-permute-done.4.w1, ...), custom_call_target="tpu_custom_call" | custom-call | flops 4294967296 | bytes 15728640 | tf_op jit(solution)/shard_map/pallas_call | solution.py:249
  175.7 10.7 %shard_map.104 = (bf16[512,4096]{1,0:T(8,128)(2,1)}, bf16[512,1024]{1,0:T(8,128)(2,1)S(1)}) custom-call(s32[7]{0:T(128)S(1)} %stack.60.at_ref, f32[512,1024]{1,0:T(8,128)S(1)} %get-tuple-element.51.pre_ref, bf16[512,1024]{1,0:T(8,128)(2,1)S(1)} %collective-permute-done.8.got_ref, bf16[256,4096]{1,0:T(8,128)(2,1)} %collective-permute-done.3.w0, ...), custom_call_target="tpu_custom_call" | custom-call | flops 4294967296 | bytes 16777216 | tf_op jit(solution)/shard_map/pallas_call | solution.py:309
  186.4 9.6 %all-to-all-start.2 = ((bf16[64,8,4096]{2,1,0:T(8,128)(2,1)}), bf16[64,8,4096]{2,1,0:T(8,128)(2,1)}, u32[]{:S(2)}, u32[]{:S(2)}) async-start(bf16[64,8,4096]{2,1,0:T(8,128)(2,1)} %bitcast.70), calls=%async_computation.2 | async-start | bytes 8388608 | tf_op jit(solution)/shard_map/all_to_all | solution.py:41
  196.0 9.2 %shard_map.105 = (bf16[256,4096]{1,0:T(8,128)(2,1)}, bf16[256,4096]{1,0:T(8,128)(2,1)}, bf16[256,4096]{1,0:T(8,128)(2,1)}, bf16[256,4096]{1,0:T(8,128)(2,1)}) custom-call(s32[7]{0:T(128)S(1)} %stack.60.at_ref, bf16[8,2,4,8,4096]{4,3,2,1,0:T(8,128)(2,1)} %bitcast.20.rows_in, bf16[512,1024]{1,0:T(8,128)(2,1)S(1)} %get-tuple-element.54.q_ref), custom_call_target="tpu_custom_call" | custom-call | flops 4294967296 | bytes 13631488 | tf_op jit(solution)/shard_map/pallas_call | solution.py:373
  205.3 3.7 collective-permute-start.11
  209.0 39.0 %all-to-all-done.2 = bf16[64,8,4096]{2,1,0:T(8,128)(2,1)} async-done(((bf16[64,8,4096]{2,1,0:T(8,128)(2,1)}), bf16[64,8,4096]{2,1,0:T(8,128)(2,1)}, u32[]{:S(2)}, u32[]{:S(2)}) %all-to-all-start.2) | async-done | bytes 4194336 | tf_op jit(solution)/shard_map/all_to_all | solution.py:41
  248.0 3.9 %shard_map.106 = (bf16[256,2048]{1,0:T(8,128)(2,1)}, bf16[256,2048]{1,0:T(8,128)(2,1)S(1)}, f32[32,256]{1,0:T(8,128)S(1)}) custom-call(bf16[32,2,8,4096]{3,2,1,0:T(8,128)(2,1)} %bitcast.22.back_ref, bf16[256,4096]{1,0:T(8,128)(2,1)S(1)} %bitcast.62), custom_call_target="tpu_custom_call" | custom-call | flops 536870912 | bytes 8388608 | tf_op jit(solution)/shard_map/pallas_call | solution.py:411
  261.2 8.3 %all-to-all-start.3 = ((bf16[16,16,2048]{2,1,0:T(8,128)(2,1)}), bf16[16,16,2048]{2,1,0:T(8,128)(2,1)S(1)}, u32[]{:S(2)}, u32[]{:S(2)}) async-start(bf16[16,16,2048]{2,1,0:T(8,128)(2,1)} %bitcast.68), calls=%async_computation.3 | async-start | bytes 2097152 | tf_op jit(solution)/shard_map/all_to_all | solution.py:41
  271.4 17.6 %collective-permute-done.11.refs_0_ = bf16[256,4096]{1,0:T(8,128)(2,1)} collective-permute-done((bf16[256,4096]{1,0:T(8,128)(2,1)}, bf16[256,4096]{1,0:T(8,128)(2,1)}, u32[]{:S(2)}, u32[]{:S(2)}) %collective-permute-start.11) | collective-permute-done | bytes 2097184 | tf_op jit(solution)/shard_map/ppermute | solution.py:546
  288.9 22.9 %collective-permute-done.12.refs_1_ = bf16[256,4096]{1,0:T(8,128)(2,1)} collective-permute-done((bf16[256,4096]{1,0:T(8,128)(2,1)}, bf16[256,4096]{1,0:T(8,128)(2,1)}, u32[]{:S(2)}, u32[]{:S(2)}) %collective-permute-start.12) | collective-permute-done | bytes 2097184 | tf_op jit(solution)/shard_map/ppermute | solution.py:546
  312.0 8.2 %all-to-all-start.4 = ((f32[128,8,128]{2,1,0:T(8,128)}), f32[128,8,128]{2,1,0:T(8,128)}, u32[]{:S(2)}, u32[]{:S(2)}) async-start(f32[128,8,128]{2,1,0:T(8,128)} %copy-done.5), calls=%async_computation.4 | async-start | bytes 1048576 | tf_op jit(solution)/shard_map/all_to_all | solution.py:41
  322.2 22.4 %all-to-all-done.4 = f32[128,8,128]{2,1,0:T(8,128)} async-done(((f32[128,8,128]{2,1,0:T(8,128)}), f32[128,8,128]{2,1,0:T(8,128)}, u32[]{:S(2)}, u32[]{:S(2)}) %all-to-all-start.4) | async-done | bytes 524320 | tf_op jit(solution)/shard_map/all_to_all | solution.py:41
  346.6 5.4 %all-to-all-start.5 = ((f32[128,8,128]{2,1,0:T(8,128)}), f32[128,8,128]{2,1,0:T(8,128)}, u32[]{:S(2)}, u32[]{:S(2)}) async-start(f32[128,8,128]{2,1,0:T(8,128)} %broadcast_in_dim.5), calls=%async_computation.5 | async-start | bytes 1048576 | tf_op jit(solution)/shard_map/all_to_all | solution.py:41
  354.7 5.3 %shard_map.108 = (bf16[2,4096,256]{2,1,0:T(8,128)(2,1)}, bf16[2,256,4096]{2,1,0:T(8,128)(2,1)}) custom-call(s32[7]{0:T(128)S(1)} %stack.60.at_ref, bf16[256,4096]{1,0:T(8,128)(2,1)} %collective-permute-done.11.refs_0_, bf16[256,4096]{1,0:T(8,128)(2,1)} %collective-permute-done.12.refs_1_, bf16[256,4096]{1,0:T(8,128)(2,1)} %collective-permute-done.13.refs_2_, ...), custom_call_target="tpu_custom_call" | custom-call | bytes 12582912 | tf_op jit(solution)/shard_map/pallas_call | solution.py:155
  360.1 4.8 %all-to-all-done.5 = f32[128,8,128]{2,1,0:T(8,128)} async-done(((f32[128,8,128]{2,1,0:T(8,128)}), f32[128,8,128]{2,1,0:T(8,128)}, u32[]{:S(2)}, u32[]{:S(2)}) %all-to-all-start.5) | async-done | bytes 524320 | tf_op jit(solution)/shard_map/all_to_all | solution.py:41
  (89 shorter events, 57.2 us)
Async XLA Ops:
  14.3 37.2 %all-to-all-start = ((bf16[16,16,4096]{2,1,0:T(8,128)(2,1)}), bf16[16,16,4096]{2,1,0:T(8,128)(2,1)S(1)}, u32[]{:S(2)}, u32[]{:S(2)}) async-start(bf16[16,16,4096]{2,1,0:T(8,128)(2,1)} %bitcast.64), calls=%async_computation | async-start | bytes 4194304 | tf_op jit(solution)/shard_map/all_to_all | solution.py:41
  22.9 38.7 %collective-permute-start.3 = (bf16[256,4096]{1,0:T(8,128)(2,1)}, bf16[256,4096]{1,0:T(8,128)(2,1)}, u32[]{:S(2)}, u32[]{:S(2)}) collective-permute-start(bf16[256,4096]{1,0:T(8,128)(2,1)} %get-tuple-element.42.p0), channel_id=1, source_target_pairs={{0,2},{2,0},{4,10},{6,8},{8,6},{10,4},{12,14},{14,12},{1,3},{3,1},... | collective-permute-start | bytes 6291464 | tf_op jit(solution)/shard_map/ppermute | solution.py:503
  26.2 62.6 %collective-permute-start.4 = (bf16[256,4096]{1,0:T(8,128)(2,1)}, bf16[256,4096]{1,0:T(8,128)(2,1)}, u32[]{:S(2)}, u32[]{:S(2)}) collective-permute-start(bf16[256,4096]{1,0:T(8,128)(2,1)} %get-tuple-element.43.p1), channel_id=1, source_target_pairs={{0,10},{2,8},{4,2},{6,0},{8,14},{10,12},{12,6},{14,4},{1,11},{3,9}... | collective-permute-start | bytes 6291464 | tf_op jit(solution)/shard_map/ppermute | solution.py:503
  51.5 196.5 %copy-start = (bf16[16,16,4096]{2,1,0:T(8,128)(2,1)}, bf16[16,16,4096]{2,1,0:T(8,128)(2,1)S(1)}, u32[]{:S(2)}) copy-start(bf16[16,16,4096]{2,1,0:T(8,128)(2,1)S(1)} %all-to-all-done) | copy-start | bytes 6291460
  52.2 1.6 collective-permute-start
  55.7 34.6 %collective-permute-start.2 = (bf16[64,4096]{1,0:T(8,128)(2,1)S(1)}, bf16[64,4096]{1,0:T(8,128)(2,1)S(1)}, u32[]{:S(2)}, u32[]{:S(2)}) collective-permute-start(bf16[64,4096]{1,0:T(8,128)(2,1)S(1)} %get-tuple-element.80), channel_id=1, source_target_pairs={{0,4},{2,6},{4,0},{6,2},{1,5},{3,7},{5,1},{7,3},{8,12},{10,14},{12... | collective-permute-start | bytes 1572872 | tf_op jit(solution)/shard_map/ppermute | solution.py:530
  58.9 31.5 %collective-permute-start.1 = (bf16[64,4096]{1,0:T(8,128)(2,1)S(1)}, bf16[64,4096]{1,0:T(8,128)(2,1)S(1)}, u32[]{:S(2)}, u32[]{:S(2)}) collective-permute-start(bf16[64,4096]{1,0:T(8,128)(2,1)S(1)} %get-tuple-element.81), channel_id=1, source_target_pairs={{0,2},{2,4},{4,6},{6,0},{1,3},{3,5},{5,7},{7,1},{8,10},{10,12},{12... | collective-permute-start | bytes 1572872 | tf_op jit(solution)/shard_map/ppermute | solution.py:530
  59.6 34.7 %collective-permute-start.5 = (bf16[64,4096]{1,0:T(8,128)(2,1)S(1)}, bf16[64,4096]{1,0:T(8,128)(2,1)S(1)}, u32[]{:S(2)}, u32[]{:S(2)}) collective-permute-start(bf16[64,4096]{1,0:T(8,128)(2,1)S(1)} %get-tuple-element.79), channel_id=1, source_target_pairs={{0,6},{2,0},{4,2},{6,4},{1,7},{3,1},{5,3},{7,5},{8,14},{10,8},{12,... | collective-permute-start | bytes 1572872 | tf_op jit(solution)/shard_map/ppermute | solution.py:530
  97.4 63.8 %all-to-all-start.1 = ((bf16[16,32,4096]{2,1,0:T(8,128)(2,1)}), bf16[16,32,4096]{2,1,0:T(8,128)(2,1)}, u32[]{:S(2)}, u32[]{:S(2)}) async-start(bf16[16,32,4096]{2,1,0:T(8,128)(2,1)} %bitcast.69), calls=%async_computation.1 | async-start | bytes 8388608 | tf_op jit(solution)/shard_map/all_to_all | solution.py:41
  104.3 29.5 %collective-permute-start.6 = (bf16[256,4096]{1,0:T(8,128)(2,1)}, bf16[256,4096]{1,0:T(8,128)(2,1)}, u32[]{:S(2)}, u32[]{:S(2)}) collective-permute-start(bf16[256,4096]{1,0:T(8,128)(2,1)} %get-tuple-element.49.p2), channel_id=1, source_target_pairs={{4,8},{6,10},{8,4},{10,6},{5,9},{7,11},{9,5},{11,7},{20,24},{22,26... | collective-permute-start | bytes 6291464 | tf_op jit(solution)/shard_map/ppermute | solution.py:503
  107.3 45.7 %collective-permute-start.7 = (bf16[256,4096]{1,0:T(8,128)(2,1)}, bf16[256,4096]{1,0:T(8,128)(2,1)}, u32[]{:S(2)}, u32[]{:S(2)}) collective-permute-start(bf16[256,4096]{1,0:T(8,128)(2,1)} %get-tuple-element.50.p3), channel_id=1, source_target_pairs={{0,8},{2,10},{4,0},{6,2},{8,12},{10,14},{12,4},{14,6},{1,9},{3,11}... | collective-permute-start | bytes 6291464 | tf_op jit(solution)/shard_map/ppermute | solution.py:503
  171.0 4.7 %collective-permute-start.8 = (bf16[512,1024]{1,0:T(8,128)(2,1)S(1)}, bf16[512,1024]{1,0:T(8,128)(2,1)S(1)}, u32[]{:S(2)}, u32[]{:S(2)}) collective-permute-start(bf16[512,1024]{1,0:T(8,128)(2,1)S(1)} %get-tuple-element.52), channel_id=1, source_target_pairs={{0,8},{8,0},{1,9},{9,1},{2,10},{10,2},{3,11},{11,3},{4,12},{12,4},... | collective-permute-start | bytes 3145736 | tf_op jit(solution)/shard_map/ppermute | solution.py:540
  186.4 61.6 %all-to-all-start.2 = ((bf16[64,8,4096]{2,1,0:T(8,128)(2,1)}), bf16[64,8,4096]{2,1,0:T(8,128)(2,1)}, u32[]{:S(2)}, u32[]{:S(2)}) async-start(bf16[64,8,4096]{2,1,0:T(8,128)(2,1)} %bitcast.70), calls=%async_computation.2 | async-start | bytes 8388608 | tf_op jit(solution)/shard_map/all_to_all | solution.py:41
  205.3 83.7 %collective-permute-start.11 = (bf16[256,4096]{1,0:T(8,128)(2,1)}, bf16[256,4096]{1,0:T(8,128)(2,1)}, u32[]{:S(2)}, u32[]{:S(2)}) collective-permute-start(bf16[256,4096]{1,0:T(8,128)(2,1)} %get-tuple-element.63.refs_3_), channel_id=1, source_target_pairs={{2,0},{0,2},{10,4},{8,6},{6,8},{4,10},{14,12},{12,14},{3,1},{1,3},... | collective-permute-start | bytes 6291464 | tf_op jit(solution)/shard_map/ppermute | solution.py:546
  209.0 102.9 %collective-permute-start.12 = (bf16[256,4096]{1,0:T(8,128)(2,1)}, bf16[256,4096]{1,0:T(8,128)(2,1)}, u32[]{:S(2)}, u32[]{:S(2)}) collective-permute-start(bf16[256,4096]{1,0:T(8,128)(2,1)} %get-tuple-element.64.refs_4_), channel_id=1, source_target_pairs={{10,0},{8,2},{2,4},{0,6},{14,8},{12,10},{6,12},{4,14},{11,1},{9,3}... | collective-permute-start | bytes 6291464 | tf_op jit(solution)/shard_map/ppermute | solution.py:546
  251.9 4.6 %collective-permute-start.10 = (bf16[256,2048]{1,0:T(8,128)(2,1)}, bf16[256,2048]{1,0:T(8,128)(2,1)S(1)}, u32[]{:S(2)}, u32[]{:S(2)}) collective-permute-start(bf16[256,2048]{1,0:T(8,128)(2,1)} %get-tuple-element.60), channel_id=1, source_target_pairs={{0,8},{8,0},{1,9},{9,1},{2,10},{10,2},{3,11},{11,3},{4,12},{12,4},... | collective-permute-start | bytes 3145736 | tf_op jit(solution)/shard_map/ppermute | solution.py:560
  254.3 2.1 collective-permute-start.9
  261.2 50.7 %copy-start.1 = (bf16[256,4096]{1,0:T(8,128)(2,1)S(1)}, bf16[256,4096]{1,0:T(8,128)(2,1)}, u32[]{:S(2)}) copy-start(bf16[256,4096]{1,0:T(8,128)(2,1)} %get-tuple-element.70.refs_1_) | copy-start | bytes 6291460
  261.2 50.7 %all-to-all-start.3 = ((bf16[16,16,2048]{2,1,0:T(8,128)(2,1)}), bf16[16,16,2048]{2,1,0:T(8,128)(2,1)S(1)}, u32[]{:S(2)}, u32[]{:S(2)}) async-start(bf16[16,16,2048]{2,1,0:T(8,128)(2,1)} %bitcast.68), calls=%async_computation.3 | async-start | bytes 2097152 | tf_op jit(solution)/shard_map/all_to_all | solution.py:41
  269.4 52.7 %collective-permute-start.13 = (bf16[256,4096]{1,0:T(8,128)(2,1)}, bf16[256,4096]{1,0:T(8,128)(2,1)}, u32[]{:S(2)}, u32[]{:S(2)}) collective-permute-start(bf16[256,4096]{1,0:T(8,128)(2,1)} %get-tuple-element.68.refs_5_), channel_id=1, source_target_pairs={{8,4},{10,6},{4,8},{6,10},{9,5},{11,7},{5,9},{7,11},{24,20},{26,22... | collective-permute-start | bytes 6291464 | tf_op jit(solution)/shard_map/ppermute | solution.py:546
  311.8 53.0 %collective-permute-start.14 = (bf16[256,4096]{1,0:T(8,128)(2,1)S(1)}, bf16[256,4096]{1,0:T(8,128)(2,1)}, u32[]{:S(2)}, u32[]{:S(2)}) collective-permute-start(bf16[256,4096]{1,0:T(8,128)(2,1)S(1)} %copy-done.1), channel_id=1, source_target_pairs={{8,0},{10,2},{0,4},{2,6},{12,8},{14,10},{4,12},{6,14},{9,1},{11,3}... | collective-permute-start | bytes 6291464 | tf_op jit(solution)/shard_map/ppermute | solution.py:546
  312.0 32.7 %all-to-all-start.4 = ((f32[128,8,128]{2,1,0:T(8,128)}), f32[128,8,128]{2,1,0:T(8,128)}, u32[]{:S(2)}, u32[]{:S(2)}) async-start(f32[128,8,128]{2,1,0:T(8,128)} %copy-done.5), calls=%async_computation.4 | async-start | bytes 1048576 | tf_op jit(solution)/shard_map/all_to_all | solution.py:41
  321.0 31.0 %copy-start.6 = (bf16[8,1,16,2048]{3,2,1,0:T(8,128)(2,1)S(1)}, bf16[8,1,16,2048]{3,2,1,0:T(8,128)(2,1)}, u32[]{:S(2)}) copy-start(bf16[8,1,16,2048]{3,2,1,0:T(8,128)(2,1)} %get-tuple-element.83) | copy-start | bytes 1572868
  346.6 18.2 %all-to-all-start.5 = ((f32[128,8,128]{2,1,0:T(8,128)}), f32[128,8,128]{2,1,0:T(8,128)}, u32[]{:S(2)}, u32[]{:S(2)}) async-start(f32[128,8,128]{2,1,0:T(8,128)} %broadcast_in_dim.5), calls=%async_computation.5 | async-start | bytes 1048576 | tf_op jit(solution)/shard_map/all_to_all | solution.py:41
  (6 other events, 20.2 us)

commit v5 on v4

--- a/solution.py
+++ b/solution.py
@@ -60,13 +60,7 @@
 
 
 def own_step(core, z):
-    table = [-1] * 8
-    for step in range(4):
-        sending = [a for a, _ in weight_round(step)]
-        for at in range(8):
-            if at not in sending:
-                table[at] = step
-    return jnp.array(table, jnp.int32)[core * 4 + z]
+    return jnp.where(z // 2 == core, 2, -1)
 
 
 def back_round(step):
@@ -83,48 +77,55 @@
     ]
 
 
-def sort_body(
-    at_ref, place_ref, tokens, cotangent, w_in, w_out, sent, p0, p1, p2, p3, held, taken, put
-):
-    packed = (p0, p1, p2, p3)
-    for step in range(4):
+def pack_body(first, at_ref, w_in, w_out, p0, p1, held, taken, put):
+    packed = (p0, p1)
+    for slot in range(2):
         for piece in range(4):
-            @pl.when(at_ref[2 + step] == piece)
+            @pl.when(at_ref[2 + first + slot] == piece)
             def _():
-                for source, target in piece_copies(piece, w_in, w_out, held.at[step]):
-                    pltpu.make_async_copy(source, target, taken.at[step]).start()
+                for source, target in piece_copies(piece, w_in, w_out, held.at[slot]):
+                    pltpu.make_async_copy(source, target, taken.at[slot]).start()
+    for slot in range(2):
+        pltpu.make_async_copy(w_out.at[0], held.at[slot], taken.at[slot]).wait()
+        pltpu.make_async_copy(held.at[slot], packed[slot], put.at[slot]).start()
+    for slot in range(2):
+        pltpu.make_async_copy(held.at[slot], packed[slot], put.at[slot]).wait()
+
+
+def pack(first, at, w_in, w_out):
+    return pl.pallas_call(
+        functools.partial(pack_body, first),
+        out_shape=(jax.ShapeDtypeStruct((256, 4096), bf16),) * 2,
+        in_specs=[smem_spec] + [any_spec] * 2,
+        out_specs=(any_spec,) * 2,
+        scratch_shapes=[
+            pltpu.VMEM((2, 256, 4096), bf16),
+            pltpu.SemaphoreType.DMA((2,)),
+            pltpu.SemaphoreType.DMA((2,)),
+        ],
+        compiler_params=roomy,
+        cost_estimate=pl.CostEstimate(flops=0, bytes_accessed=8 << 20, transcendentals=0),
+    )(at, w_in, w_out)
+
+
+def sort_body(place_ref, tokens, cotangent, sent):
     rows = tokens.shape[0]
     hot = (lax.broadcasted_iota(jnp.int32, (rows, rows), 0) == place_ref[...]).astype(bf16)
-
-    def step(index, carry):
-        here = block_at(index, 512)
+    for start in range(0, tokens.shape[1], 512):
+        here = pl.ds(start, 512)
         sent[:, 0, :, here] = mm(hot, tokens[:, here]).astype(bf16).reshape(8, 16, 512)
         sent[:, 1, :, here] = mm(hot, cotangent[:, here]).astype(bf16).reshape(8, 16, 512)
-        return carry
-
-    lax.fori_loop(0, tokens.shape[1] // 512, step, 0)
-    for step in range(4):
-        pltpu.make_async_copy(w_out.at[0], held.at[step], taken.at[step]).wait()
-        pltpu.make_async_copy(held.at[step], packed[step], put.at[step]).start()
-    for step in range(4):
-        pltpu.make_async_copy(held.at[step], packed[step], put.at[step]).wait()
-
-
-def sort_and_pack(at, place, tokens, cotangent, w_in, w_out):
-    shape = jax.ShapeDtypeStruct((256, 4096), bf16)
+
+
+def sort(place, tokens, cotangent):
     return pl.pallas_call(
         sort_body,
-        out_shape=(jax.ShapeDtypeStruct((8, 2, 16, 4096), bf16),) + (shape,) * 4,
-        in_specs=[smem_spec] + [vmem_spec] * 3 + [any_spec] * 2,
-        out_specs=(vmem_spec,) + (any_spec,) * 4,
-        scratch_shapes=[
-            pltpu.VMEM((4, 256, 4096), bf16),
-            pltpu.SemaphoreType.DMA((4,)),
-            pltpu.SemaphoreType.DMA((4,)),
-        ],
-        compiler_params=roomy,
-        cost_estimate=pl.CostEstimate(flops=0, bytes_accessed=20 << 20, transcendentals=0),
-    )(at, place, tokens, cotangent, w_in, w_out)
+        out_shape=jax.ShapeDtypeStruct((8, 2, 16, 4096), bf16),
+        in_specs=[vmem_spec] * 3,
+        out_specs=vmem_spec,
+        compiler_params=roomy,
+        cost_estimate=pl.CostEstimate(flops=1 << 28, bytes_accessed=4 << 20, transcendentals=0),
+    )(place, tokens, cotangent)
 
 
 def unpack_body(steps, at_ref, *refs):
@@ -270,7 +271,7 @@
 
 def down_body(
     at_ref, pre_ref, got_ref, w0, w1, w2, w3, p0, p1, p2, p3,
-    part_ref, q_ref, tall, wide, sems,
+    part, q_ref, tall, wide, part_ref, part_sem, sems,
 ):
     core = at_ref[0]
     weights = (w0, w1, w2, w3)
@@ -292,17 +293,25 @@
     for slot in range(4):
         wait_weights(slot, weights, wide, sems)
 
+    def put(here):
+        here = pl.ds(here.start, 512)
+        pltpu.make_async_copy(part_ref.at[:, here], part.at[:, here], part_sem).start()
+
     @pl.when(core == 0)
     def _():
         for index in range(8):
             here = slice(512 * index, 512 * index + 512)
             part_ref[:, here] = mm(q_ref[...], tall[here, :], NT).astype(bf16)
+            put(here)
 
     @pl.when(core == 1)
     def _():
         for index in range(8):
             here = slice(512 * index, 512 * index + 512)
             part_ref[:, here] = mm(q_ref[...], wide[:, here]).astype(bf16)
+            put(here)
+
+    pltpu.make_async_copy(part_ref, part, part_sem).wait()
 
 
 def down(at, pre_act, got, weights, packed):
@@ -313,10 +322,12 @@
             jax.ShapeDtypeStruct((512, 1024), bf16),
         ),
         in_specs=[smem_spec] + [vmem_spec] * 2 + [any_spec] * 8,
-        out_specs=(vmem_spec,) * 2,
+        out_specs=(any_spec, vmem_spec),
         scratch_shapes=[
             pltpu.VMEM((4096, 1024), bf16),
             pltpu.VMEM((1024, 4096), bf16),
+            pltpu.VMEM((512, 4096), bf16),
+            pltpu.SemaphoreType.DMA,
             pltpu.SemaphoreType.DMA((4,)),
         ],
         compiler_params=roomy,
@@ -493,16 +504,19 @@
     member = jnp.sum(same.astype(jnp.int32), axis=1)
     place = home * 8 + jnp.arange(positions, dtype=jnp.int32)[None, :] * 2 + member
     place = place.reshape(1, rows)
-    sent, *packed = sort_and_pack(
-        at, place, tokens.reshape(rows, width), cotangent.reshape(rows, width), w_in, w_out
-    )
+    packed = pack(0, at, w_in, w_out)
+    place, *packed = tie((place, *packed))
+    sent = sort(place, tokens.reshape(rows, width), cotangent.reshape(rows, width))
     hot = (place == jnp.arange(rows, dtype=jnp.int32)[:, None]).astype(bf16)
     held = exchange(sent.reshape(16, 16, width), owners).reshape(256, width)
 
     def send_weights(step, piece):
         return lax.ppermute(piece, column, weight_round(step))
 
-    weights = [send_weights(0, packed[0]), send_weights(1, packed[1])]
+    weights = [send_weights(0, packed[0])]
+    weights[0], second = tie((weights[0], packed[1]))
+    weights.append(send_weights(1, second))
+    packed += pack(2, at, w_in, w_out)
 
     planes = [(plane + d) % 4 for d in range(4)]
     mixer_e = mixer.T.reshape(8, 4, width)
@@ -524,13 +538,12 @@
         return [(s, (s + by) % 4) for s in range(4)]
 
     mix = (mm(flat_high, held) + mm(flat_low, held)).astype(bf16)
+    mix, weights[1] = tie((mix, weights[1]))
     blocks = {}
     for d in (2, 1, 3, 0):
         block = mix[64 * d : 64 * d + 64]
         blocks[d] = lax.ppermute(block, "z", shift(d)) if d else block
-    blocks[2], weights[0], weights[1], *later = tie(
-        (blocks[2], weights[0], weights[1], *packed[2:])
-    )
+    blocks[2], *later = tie((blocks[2], *packed[2:]))
     weights += [send_weights(step + 2, piece) for step, piece in enumerate(later)]
     sent = jnp.stack([blocks[d].reshape(8, 8, width) for d in range(4)], axis=1)
     sent = jnp.broadcast_to(sent[:, None], (8, 2, 4, 8, width)).reshape(16, 32, width)
@@ -564,12 +577,10 @@
     )
     grads.append(send_grads(2, later[0]))
     grad_rows = exchange(grad_rows.reshape(16, 16, half), owners)
-    grad_rows, mixer_part, grads[0], grads[1], last = tie(
-        (grad_rows, mixer_part, grads[0], grads[1], later[1])
-    )
+    grad_rows, mixer_part, grads[0] = tie((grad_rows, mixer_part, grads[0]))
     pieces = exchange(mixer_part, axes)
+    pieces, grads[1], grads[2], last = tie((pieces, grads[1], grads[2], later[1]))
     grads.append(send_grads(3, last))
-    pieces, grads[2] = tie((pieces, grads[2]))
     total = jnp.sum(pieces, axis=0, keepdims=True)
     whole = exchange(jnp.broadcast_to(total, (128, 8, 128)), axes)
     grad_mixer = whole.reshape(4, 32, 8, 128).transpose(1, 3, 0, 2).reshape(width, 32)

time: 371 us -> 349 us (0.941)
  waiting for transfers between devices: 222 us -> 197 us
    all_to_all x6, waiting for transfers between devices: 98.6 us -> 79 us  [exchange(): return lax.all_to_all(array, names, split_axis=0, concat_axis=0, tiled=True)]
    ppermute x3, waiting for transfers between devices: 5.51 us -> 19.7 us  [shards(): blocks[d] = lax.ppermute(block, 'z', shift(d)) if d else block]
    ppermute x4, waiting for transfers between devices: 40.5 us -> 27.2 us  [send_grads(): return lax.ppermute(piece, column, back_round(step))]
    ppermute x4, waiting for transfers between devices: 72.1 us -> 67 us  [send_weights(): return lax.ppermute(piece, column, weight_round(step))]
    all_to_all x6, starting transfers between devices: 46.9 us -> 43.1 us  [exchange(): return lax.all_to_all(array, names, split_axis=0, concat_axis=0, tiled=True)]
    unnamed x19 -> x27, local copies, waits for them, and re-layouts: 4.97 us -> 7.69 us
  transfers between devices with their start and end apart: 21 -> 21, of which waited for: 16 -> 18; matrix products, arithmetic and copies ran while one was open for 3% -> 3% of each run, Pallas kernels for 6% -> 7%
where the time goes in v5:
time: 349 us; the launch traced here: 347 us
  waiting for transfers between devices  197 us (56%)
  starting transfers between devices  72.9 us (21%)
  Pallas kernels  51.4 us (15%)
  local copies, waits for them, and re-layouts  15.5 us (4%)
  other arithmetic  4.54 us (1%)
  matrix products  3.79 us (1%)
    all_to_all x6, waiting for transfers between devices, exchange(): return lax.all_to_all(array, names, split_axis=0, concat_axis=0, tiled=True)  79 us
    ppermute x4, waiting for transfers between devices, send_weights(): return lax.ppermute(piece, column, weight_round(step))  67 us
    all_to_all x6, starting transfers between devices, exchange(): return lax.all_to_all(array, names, split_axis=0, concat_axis=0, tiled=True)  43.1 us
    ppermute x4, waiting for transfers between devices, send_grads(): return lax.ppermute(piece, column, back_round(step))  27.2 us
    ppermute x3, waiting for transfers between devices, shards(): blocks[d] = lax.ppermute(block, 'z', shift(d)) if d else block  19.7 us
    pallas_call x1, Pallas kernels, up(): pl.pallas_call(up_body, out_shape=(jax.ShapeDtypeStruct((512, 1024), f32)...  9.76 us
    ppermute x4, starting transfers between devices, send_weights(): return lax.ppermute(piece, column, weight_round(step))  9.66 us
    pallas_call x1, Pallas kernels, down(): pl.pallas_call(down_body, out_shape=(jax.ShapeDtypeStruct((512, 4096), bf...  9.43 us
  transfers between devices with their start and end apart: 21, of which 18 were waited for; matrix products, arithmetic and copies ran while one was open for 3% of the time, Pallas kernels for 7%

profile of v5, /device:TPU:1, one launch (start us, length us, event | category | flops | bytes accessed | tf_op | source)
XLA Modules:
  0.0 346.5 jit_solution(7536828228963162615)
XLA Ops:
  7.7 5.1 %collective-permute-start.1 = (bf16[256,4096]{1,0:T(8,128)(2,1)}, bf16[256,4096]{1,0:T(8,128)(2,1)}, u32[]{:S(2)}, u32[]{:S(2)}) collective-permute-start(bf16[256,4096]{1,0:T(8,128)(2,1)} %get-tuple-element.48.p0), channel_id=1, source_target_pairs={{0,2},{2,0},{4,10},{6,8},{8,6},{10,4},{12,14},{14,12},{1,3},{3,1},... | collective-permute-start | bytes 6291464 | tf_op jit(solution)/shard_map/ppermute | solution.py:514
  15.4 7.2 %all-to-all-start = ((bf16[16,16,4096]{2,1,0:T(8,128)(2,1)}), bf16[16,16,4096]{2,1,0:T(8,128)(2,1)S(1)}, u32[]{:S(2)}, u32[]{:S(2)}) async-start(bf16[16,16,4096]{2,1,0:T(8,128)(2,1)} %bitcast.66), calls=%async_computation | async-start | bytes 4194304 | tf_op jit(solution)/shard_map/all_to_all | solution.py:41
  23.5 13.5 %collective-permute-done.1.w0 = bf16[256,4096]{1,0:T(8,128)(2,1)} collective-permute-done((bf16[256,4096]{1,0:T(8,128)(2,1)}, bf16[256,4096]{1,0:T(8,128)(2,1)}, u32[]{:S(2)}, u32[]{:S(2)}) %collective-permute-start.1) | collective-permute-done | bytes 2097184 | tf_op jit(solution)/shard_map/ppermute | solution.py:514
  37.9 13.3 %all-to-all-done = bf16[16,16,4096]{2,1,0:T(8,128)(2,1)S(1)} async-done(((bf16[16,16,4096]{2,1,0:T(8,128)(2,1)}), bf16[16,16,4096]{2,1,0:T(8,128)(2,1)S(1)}, u32[]{:S(2)}, u32[]{:S(2)}) %all-to-all-start) | async-done | bytes 2097184 | tf_op jit(solution)/shard_map/all_to_all | solution.py:41
  55.3 7.8 %collective-permute-done.2.w1 = bf16[256,4096]{1,0:T(8,128)(2,1)} collective-permute-done((bf16[256,4096]{1,0:T(8,128)(2,1)}, bf16[256,4096]{1,0:T(8,128)(2,1)}, u32[]{:S(2)}, u32[]{:S(2)}) %collective-permute-start.2) | collective-permute-done | bytes 2097184 | tf_op jit(solution)/shard_map/ppermute | solution.py:514
  70.3 6.6 %collective-permute-done.4 = bf16[64,4096]{1,0:T(8,128)(2,1)S(1)} collective-permute-done((bf16[64,4096]{1,0:T(8,128)(2,1)S(1)}, bf16[64,4096]{1,0:T(8,128)(2,1)S(1)}, u32[]{:S(2)}, u32[]{:S(2)}) %collective-permute-start.4) | collective-permute-done | bytes 524320 | tf_op jit(solution)/shard_map/ppermute | solution.py:545
  76.9 13.1 %collective-permute-done.3 = bf16[64,4096]{1,0:T(8,128)(2,1)S(1)} collective-permute-done((bf16[64,4096]{1,0:T(8,128)(2,1)S(1)}, bf16[64,4096]{1,0:T(8,128)(2,1)S(1)}, u32[]{:S(2)}, u32[]{:S(2)}) %collective-permute-start.3) | collective-permute-done | bytes 524320 | tf_op jit(solution)/shard_map/ppermute | solution.py:545
  93.0 6.8 %all-to-all-start.1 = ((bf16[16,32,4096]{2,1,0:T(8,128)(2,1)}), bf16[16,32,4096]{2,1,0:T(8,128)(2,1)}, u32[]{:S(2)}, u32[]{:S(2)}) async-start(bf16[16,32,4096]{2,1,0:T(8,128)(2,1)} %bitcast.73), calls=%async_computation.1 | async-start | bytes 8388608 | tf_op jit(solution)/shard_map/all_to_all | solution.py:41
  103.7 25.6 %collective-permute-done.6.w2 = bf16[256,4096]{1,0:T(8,128)(2,1)} collective-permute-done((bf16[256,4096]{1,0:T(8,128)(2,1)}, bf16[256,4096]{1,0:T(8,128)(2,1)}, u32[]{:S(2)}, u32[]{:S(2)}) %collective-permute-start.6) | collective-permute-done | bytes 2097184 | tf_op jit(solution)/shard_map/ppermute | solution.py:514
  129.3 20.0 %collective-permute-done.7.w3 = bf16[256,4096]{1,0:T(8,128)(2,1)} collective-permute-done((bf16[256,4096]{1,0:T(8,128)(2,1)}, bf16[256,4096]{1,0:T(8,128)(2,1)}, u32[]{:S(2)}, u32[]{:S(2)}) %collective-permute-start.7) | collective-permute-done | bytes 2097184 | tf_op jit(solution)/shard_map/ppermute | solution.py:514
  149.3 7.6 %all-to-all-done.1 = bf16[16,32,4096]{2,1,0:T(8,128)(2,1)} async-done(((bf16[16,32,4096]{2,1,0:T(8,128)(2,1)}), bf16[16,32,4096]{2,1,0:T(8,128)(2,1)}, u32[]{:S(2)}, u32[]{:S(2)}) %all-to-all-start.1) | async-done | bytes 4194336 | tf_op jit(solution)/shard_map/all_to_all | solution.py:41
  157.0 9.8 %shard_map.96 = (f32[512,1024]{1,0:T(8,128)S(1)}, bf16[512,1024]{1,0:T(8,128)(2,1)S(1)}) custom-call(s32[7]{0:T(128)S(1)} %stack.64.at_ref, bf16[8,2,4,8,4096]{4,3,2,1,0:T(8,128)(2,1)} %bitcast.22.rows_in, bf16[256,4096]{1,0:T(8,128)(2,1)} %collective-permute-done.1.w0, bf16[256,4096]{1,0:T(8,128)(2,1)} %collective-permute-done.2.w1, ...), custom_call_target="tpu_custom_call" | custom-call | flops 4294967296 | bytes 15728640 | tf_op jit(solution)/shard_map/pallas_call | solution.py:250
  171.6 9.4 %shard_map.97 = (bf16[512,4096]{1,0:T(8,128)(2,1)}, bf16[512,1024]{1,0:T(8,128)(2,1)S(1)}) custom-call(s32[7]{0:T(128)S(1)} %stack.64.at_ref, f32[512,1024]{1,0:T(8,128)S(1)} %get-tuple-element.59.pre_ref, bf16[512,1024]{1,0:T(8,128)(2,1)S(1)} %collective-permute-done.8.got_ref, bf16[256,4096]{1,0:T(8,128)(2,1)} %collective-permute-done.1.w0, ...), custom_call_target="tpu_custom_call" | custom-call | flops 4294967296 | bytes 16777216 | tf_op jit(solution)/shard_map/pallas_call | solution.py:318
  181.0 6.0 %all-to-all-start.2 = ((bf16[64,8,4096]{2,1,0:T(8,128)(2,1)}), bf16[64,8,4096]{2,1,0:T(8,128)(2,1)}, u32[]{:S(2)}, u32[]{:S(2)}) async-start(bf16[64,8,4096]{2,1,0:T(8,128)(2,1)} %bitcast.74), calls=%async_computation.2 | async-start | bytes 8388608 | tf_op jit(solution)/shard_map/all_to_all | solution.py:41
  187.0 9.4 %shard_map.98 = (bf16[256,4096]{1,0:T(8,128)(2,1)}, bf16[256,4096]{1,0:T(8,128)(2,1)S(1)}, bf16[256,4096]{1,0:T(8,128)(2,1)}, bf16[256,4096]{1,0:T(8,128)(2,1)}) custom-call(s32[7]{0:T(128)S(1)} %stack.64.at_ref, bf16[8,2,4,8,4096]{4,3,2,1,0:T(8,128)(2,1)} %bitcast.22.rows_in, bf16[512,1024]{1,0:T(8,128)(2,1)S(1)} %get-tuple-element.62.q_ref), custom_call_target="tpu_custom_call" | custom-call | flops 4294967296 | bytes 13631488 | tf_op jit(solution)/shard_map/pallas_call | solution.py:384
  201.4 36.4 %all-to-all-done.2 = bf16[64,8,4096]{2,1,0:T(8,128)(2,1)} async-done(((bf16[64,8,4096]{2,1,0:T(8,128)(2,1)}), bf16[64,8,4096]{2,1,0:T(8,128)(2,1)}, u32[]{:S(2)}, u32[]{:S(2)}) %all-to-all-start.2) | async-done | bytes 4194336 | tf_op jit(solution)/shard_map/all_to_all | solution.py:41
  256.4 5.2 %all-to-all-start.3 = ((bf16[16,16,2048]{2,1,0:T(8,128)(2,1)}), bf16[16,16,2048]{2,1,0:T(8,128)(2,1)S(1)}, u32[]{:S(2)}, u32[]{:S(2)}) async-start(bf16[16,16,2048]{2,1,0:T(8,128)(2,1)} %bitcast.70), calls=%async_computation.3 | async-start | bytes 2097152 | tf_op jit(solution)/shard_map/all_to_all | solution.py:41
  266.3 12.7 %all-to-all-done.3 = bf16[16,16,2048]{2,1,0:T(8,128)(2,1)S(1)} async-done(((bf16[16,16,2048]{2,1,0:T(8,128)(2,1)}), bf16[16,16,2048]{2,1,0:T(8,128)(2,1)S(1)}, u32[]{:S(2)}, u32[]{:S(2)}) %all-to-all-start.3) | async-done | bytes 1048608 | tf_op jit(solution)/shard_map/all_to_all | solution.py:41
  279.0 6.7 %all-to-all-start.4 = ((f32[128,8,128]{2,1,0:T(8,128)}), f32[128,8,128]{2,1,0:T(8,128)}, u32[]{:S(2)}, u32[]{:S(2)}) async-start(f32[128,8,128]{2,1,0:T(8,128)} %copy-done.9), calls=%async_computation.4 | async-start | bytes 1048576 | tf_op jit(solution)/shard_map/all_to_all | solution.py:41
  285.7 8.7 %collective-permute-done.12.refs_1_ = bf16[256,4096]{1,0:T(8,128)(2,1)} collective-permute-done((bf16[256,4096]{1,0:T(8,128)(2,1)}, bf16[256,4096]{1,0:T(8,128)(2,1)}, u32[]{:S(2)}, u32[]{:S(2)}) %collective-permute-start.12) | collective-permute-done | bytes 2097184 | tf_op jit(solution)/shard_map/ppermute | solution.py:559
  294.3 13.9 %collective-permute-done.13.refs_2_ = bf16[256,4096]{1,0:T(8,128)(2,1)} collective-permute-done((bf16[256,4096]{1,0:T(8,128)(2,1)}, bf16[256,4096]{1,0:T(8,128)(2,1)}, u32[]{:S(2)}, u32[]{:S(2)}) %collective-permute-start.13) | collective-permute-done | bytes 2097184 | tf_op jit(solution)/shard_map/ppermute | solution.py:559
  313.2 11.3 %all-to-all-start.5 = ((f32[128,8,128]{2,1,0:T(8,128)}), f32[128,8,128]{2,1,0:T(8,128)}, u32[]{:S(2)}, u32[]{:S(2)}) async-start(f32[128,8,128]{2,1,0:T(8,128)} %broadcast_in_dim.5), calls=%async_computation.5 | async-start | bytes 1048576 | tf_op jit(solution)/shard_map/all_to_all | solution.py:41
  327.1 5.3 %shard_map.101 = (bf16[2,4096,256]{2,1,0:T(8,128)(2,1)}, bf16[2,256,4096]{2,1,0:T(8,128)(2,1)}) custom-call(s32[7]{0:T(128)S(1)} %stack.64.at_ref, bf16[256,4096]{1,0:T(8,128)(2,1)} %collective-permute-done.11.refs_0_, bf16[256,4096]{1,0:T(8,128)(2,1)} %collective-permute-done.12.refs_1_, bf16[256,4096]{1,0:T(8,128)(2,1)} %collective-permute-done.13.refs_2_, ...), custom_call_target="tpu_custom_call" | custom-call | bytes 12582912 | tf_op jit(solution)/shard_map/pallas_call | solution.py:156
  332.5 8.7 %all-to-all-done.5 = f32[128,8,128]{2,1,0:T(8,128)} async-done(((f32[128,8,128]{2,1,0:T(8,128)}), f32[128,8,128]{2,1,0:T(8,128)}, u32[]{:S(2)}, u32[]{:S(2)}) %all-to-all-start.5) | async-done | bytes 524320 | tf_op jit(solution)/shard_map/all_to_all | solution.py:41
  (97 shorter events, 75.2 us)
Async XLA Ops:
  7.7 29.4 %collective-permute-start.1 = (bf16[256,4096]{1,0:T(8,128)(2,1)}, bf16[256,4096]{1,0:T(8,128)(2,1)}, u32[]{:S(2)}, u32[]{:S(2)}) collective-permute-start(bf16[256,4096]{1,0:T(8,128)(2,1)} %get-tuple-element.48.p0), channel_id=1, source_target_pairs={{0,2},{2,0},{4,10},{6,8},{8,6},{10,4},{12,14},{14,12},{1,3},{3,1},... | collective-permute-start | bytes 6291464 | tf_op jit(solution)/shard_map/ppermute | solution.py:514
  15.4 35.8 %all-to-all-start = ((bf16[16,16,4096]{2,1,0:T(8,128)(2,1)}), bf16[16,16,4096]{2,1,0:T(8,128)(2,1)S(1)}, u32[]{:S(2)}, u32[]{:S(2)}) async-start(bf16[16,16,4096]{2,1,0:T(8,128)(2,1)} %bitcast.66), calls=%async_computation | async-start | bytes 4194304 | tf_op jit(solution)/shard_map/all_to_all | solution.py:41
  37.1 26.1 %collective-permute-start.2 = (bf16[256,4096]{1,0:T(8,128)(2,1)}, bf16[256,4096]{1,0:T(8,128)(2,1)}, u32[]{:S(2)}, u32[]{:S(2)}) collective-permute-start(bf16[256,4096]{1,0:T(8,128)(2,1)} %copy-done.2), channel_id=1, source_target_pairs={{0,10},{2,8},{4,2},{6,0},{8,14},{10,12},{12,6},{14,4},{1,11},{3,9}... | collective-permute-start | bytes 6291464 | tf_op jit(solution)/shard_map/ppermute | solution.py:514
  51.2 186.7 %copy-start = (bf16[16,16,4096]{2,1,0:T(8,128)(2,1)}, bf16[16,16,4096]{2,1,0:T(8,128)(2,1)S(1)}, u32[]{:S(2)}) copy-start(bf16[16,16,4096]{2,1,0:T(8,128)(2,1)S(1)} %all-to-all-done) | copy-start | bytes 6291460
  51.9 1.6 collective-permute-start
  63.3 13.6 %collective-permute-start.4 = (bf16[64,4096]{1,0:T(8,128)(2,1)S(1)}, bf16[64,4096]{1,0:T(8,128)(2,1)S(1)}, u32[]{:S(2)}, u32[]{:S(2)}) collective-permute-start(bf16[64,4096]{1,0:T(8,128)(2,1)S(1)} %get-tuple-element.88), channel_id=1, source_target_pairs={{0,4},{2,6},{4,0},{6,2},{1,5},{3,7},{5,1},{7,3},{8,12},{10,14},{12... | collective-permute-start | bytes 1572872 | tf_op jit(solution)/shard_map/ppermute | solution.py:545
  64.6 25.4 %collective-permute-start.3 = (bf16[64,4096]{1,0:T(8,128)(2,1)S(1)}, bf16[64,4096]{1,0:T(8,128)(2,1)S(1)}, u32[]{:S(2)}, u32[]{:S(2)}) collective-permute-start(bf16[64,4096]{1,0:T(8,128)(2,1)S(1)} %get-tuple-element.89), channel_id=1, source_target_pairs={{0,2},{2,4},{4,6},{6,0},{1,3},{3,5},{5,7},{7,1},{8,10},{10,12},{12... | collective-permute-start | bytes 1572872 | tf_op jit(solution)/shard_map/ppermute | solution.py:545
  65.0 25.0 %collective-permute-start.5 = (bf16[64,4096]{1,0:T(8,128)(2,1)S(1)}, bf16[64,4096]{1,0:T(8,128)(2,1)S(1)}, u32[]{:S(2)}, u32[]{:S(2)}) collective-permute-start(bf16[64,4096]{1,0:T(8,128)(2,1)S(1)} %get-tuple-element.87), channel_id=1, source_target_pairs={{0,6},{2,0},{4,2},{6,4},{1,7},{3,1},{5,3},{7,5},{8,14},{10,8},{12,... | collective-permute-start | bytes 1572872 | tf_op jit(solution)/shard_map/ppermute | solution.py:545
  70.3 19.9 %copy-start.3 = (bf16[256,4096]{1,0:T(8,128)(2,1)}, bf16[256,4096]{1,0:T(8,128)(2,1)S(1)}, u32[]{:S(2)}) copy-start(bf16[256,4096]{1,0:T(8,128)(2,1)S(1)} %get-tuple-element.57.p2) | copy-start | bytes 6291460
  93.0 63.9 %all-to-all-start.1 = ((bf16[16,32,4096]{2,1,0:T(8,128)(2,1)}), bf16[16,32,4096]{2,1,0:T(8,128)(2,1)}, u32[]{:S(2)}, u32[]{:S(2)}) async-start(bf16[16,32,4096]{2,1,0:T(8,128)(2,1)} %bitcast.73), calls=%async_computation.1 | async-start | bytes 8388608 | tf_op jit(solution)/shard_map/all_to_all | solution.py:41
  99.9 29.5 %collective-permute-start.6 = (bf16[256,4096]{1,0:T(8,128)(2,1)}, bf16[256,4096]{1,0:T(8,128)(2,1)}, u32[]{:S(2)}, u32[]{:S(2)}) collective-permute-start(bf16[256,4096]{1,0:T(8,128)(2,1)} %copy-done.3), channel_id=1, source_target_pairs={{4,8},{6,10},{8,4},{10,6},{5,9},{7,11},{9,5},{11,7},{20,24},{22,26... | collective-permute-start | bytes 6291464 | tf_op jit(solution)/shard_map/ppermute | solution.py:514
  103.6 45.7 %collective-permute-start.7 = (bf16[256,4096]{1,0:T(8,128)(2,1)}, bf16[256,4096]{1,0:T(8,128)(2,1)}, u32[]{:S(2)}, u32[]{:S(2)}) collective-permute-start(bf16[256,4096]{1,0:T(8,128)(2,1)} %copy-done.4), channel_id=1, source_target_pairs={{0,8},{2,10},{4,0},{6,2},{8,12},{10,14},{12,4},{14,6},{1,9},{3,11}... | collective-permute-start | bytes 6291464 | tf_op jit(solution)/shard_map/ppermute | solution.py:514
  166.7 4.9 %collective-permute-start.8 = (bf16[512,1024]{1,0:T(8,128)(2,1)S(1)}, bf16[512,1024]{1,0:T(8,128)(2,1)S(1)}, u32[]{:S(2)}, u32[]{:S(2)}) collective-permute-start(bf16[512,1024]{1,0:T(8,128)(2,1)S(1)} %get-tuple-element.60), channel_id=1, source_target_pairs={{0,8},{8,0},{1,9},{9,1},{2,10},{10,2},{3,11},{11,3},{4,12},{12,4},... | collective-permute-start | bytes 3145736 | tf_op jit(solution)/shard_map/ppermute | solution.py:553
  181.0 56.8 %all-to-all-start.2 = ((bf16[64,8,4096]{2,1,0:T(8,128)(2,1)}), bf16[64,8,4096]{2,1,0:T(8,128)(2,1)}, u32[]{:S(2)}, u32[]{:S(2)}) async-start(bf16[64,8,4096]{2,1,0:T(8,128)(2,1)} %bitcast.74), calls=%async_computation.2 | async-start | bytes 8388608 | tf_op jit(solution)/shard_map/all_to_all | solution.py:41
  197.8 68.6 %collective-permute-start.11 = (bf16[256,4096]{1,0:T(8,128)(2,1)}, bf16[256,4096]{1,0:T(8,128)(2,1)}, u32[]{:S(2)}, u32[]{:S(2)}) collective-permute-start(bf16[256,4096]{1,0:T(8,128)(2,1)} %get-tuple-element.71.refs_3_), channel_id=1, source_target_pairs={{2,0},{0,2},{10,4},{8,6},{6,8},{4,10},{14,12},{12,14},{3,1},{1,3},... | collective-permute-start | bytes 6291464 | tf_op jit(solution)/shard_map/ppermute | solution.py:559
  241.8 10.0 %collective-permute-start.10 = (bf16[256,2048]{1,0:T(8,128)(2,1)}, bf16[256,2048]{1,0:T(8,128)(2,1)S(1)}, u32[]{:S(2)}, u32[]{:S(2)}) collective-permute-start(bf16[256,2048]{1,0:T(8,128)(2,1)} %get-tuple-element.68), channel_id=1, source_target_pairs={{0,8},{8,0},{1,9},{9,1},{2,10},{10,2},{3,11},{11,3},{4,12},{12,4},... | collective-permute-start | bytes 3145736 | tf_op jit(solution)/shard_map/ppermute | solution.py:573
  245.3 49.1 %collective-permute-start.12 = (bf16[256,4096]{1,0:T(8,128)(2,1)}, bf16[256,4096]{1,0:T(8,128)(2,1)}, u32[]{:S(2)}, u32[]{:S(2)}) collective-permute-start(bf16[256,4096]{1,0:T(8,128)(2,1)} %copy-done.6), channel_id=1, source_target_pairs={{10,0},{8,2},{2,4},{0,6},{14,8},{12,10},{6,12},{4,14},{11,1},{9,3}... | collective-permute-start | bytes 6291464 | tf_op jit(solution)/shard_map/ppermute | solution.py:559
  246.5 61.8 %collective-permute-start.13 = (bf16[256,4096]{1,0:T(8,128)(2,1)}, bf16[256,4096]{1,0:T(8,128)(2,1)}, u32[]{:S(2)}, u32[]{:S(2)}) collective-permute-start(bf16[256,4096]{1,0:T(8,128)(2,1)} %get-tuple-element.75.refs_5_), channel_id=1, source_target_pairs={{8,4},{10,6},{4,8},{6,10},{9,5},{11,7},{5,9},{7,11},{24,20},{26,22... | collective-permute-start | bytes 6291464 | tf_op jit(solution)/shard_map/ppermute | solution.py:559
  250.5 1.3 collective-permute-start.9
  256.4 52.1 %copy-start.5 = (bf16[256,4096]{1,0:T(8,128)(2,1)S(1)}, bf16[256,4096]{1,0:T(8,128)(2,1)}, u32[]{:S(2)}) copy-start(bf16[256,4096]{1,0:T(8,128)(2,1)} %get-tuple-element.78.refs_1_) | copy-start | bytes 6291460
  256.4 22.6 %all-to-all-start.3 = ((bf16[16,16,2048]{2,1,0:T(8,128)(2,1)}), bf16[16,16,2048]{2,1,0:T(8,128)(2,1)S(1)}, u32[]{:S(2)}, u32[]{:S(2)}) async-start(bf16[16,16,2048]{2,1,0:T(8,128)(2,1)} %bitcast.70), calls=%async_computation.3 | async-start | bytes 2097152 | tf_op jit(solution)/shard_map/all_to_all | solution.py:41
  279.0 29.5 %all-to-all-start.4 = ((f32[128,8,128]{2,1,0:T(8,128)}), f32[128,8,128]{2,1,0:T(8,128)}, u32[]{:S(2)}, u32[]{:S(2)}) async-start(f32[128,8,128]{2,1,0:T(8,128)} %copy-done.9), calls=%async_computation.4 | async-start | bytes 1048576 | tf_op jit(solution)/shard_map/all_to_all | solution.py:41
  308.6 32.6 %collective-permute-start.14 = (bf16[256,4096]{1,0:T(8,128)(2,1)S(1)}, bf16[256,4096]{1,0:T(8,128)(2,1)}, u32[]{:S(2)}, u32[]{:S(2)}) collective-permute-start(bf16[256,4096]{1,0:T(8,128)(2,1)S(1)} %copy-done.5), channel_id=1, source_target_pairs={{8,0},{10,2},{0,4},{2,6},{12,8},{14,10},{4,12},{6,14},{9,1},{11,3}... | collective-permute-start | bytes 6291464 | tf_op jit(solution)/shard_map/ppermute | solution.py:559
  313.2 28.0 %all-to-all-start.5 = ((f32[128,8,128]{2,1,0:T(8,128)}), f32[128,8,128]{2,1,0:T(8,128)}, u32[]{:S(2)}, u32[]{:S(2)}) async-start(f32[128,8,128]{2,1,0:T(8,128)} %broadcast_in_dim.5), calls=%async_computation.5 | async-start | bytes 1048576 | tf_op jit(solution)/shard_map/all_to_all | solution.py:41
  (10 other events, 62.9 us)

commit v6 on v5

--- a/solution.py
+++ b/solution.py
@@ -77,35 +77,41 @@
     ]
 
 
-def pack_body(first, at_ref, w_in, w_out, p0, p1, held, taken, put):
-    packed = (p0, p1)
-    for slot in range(2):
+def pack_body(steps, at_ref, w_in, w_out, *refs):
+    count = len(steps)
+    packed, (held, taken, put) = refs[:count], refs[count:]
+    for slot, step in enumerate(steps):
         for piece in range(4):
-            @pl.when(at_ref[2 + first + slot] == piece)
+            @pl.when(at_ref[2 + step] == piece)
             def _():
                 for source, target in piece_copies(piece, w_in, w_out, held.at[slot]):
                     pltpu.make_async_copy(source, target, taken.at[slot]).start()
-    for slot in range(2):
+    for slot in range(count):
         pltpu.make_async_copy(w_out.at[0], held.at[slot], taken.at[slot]).wait()
         pltpu.make_async_copy(held.at[slot], packed[slot], put.at[slot]).start()
-    for slot in range(2):
+    for slot in range(count):
         pltpu.make_async_copy(held.at[slot], packed[slot], put.at[slot]).wait()
 
 
-def pack(first, at, w_in, w_out):
-    return pl.pallas_call(
-        functools.partial(pack_body, first),
-        out_shape=(jax.ShapeDtypeStruct((256, 4096), bf16),) * 2,
-        in_specs=[smem_spec] + [any_spec] * 2,
-        out_specs=(any_spec,) * 2,
-        scratch_shapes=[
-            pltpu.VMEM((2, 256, 4096), bf16),
-            pltpu.SemaphoreType.DMA((2,)),
-            pltpu.SemaphoreType.DMA((2,)),
-        ],
-        compiler_params=roomy,
-        cost_estimate=pl.CostEstimate(flops=0, bytes_accessed=8 << 20, transcendentals=0),
-    )(at, w_in, w_out)
+def pack(steps, at, w_in, w_out):
+    count = len(steps)
+    return list(
+        pl.pallas_call(
+            functools.partial(pack_body, steps),
+            out_shape=(jax.ShapeDtypeStruct((256, 4096), bf16),) * count,
+            in_specs=[smem_spec] + [any_spec] * 2,
+            out_specs=(any_spec,) * count,
+            scratch_shapes=[
+                pltpu.VMEM((count, 256, 4096), bf16),
+                pltpu.SemaphoreType.DMA((count,)),
+                pltpu.SemaphoreType.DMA((count,)),
+            ],
+            compiler_params=roomy,
+            cost_estimate=pl.CostEstimate(
+                flops=0, bytes_accessed=count << 22, transcendentals=0
+            ),
+        )(at, w_in, w_out)
+    )
 
 
 def sort_body(place_ref, tokens, cotangent, sent):
@@ -504,7 +510,7 @@
     member = jnp.sum(same.astype(jnp.int32), axis=1)
     place = home * 8 + jnp.arange(positions, dtype=jnp.int32)[None, :] * 2 + member
     place = place.reshape(1, rows)
-    packed = pack(0, at, w_in, w_out)
+    packed = pack((0,), at, w_in, w_out)
     place, *packed = tie((place, *packed))
     sent = sort(place, tokens.reshape(rows, width), cotangent.reshape(rows, width))
     hot = (place == jnp.arange(rows, dtype=jnp.int32)[:, None]).astype(bf16)
@@ -514,9 +520,10 @@
         return lax.ppermute(piece, column, weight_round(step))
 
     weights = [send_weights(0, packed[0])]
+    packed += pack((1,), at, w_in, w_out)
     weights[0], second = tie((weights[0], packed[1]))
     weights.append(send_weights(1, second))
-    packed += pack(2, at, w_in, w_out)
+    packed += pack((2, 3), at, w_in, w_out)
 
     planes = [(plane + d) % 4 for d in range(4)]
     mixer_e = mixer.T.reshape(8, 4, width)
@@ -583,7 +590,6 @@
     grads.append(send_grads(3, last))
     total = jnp.sum(pieces, axis=0, keepdims=True)
     whole = exchange(jnp.broadcast_to(total, (128, 8, 128)), axes)
-    grad_mixer = whole.reshape(4, 32, 8, 128).transpose(1, 3, 0, 2).reshape(width, 32)
 
     most = unpack((0, 1, 2), at, grads, made)
     grad_in, grad_out = unpack((3,), at, grads, made, most)
@@ -592,6 +598,8 @@
         [mm(hot, grad_rows[:, 1 - side].reshape(rows, half), TN).astype(bf16) for side in range(2)],
         axis=1,
     ).reshape(seqs, positions, width)
+    whole, grad_in, grad_out = tie((whole, grad_in, grad_out))
+    grad_mixer = whole.reshape(4, 32, 8, 128).transpose(1, 3, 0, 2).reshape(width, 32)
     return (grad_tokens, grad_mixer, grad_in, grad_out)
 
 

time: 349 us -> 348 us (level)
  waiting for transfers between devices: 197 us -> 193 us
  Pallas kernels: 51.4 us -> 54.9 us
    all_to_all x6, waiting for transfers between devices: 79 us -> 70.4 us  [exchange(): return lax.all_to_all(array, names, split_axis=0, concat_axis=0, tiled=True)]
    ppermute x4, waiting for transfers between devices: 27.2 us -> 35.5 us  [send_grads(): return lax.ppermute(piece, column, back_round(step))]
    ppermute x4, waiting for transfers between devices: 67 us -> 63.4 us  [send_weights(): return lax.ppermute(piece, column, weight_round(step))]
    pallas_call x2 -> x3, Pallas kernels: 6.58 us -> 10.1 us  [pack(): pl.pallas_call(functools.partial(pack_body, steps), out_shape=(jax.ShapeD...]
    unnamed x27 -> x25, local copies, waits for them, and re-layouts: 7.69 us -> 6.29 us
  transfers between devices with their start and end apart: 21 -> 21, of which waited for: 18 -> 18; matrix products, arithmetic and copies ran while one was open for 3% -> 3% of each run, Pallas kernels for 7% -> 9%
where the time goes in v6:
time: 348 us; the launch traced here: 345 us
  waiting for transfers between devices  193 us (55%)
  starting transfers between devices  73 us (21%)
  Pallas kernels  54.9 us (16%)
  local copies, waits for them, and re-layouts  14.1 us (4%)
  other arithmetic  4.54 us (1%)
  matrix products  3.79 us (1%)
    all_to_all x6, waiting for transfers between devices, exchange(): return lax.all_to_all(array, names, split_axis=0, concat_axis=0, tiled=True)  70.4 us
    ppermute x4, waiting for transfers between devices, send_weights(): return lax.ppermute(piece, column, weight_round(step))  63.4 us
    all_to_all x6, starting transfers between devices, exchange(): return lax.all_to_all(array, names, split_axis=0, concat_axis=0, tiled=True)  43.1 us
    ppermute x4, waiting for transfers between devices, send_grads(): return lax.ppermute(piece, column, back_round(step))  35.5 us
    ppermute x3, waiting for transfers between devices, shards(): blocks[d] = lax.ppermute(block, 'z', shift(d)) if d else block  19.7 us
    pallas_call x3, Pallas kernels, pack(): pl.pallas_call(functools.partial(pack_body, steps), out_shape=(jax.ShapeD...  10.1 us
    pallas_call x1, Pallas kernels, up(): pl.pallas_call(up_body, out_shape=(jax.ShapeDtypeStruct((512, 1024), f32)...  9.74 us
    ppermute x4, starting transfers between devices, send_weights(): return lax.ppermute(piece, column, weight_round(step))  9.73 us
  transfers between devices with their start and end apart: 21, of which 18 were waited for; matrix products, arithmetic and copies ran while one was open for 3% of the time, Pallas kernels for 9%

profile of v6, /device:TPU:1, one launch (start us, length us, event | category | flops | bytes accessed | tf_op | source)
XLA Modules:
  0.0 344.7 jit_solution(14350941424477568630)
XLA Ops:
  6.3 5.2 %collective-permute-start.1 = (bf16[256,4096]{1,0:T(8,128)(2,1)}, bf16[256,4096]{1,0:T(8,128)(2,1)}, u32[]{:S(2)}, u32[]{:S(2)}) collective-permute-start(bf16[256,4096]{1,0:T(8,128)(2,1)} %shard_map.93.p0), channel_id=1, source_target_pairs={{0,2},{2,0},{4,10},{6,8},{8,6},{10,4},{12,14},{14,12},{1,3},{3,1},... | collective-permute-start | bytes 6291464 | tf_op jit(solution)/shard_map/ppermute | solution.py:520
  14.1 7.2 %all-to-all-start = ((bf16[16,16,4096]{2,1,0:T(8,128)(2,1)}), bf16[16,16,4096]{2,1,0:T(8,128)(2,1)S(1)}, u32[]{:S(2)}, u32[]{:S(2)}) async-start(bf16[16,16,4096]{2,1,0:T(8,128)(2,1)} %bitcast.66), calls=%async_computation | async-start | bytes 4194304 | tf_op jit(solution)/shard_map/all_to_all | solution.py:41
  25.8 9.9 %collective-permute-done.1.w0 = bf16[256,4096]{1,0:T(8,128)(2,1)} collective-permute-done((bf16[256,4096]{1,0:T(8,128)(2,1)}, bf16[256,4096]{1,0:T(8,128)(2,1)}, u32[]{:S(2)}, u32[]{:S(2)}) %collective-permute-start.1) | collective-permute-done | bytes 2097184 | tf_op jit(solution)/shard_map/ppermute | solution.py:520
  36.6 13.3 %all-to-all-done = bf16[16,16,4096]{2,1,0:T(8,128)(2,1)S(1)} async-done(((bf16[16,16,4096]{2,1,0:T(8,128)(2,1)}), bf16[16,16,4096]{2,1,0:T(8,128)(2,1)S(1)}, u32[]{:S(2)}, u32[]{:S(2)}) %all-to-all-start) | async-done | bytes 2097184 | tf_op jit(solution)/shard_map/all_to_all | solution.py:41
  54.0 7.8 %collective-permute-done.2.w1 = bf16[256,4096]{1,0:T(8,128)(2,1)} collective-permute-done((bf16[256,4096]{1,0:T(8,128)(2,1)}, bf16[256,4096]{1,0:T(8,128)(2,1)}, u32[]{:S(2)}, u32[]{:S(2)}) %collective-permute-start.2) | collective-permute-done | bytes 2097184 | tf_op jit(solution)/shard_map/ppermute | solution.py:520
  69.0 6.6 %collective-permute-done.4 = bf16[64,4096]{1,0:T(8,128)(2,1)S(1)} collective-permute-done((bf16[64,4096]{1,0:T(8,128)(2,1)S(1)}, bf16[64,4096]{1,0:T(8,128)(2,1)S(1)}, u32[]{:S(2)}, u32[]{:S(2)}) %collective-permute-start.4) | collective-permute-done | bytes 524320 | tf_op jit(solution)/shard_map/ppermute | solution.py:552
  75.6 13.1 %collective-permute-done.3 = bf16[64,4096]{1,0:T(8,128)(2,1)S(1)} collective-permute-done((bf16[64,4096]{1,0:T(8,128)(2,1)S(1)}, bf16[64,4096]{1,0:T(8,128)(2,1)S(1)}, u32[]{:S(2)}, u32[]{:S(2)}) %collective-permute-start.3) | collective-permute-done | bytes 524320 | tf_op jit(solution)/shard_map/ppermute | solution.py:552
  91.7 6.8 %all-to-all-start.1 = ((bf16[16,32,4096]{2,1,0:T(8,128)(2,1)}), bf16[16,32,4096]{2,1,0:T(8,128)(2,1)}, u32[]{:S(2)}, u32[]{:S(2)}) async-start(bf16[16,32,4096]{2,1,0:T(8,128)(2,1)} %bitcast.73), calls=%async_computation.1 | async-start | bytes 8388608 | tf_op jit(solution)/shard_map/all_to_all | solution.py:41
  102.3 25.7 %collective-permute-done.6.w2 = bf16[256,4096]{1,0:T(8,128)(2,1)} collective-permute-done((bf16[256,4096]{1,0:T(8,128)(2,1)}, bf16[256,4096]{1,0:T(8,128)(2,1)}, u32[]{:S(2)}, u32[]{:S(2)}) %collective-permute-start.6) | collective-permute-done | bytes 2097184 | tf_op jit(solution)/shard_map/ppermute | solution.py:520
  128.0 20.0 %collective-permute-done.7.w3 = bf16[256,4096]{1,0:T(8,128)(2,1)} collective-permute-done((bf16[256,4096]{1,0:T(8,128)(2,1)}, bf16[256,4096]{1,0:T(8,128)(2,1)}, u32[]{:S(2)}, u32[]{:S(2)}) %collective-permute-start.7) | collective-permute-done | bytes 2097184 | tf_op jit(solution)/shard_map/ppermute | solution.py:520
  148.0 7.7 %all-to-all-done.1 = bf16[16,32,4096]{2,1,0:T(8,128)(2,1)} async-done(((bf16[16,32,4096]{2,1,0:T(8,128)(2,1)}), bf16[16,32,4096]{2,1,0:T(8,128)(2,1)}, u32[]{:S(2)}, u32[]{:S(2)}) %all-to-all-start.1) | async-done | bytes 4194336 | tf_op jit(solution)/shard_map/all_to_all | solution.py:41
  155.6 9.7 %shard_map.97 = (f32[512,1024]{1,0:T(8,128)S(1)}, bf16[512,1024]{1,0:T(8,128)(2,1)S(1)}) custom-call(s32[7]{0:T(128)S(1)} %stack.64.at_ref, bf16[8,2,4,8,4096]{4,3,2,1,0:T(8,128)(2,1)} %bitcast.22.rows_in, bf16[256,4096]{1,0:T(8,128)(2,1)} %collective-permute-done.1.w0, bf16[256,4096]{1,0:T(8,128)(2,1)} %collective-permute-done.2.w1, ...), custom_call_target="tpu_custom_call" | custom-call | flops 4294967296 | bytes 15728640 | tf_op jit(solution)/shard_map/pallas_call | solution.py:256
  170.3 9.4 %shard_map.98 = (bf16[512,4096]{1,0:T(8,128)(2,1)}, bf16[512,1024]{1,0:T(8,128)(2,1)S(1)}) custom-call(s32[7]{0:T(128)S(1)} %stack.64.at_ref, f32[512,1024]{1,0:T(8,128)S(1)} %get-tuple-element.56.pre_ref, bf16[512,1024]{1,0:T(8,128)(2,1)S(1)} %collective-permute-done.8.got_ref, bf16[256,4096]{1,0:T(8,128)(2,1)} %collective-permute-done.1.w0, ...), custom_call_target="tpu_custom_call" | custom-call | flops 4294967296 | bytes 16777216 | tf_op jit(solution)/shard_map/pallas_call | solution.py:324
  179.7 6.0 %all-to-all-start.2 = ((bf16[64,8,4096]{2,1,0:T(8,128)(2,1)}), bf16[64,8,4096]{2,1,0:T(8,128)(2,1)}, u32[]{:S(2)}, u32[]{:S(2)}) async-start(bf16[64,8,4096]{2,1,0:T(8,128)(2,1)} %bitcast.74), calls=%async_computation.2 | async-start | bytes 8388608 | tf_op jit(solution)/shard_map/all_to_all | solution.py:41
  185.7 9.4 %shard_map.99 = (bf16[256,4096]{1,0:T(8,128)(2,1)}, bf16[256,4096]{1,0:T(8,128)(2,1)S(1)}, bf16[256,4096]{1,0:T(8,128)(2,1)}, bf16[256,4096]{1,0:T(8,128)(2,1)}) custom-call(s32[7]{0:T(128)S(1)} %stack.64.at_ref, bf16[8,2,4,8,4096]{4,3,2,1,0:T(8,128)(2,1)} %bitcast.22.rows_in, bf16[512,1024]{1,0:T(8,128)(2,1)S(1)} %get-tuple-element.59.q_ref), custom_call_target="tpu_custom_call" | custom-call | flops 4294967296 | bytes 13631488 | tf_op jit(solution)/shard_map/pallas_call | solution.py:390
  200.1 36.4 %all-to-all-done.2 = bf16[64,8,4096]{2,1,0:T(8,128)(2,1)} async-done(((bf16[64,8,4096]{2,1,0:T(8,128)(2,1)}), bf16[64,8,4096]{2,1,0:T(8,128)(2,1)}, u32[]{:S(2)}, u32[]{:S(2)}) %all-to-all-start.2) | async-done | bytes 4194336 | tf_op jit(solution)/shard_map/all_to_all | solution.py:41
  255.1 5.2 %all-to-all-start.3 = ((bf16[16,16,2048]{2,1,0:T(8,128)(2,1)}), bf16[16,16,2048]{2,1,0:T(8,128)(2,1)S(1)}, u32[]{:S(2)}, u32[]{:S(2)}) async-start(bf16[16,16,2048]{2,1,0:T(8,128)(2,1)} %bitcast.70), calls=%async_computation.3 | async-start | bytes 2097152 | tf_op jit(solution)/shard_map/all_to_all | solution.py:41
  265.0 12.7 %all-to-all-done.3 = bf16[16,16,2048]{2,1,0:T(8,128)(2,1)S(1)} async-done(((bf16[16,16,2048]{2,1,0:T(8,128)(2,1)}), bf16[16,16,2048]{2,1,0:T(8,128)(2,1)S(1)}, u32[]{:S(2)}, u32[]{:S(2)}) %all-to-all-start.3) | async-done | bytes 1048608 | tf_op jit(solution)/shard_map/all_to_all | solution.py:41
  277.7 6.7 %all-to-all-start.4 = ((f32[128,8,128]{2,1,0:T(8,128)}), f32[128,8,128]{2,1,0:T(8,128)}, u32[]{:S(2)}, u32[]{:S(2)}) async-start(f32[128,8,128]{2,1,0:T(8,128)} %copy-done.8), calls=%async_computation.4 | async-start | bytes 1048576 | tf_op jit(solution)/shard_map/all_to_all | solution.py:41
  284.4 8.6 %collective-permute-done.12.refs_1_ = bf16[256,4096]{1,0:T(8,128)(2,1)} collective-permute-done((bf16[256,4096]{1,0:T(8,128)(2,1)}, bf16[256,4096]{1,0:T(8,128)(2,1)}, u32[]{:S(2)}, u32[]{:S(2)}) %collective-permute-start.12) | collective-permute-done | bytes 2097184 | tf_op jit(solution)/shard_map/ppermute | solution.py:566
  293.0 13.9 %collective-permute-done.13.refs_2_ = bf16[256,4096]{1,0:T(8,128)(2,1)} collective-permute-done((bf16[256,4096]{1,0:T(8,128)(2,1)}, bf16[256,4096]{1,0:T(8,128)(2,1)}, u32[]{:S(2)}, u32[]{:S(2)}) %collective-permute-start.13) | collective-permute-done | bytes 2097184 | tf_op jit(solution)/shard_map/ppermute | solution.py:566
  311.8 11.3 %all-to-all-start.5 = ((f32[128,8,128]{2,1,0:T(8,128)}), f32[128,8,128]{2,1,0:T(8,128)}, u32[]{:S(2)}, u32[]{:S(2)}) async-start(f32[128,8,128]{2,1,0:T(8,128)} %broadcast_in_dim.5), calls=%async_computation.5 | async-start | bytes 1048576 | tf_op jit(solution)/shard_map/all_to_all | solution.py:41
  325.8 5.3 %shard_map.102 = (bf16[2,4096,256]{2,1,0:T(8,128)(2,1)}, bf16[2,256,4096]{2,1,0:T(8,128)(2,1)}) custom-call(s32[7]{0:T(128)S(1)} %stack.64.at_ref, bf16[256,4096]{1,0:T(8,128)(2,1)} %collective-permute-done.11.refs_0_, bf16[256,4096]{1,0:T(8,128)(2,1)} %collective-permute-done.12.refs_1_, bf16[256,4096]{1,0:T(8,128)(2,1)} %collective-permute-done.13.refs_2_, ...), custom_call_target="tpu_custom_call" | custom-call | bytes 12582912 | tf_op jit(solution)/shard_map/pallas_call | solution.py:162
  331.1 8.2 %collective-permute-done.14.refs_0_ = bf16[256,4096]{1,0:T(8,128)(2,1)} collective-permute-done((bf16[256,4096]{1,0:T(8,128)(2,1)S(1)}, bf16[256,4096]{1,0:T(8,128)(2,1)}, u32[]{:S(2)}, u32[]{:S(2)}) %collective-permute-start.14) | collective-permute-done | bytes 2097184 | tf_op jit(solution)/shard_map/ppermute | solution.py:566
  (96 shorter events, 77.4 us)
Async XLA Ops:
  6.3 29.5 %collective-permute-start.1 = (bf16[256,4096]{1,0:T(8,128)(2,1)}, bf16[256,4096]{1,0:T(8,128)(2,1)}, u32[]{:S(2)}, u32[]{:S(2)}) collective-permute-start(bf16[256,4096]{1,0:T(8,128)(2,1)} %shard_map.93.p0), channel_id=1, source_target_pairs={{0,2},{2,0},{4,10},{6,8},{8,6},{10,4},{12,14},{14,12},{1,3},{3,1},... | collective-permute-start | bytes 6291464 | tf_op jit(solution)/shard_map/ppermute | solution.py:520
  14.1 35.8 %all-to-all-start = ((bf16[16,16,4096]{2,1,0:T(8,128)(2,1)}), bf16[16,16,4096]{2,1,0:T(8,128)(2,1)S(1)}, u32[]{:S(2)}, u32[]{:S(2)}) async-start(bf16[16,16,4096]{2,1,0:T(8,128)(2,1)} %bitcast.66), calls=%async_computation | async-start | bytes 4194304 | tf_op jit(solution)/shard_map/all_to_all | solution.py:41
  35.7 26.1 %collective-permute-start.2 = (bf16[256,4096]{1,0:T(8,128)(2,1)}, bf16[256,4096]{1,0:T(8,128)(2,1)}, u32[]{:S(2)}, u32[]{:S(2)}) collective-permute-start(bf16[256,4096]{1,0:T(8,128)(2,1)} %shard_map.95.p1), channel_id=1, source_target_pairs={{0,10},{2,8},{4,2},{6,0},{8,14},{10,12},{12,6},{14,4},{1,11},{3,9}... | collective-permute-start | bytes 6291464 | tf_op jit(solution)/shard_map/ppermute | solution.py:520
  49.9 186.7 %copy-start = (bf16[16,16,4096]{2,1,0:T(8,128)(2,1)}, bf16[16,16,4096]{2,1,0:T(8,128)(2,1)S(1)}, u32[]{:S(2)}) copy-start(bf16[16,16,4096]{2,1,0:T(8,128)(2,1)S(1)} %all-to-all-done) | copy-start | bytes 6291460
  50.6 1.6 collective-permute-start
  62.0 13.6 %collective-permute-start.4 = (bf16[64,4096]{1,0:T(8,128)(2,1)S(1)}, bf16[64,4096]{1,0:T(8,128)(2,1)S(1)}, u32[]{:S(2)}, u32[]{:S(2)}) collective-permute-start(bf16[64,4096]{1,0:T(8,128)(2,1)S(1)} %get-tuple-element.88), channel_id=1, source_target_pairs={{0,4},{2,6},{4,0},{6,2},{1,5},{3,7},{5,1},{7,3},{8,12},{10,14},{12... | collective-permute-start | bytes 1572872 | tf_op jit(solution)/shard_map/ppermute | solution.py:552
  63.2 25.4 %collective-permute-start.3 = (bf16[64,4096]{1,0:T(8,128)(2,1)S(1)}, bf16[64,4096]{1,0:T(8,128)(2,1)S(1)}, u32[]{:S(2)}, u32[]{:S(2)}) collective-permute-start(bf16[64,4096]{1,0:T(8,128)(2,1)S(1)} %get-tuple-element.89), channel_id=1, source_target_pairs={{0,2},{2,4},{4,6},{6,0},{1,3},{3,5},{5,7},{7,1},{8,10},{10,12},{12... | collective-permute-start | bytes 1572872 | tf_op jit(solution)/shard_map/ppermute | solution.py:552
  63.7 25.0 %collective-permute-start.5 = (bf16[64,4096]{1,0:T(8,128)(2,1)S(1)}, bf16[64,4096]{1,0:T(8,128)(2,1)S(1)}, u32[]{:S(2)}, u32[]{:S(2)}) collective-permute-start(bf16[64,4096]{1,0:T(8,128)(2,1)S(1)} %get-tuple-element.87), channel_id=1, source_target_pairs={{0,6},{2,0},{4,2},{6,4},{1,7},{3,1},{5,3},{7,5},{8,14},{10,8},{12,... | collective-permute-start | bytes 1572872 | tf_op jit(solution)/shard_map/ppermute | solution.py:552
  69.0 20.0 %copy-start.2 = (bf16[256,4096]{1,0:T(8,128)(2,1)}, bf16[256,4096]{1,0:T(8,128)(2,1)S(1)}, u32[]{:S(2)}) copy-start(bf16[256,4096]{1,0:T(8,128)(2,1)S(1)} %get-tuple-element.54.p2) | copy-start | bytes 6291460
  91.7 63.9 %all-to-all-start.1 = ((bf16[16,32,4096]{2,1,0:T(8,128)(2,1)}), bf16[16,32,4096]{2,1,0:T(8,128)(2,1)}, u32[]{:S(2)}, u32[]{:S(2)}) async-start(bf16[16,32,4096]{2,1,0:T(8,128)(2,1)} %bitcast.73), calls=%async_computation.1 | async-start | bytes 8388608 | tf_op jit(solution)/shard_map/all_to_all | solution.py:41
  98.5 29.5 %collective-permute-start.6 = (bf16[256,4096]{1,0:T(8,128)(2,1)}, bf16[256,4096]{1,0:T(8,128)(2,1)}, u32[]{:S(2)}, u32[]{:S(2)}) collective-permute-start(bf16[256,4096]{1,0:T(8,128)(2,1)} %copy-done.2), channel_id=1, source_target_pairs={{4,8},{6,10},{8,4},{10,6},{5,9},{7,11},{9,5},{11,7},{20,24},{22,26... | collective-permute-start | bytes 6291464 | tf_op jit(solution)/shard_map/ppermute | solution.py:520
  102.2 45.7 %collective-permute-start.7 = (bf16[256,4096]{1,0:T(8,128)(2,1)}, bf16[256,4096]{1,0:T(8,128)(2,1)}, u32[]{:S(2)}, u32[]{:S(2)}) collective-permute-start(bf16[256,4096]{1,0:T(8,128)(2,1)} %copy-done.3), channel_id=1, source_target_pairs={{0,8},{2,10},{4,0},{6,2},{8,12},{10,14},{12,4},{14,6},{1,9},{3,11}... | collective-permute-start | bytes 6291464 | tf_op jit(solution)/shard_map/ppermute | solution.py:520
  165.4 4.9 %collective-permute-start.8 = (bf16[512,1024]{1,0:T(8,128)(2,1)S(1)}, bf16[512,1024]{1,0:T(8,128)(2,1)S(1)}, u32[]{:S(2)}, u32[]{:S(2)}) collective-permute-start(bf16[512,1024]{1,0:T(8,128)(2,1)S(1)} %get-tuple-element.57), channel_id=1, source_target_pairs={{0,8},{8,0},{1,9},{9,1},{2,10},{10,2},{3,11},{11,3},{4,12},{12,4},... | collective-permute-start | bytes 3145736 | tf_op jit(solution)/shard_map/ppermute | solution.py:560
  179.7 56.8 %all-to-all-start.2 = ((bf16[64,8,4096]{2,1,0:T(8,128)(2,1)}), bf16[64,8,4096]{2,1,0:T(8,128)(2,1)}, u32[]{:S(2)}, u32[]{:S(2)}) async-start(bf16[64,8,4096]{2,1,0:T(8,128)(2,1)} %bitcast.74), calls=%async_computation.2 | async-start | bytes 8388608 | tf_op jit(solution)/shard_map/all_to_all | solution.py:41
  196.4 68.6 %collective-permute-start.11 = (bf16[256,4096]{1,0:T(8,128)(2,1)}, bf16[256,4096]{1,0:T(8,128)(2,1)}, u32[]{:S(2)}, u32[]{:S(2)}) collective-permute-start(bf16[256,4096]{1,0:T(8,128)(2,1)} %get-tuple-element.68.refs_3_), channel_id=1, source_target_pairs={{2,0},{0,2},{10,4},{8,6},{6,8},{4,10},{14,12},{12,14},{3,1},{1,3},... | collective-permute-start | bytes 6291464 | tf_op jit(solution)/shard_map/ppermute | solution.py:566
  240.4 10.0 %collective-permute-start.10 = (bf16[256,2048]{1,0:T(8,128)(2,1)}, bf16[256,2048]{1,0:T(8,128)(2,1)S(1)}, u32[]{:S(2)}, u32[]{:S(2)}) collective-permute-start(bf16[256,2048]{1,0:T(8,128)(2,1)} %get-tuple-element.65), channel_id=1, source_target_pairs={{0,8},{8,0},{1,9},{9,1},{2,10},{10,2},{3,11},{11,3},{4,12},{12,4},... | collective-permute-start | bytes 3145736 | tf_op jit(solution)/shard_map/ppermute | solution.py:580
  243.9 49.1 %collective-permute-start.12 = (bf16[256,4096]{1,0:T(8,128)(2,1)}, bf16[256,4096]{1,0:T(8,128)(2,1)}, u32[]{:S(2)}, u32[]{:S(2)}) collective-permute-start(bf16[256,4096]{1,0:T(8,128)(2,1)} %copy-done.5), channel_id=1, source_target_pairs={{10,0},{8,2},{2,4},{0,6},{14,8},{12,10},{6,12},{4,14},{11,1},{9,3}... | collective-permute-start | bytes 6291464 | tf_op jit(solution)/shard_map/ppermute | solution.py:566
  245.1 61.8 %collective-permute-start.13 = (bf16[256,4096]{1,0:T(8,128)(2,1)}, bf16[256,4096]{1,0:T(8,128)(2,1)}, u32[]{:S(2)}, u32[]{:S(2)}) collective-permute-start(bf16[256,4096]{1,0:T(8,128)(2,1)} %get-tuple-element.72.refs_5_), channel_id=1, source_target_pairs={{8,4},{10,6},{4,8},{6,10},{9,5},{11,7},{5,9},{7,11},{24,20},{26,22... | collective-permute-start | bytes 6291464 | tf_op jit(solution)/shard_map/ppermute | solution.py:566
  249.2 1.3 collective-permute-start.9
  255.1 52.1 %copy-start.4 = (bf16[256,4096]{1,0:T(8,128)(2,1)S(1)}, bf16[256,4096]{1,0:T(8,128)(2,1)}, u32[]{:S(2)}) copy-start(bf16[256,4096]{1,0:T(8,128)(2,1)} %get-tuple-element.75.refs_1_) | copy-start | bytes 6291460
  255.1 22.6 %all-to-all-start.3 = ((bf16[16,16,2048]{2,1,0:T(8,128)(2,1)}), bf16[16,16,2048]{2,1,0:T(8,128)(2,1)S(1)}, u32[]{:S(2)}, u32[]{:S(2)}) async-start(bf16[16,16,2048]{2,1,0:T(8,128)(2,1)} %bitcast.70), calls=%async_computation.3 | async-start | bytes 2097152 | tf_op jit(solution)/shard_map/all_to_all | solution.py:41
  277.7 29.5 %all-to-all-start.4 = ((f32[128,8,128]{2,1,0:T(8,128)}), f32[128,8,128]{2,1,0:T(8,128)}, u32[]{:S(2)}, u32[]{:S(2)}) async-start(f32[128,8,128]{2,1,0:T(8,128)} %copy-done.8), calls=%async_computation.4 | async-start | bytes 1048576 | tf_op jit(solution)/shard_map/all_to_all | solution.py:41
  307.2 32.2 %collective-permute-start.14 = (bf16[256,4096]{1,0:T(8,128)(2,1)S(1)}, bf16[256,4096]{1,0:T(8,128)(2,1)}, u32[]{:S(2)}, u32[]{:S(2)}) collective-permute-start(bf16[256,4096]{1,0:T(8,128)(2,1)S(1)} %copy-done.4), channel_id=1, source_target_pairs={{8,0},{10,2},{0,4},{2,6},{12,8},{14,10},{4,12},{6,14},{9,1},{11,3}... | collective-permute-start | bytes 6291464 | tf_op jit(solution)/shard_map/ppermute | solution.py:566
  311.8 31.0 %all-to-all-start.5 = ((f32[128,8,128]{2,1,0:T(8,128)}), f32[128,8,128]{2,1,0:T(8,128)}, u32[]{:S(2)}, u32[]{:S(2)}) async-start(f32[128,8,128]{2,1,0:T(8,128)} %broadcast_in_dim.5), calls=%async_computation.5 | async-start | bytes 1048576 | tf_op jit(solution)/shard_map/all_to_all | solution.py:41
  (9 other events, 60.3 us)
